TPU v7x, 32 devices: a whole 2x2x4 slice. The times are simulated.
32 devices in a mesh: clips: 2 (over y), tiles: 16 (over z, x, core).
Axes of the slice: x: 2, y: 2, z: 4, core: 2. Of those that a mesh axis runs over, the one named last changes fastest.
Arguments:
- frames: bfloat16 [4, 64, 256, 128], P(None, None, ('clips', 'tiles')), parts along dimension 2, may hold values from -6 to 6
- motion_forward: int32 [3, 512], P(None, ('clips', 'tiles')), parts along dimension 1, may hold values from 0 to 255, as said below
- motion_backward: int32 [3, 512], P(None, ('clips', 'tiles')), parts along dimension 1, may hold values from 0 to 255, as said below
- join_weight: bfloat16 [2, 64, 128], replicated, may hold values from -0.5 to 0.5
- conv_weight: bfloat16 [2, 4, 9, 64, 64], replicated, may hold values from -0.125 to 0.125
Outputs:
- forward_features: bfloat16 [4, 64, 256, 128], P(None, None, ('clips', 'tiles')), parts along dimension 2
- backward_features: bfloat16 [4, 64, 256, 128], P(None, None, ('clips', 'tiles')), parts along dimension 2
There are 2 independent parts, one for each index of `clips`. A program takes and returns all parts, laid end to end along the dimension named above; an argument that names none is the same for every part. Nothing has to cross between parts.
Inputs may be any that keep to these rules, and one draw needn't show every extreme that they name: `motion_forward`: entries are block numbers of the frame; block number k lies in rows held by device k // 16. A block of device d takes a block of a device at most 2 away from d, at most two block columns to either side of its own column. Of the 16 blocks of one device, either none or exactly 4 take blocks of any one other device; in every frame some device takes 4 blocks from each device up to 2 away on both sides. `motion_backward`: entries are block numbers of the frame; block number k lies in rows held by device k // 16. A block of device d takes a block of a device at most 2 away from d, at most two block columns to either side of its own column. Of the 16 blocks of one device, either none or exactly 4 take blocks of any one other device; in every frame some device takes 4 blocks from each device up to 2 away on both sides.
All inputs are finite; a program needn't handle non-finite values.
Results may differ from a plain program's by a relative error of at most 0.018.
Values may be sent and summed in bfloat16 or wider, within the bound.
No kernel may reach another device: no remote copies, remote signals or barrier semaphores. Data moves between devices by JAX's collectives and lax.ppermute only.
A program may use at most 64 MiB of HBM per device.

v0:
```python
import functools

import jax
import jax.numpy as jnp
from jax import lax
from jax.experimental import pallas as pl
from jax.experimental.pallas import tpu as pltpu
from jax.sharding import PartitionSpec as P

BS = 8
REACH = 2
QUAD = 4
HALO = 4
CAPACITY = 4
BF = jnp.bfloat16
F32 = jnp.float32


class Place:
    def __init__(self):
        me = lax.axis_index("tiles")
        self.me = me
        self.strip = me % QUAD
        self.core = me % 2
        self.side = self.strip // 2
        self.group = me // QUAD
        self.odd = self.group % 2
        self.top = self.group == 0
        self.bottom = self.group == lax.axis_size("tiles") // QUAD - 1


def leaky(value):
    widened = value.astype(F32)
    return jnp.maximum(widened, 0.1 * widened).astype(BF)


def rows_first(src, src_start, dst, dst_start, tmp, ch):
    tmp[...] = src[pl.ds(src_start, BS * ch), :].astype(F32)
    for r in range(BS):
        row = tmp[pl.ds(r, ch, stride=BS), :]
        dst[pl.ds(dst_start + r * ch, ch), :] = row.astype(BF)


def channels_first(src, src_start, dst, tmp, ch):
    for r in range(BS):
        tmp[pl.ds(r, ch, stride=BS), :] = src[pl.ds(src_start + r * ch, ch), :].astype(F32)
    dst[...] = tmp[...].astype(BF)


def pack_first_kernel(ch, crow, frames, motion_f, motion_b, mine, other, following, motion_buf, tmp, sems):
    place = Place()
    steps, strip = frames.shape[:2]
    half = HALO * ch
    core = place.core
    outs = (mine, other)
    lists = [
        pltpu.make_async_copy(motion, motion_buf.at[n], sems.at[4 + n]) for n, motion in enumerate((motion_f, motion_b))
    ]
    copies = []
    for n in range(2):
        back = 1 - core if n else core
        copies.append(frame_copy(frames, 0, back, outs[n].at[pl.ds(0, strip)], sems.at[n]))
        copies.append(frame_copy(frames, 1, back, following.at[n], sems.at[2 + n]))
    for copy in lists + copies:
        copy.start()
    for copy in lists:
        copy.wait()
    blocks = motion_f.shape[1]
    width = mine.shape[1]
    column = lax.broadcasted_iota(jnp.int32, motion_f.shape, 1)
    spread = jnp.where(
        lax.broadcasted_iota(jnp.int32, (blocks, width), 1) // BS
        == lax.broadcasted_iota(jnp.int32, (blocks, width), 0),
        1.0,
        0.0,
    ).astype(BF)
    wides = []
    for n in range(2):
        taken = motion_buf[n]
        across = taken // blocks
        code = (across - place.me + REACH) * (2 * blocks) + (taken - across * blocks - column + blocks - 1)
        wide = jnp.dot(code.astype(BF), spread, preferred_element_type=F32).astype(BF)
        frames_order = range(steps - 1) if n == 0 else range(steps - 2, -1, -1)
        wides += [wide[frame : frame + 1] for frame in frames_order]
    wides.append(jnp.zeros((crow - len(wides), width), BF))
    code = jnp.concatenate(wides, axis=0)
    for out in outs:
        out[pl.ds(strip, crow), :] = code
    for copy in copies:
        copy.wait()
    for n, out in enumerate(outs):
        tmp[...] = following[n].astype(F32)
        for r in range(HALO):
            row = tmp[pl.ds(place.side * (BS - HALO) + r, ch, stride=BS), :]
            out[pl.ds(strip + crow + r * ch, ch), :] = row.astype(BF)


def pair_first_kernel(ch, crow, mine, swapped, out):
    place = Place()
    strip = BS * ch
    half = HALO * ch
    for n, piece in enumerate((mine, swapped)):
        at = place.core ^ n
        out[pl.ds(pl.multiple_of(at * strip, strip), strip), :] = piece[pl.ds(0, strip), :]
        out[pl.ds(pl.multiple_of(2 * strip + at * crow, crow), crow), :] = piece[pl.ds(strip, crow), :]

        @pl.when(at == place.side)
        def _(piece=piece):
            out[pl.ds(2 * (strip + crow), half), :] = piece[pl.ds(strip + crow, half), :]


def frame_copy(frames, step, back, out, sem):
    steps = frames.shape[0]
    return pltpu.make_async_copy(frames.at[step + back * (steps - 1 - 2 * step)], out, sem)


def pack_rest_kernel(frames, after, other, sems):
    steps = frames.shape[0]
    strip = frames.shape[1]
    core = Place().core
    copies = [
        frame_copy(frames, step, 1 - core, other.at[pl.ds((step - 1) * strip, strip)], sems.at[step - 1])
        for step in range(1, steps)
    ]
    for copy in copies:
        copy.start()
    for copy in copies:
        copy.wait()


def pair_copies(frames, swapped, core, first, count, out, sems):
    strip = frames.shape[1]
    copies = []
    for n in range(count):
        step = first + n
        own = out.at[pl.ds(pl.multiple_of((2 * n + core) * strip, strip), strip)]
        his = out.at[pl.ds(pl.multiple_of((2 * n + 1 - core) * strip, strip), strip)]
        copies.append(frame_copy(frames, step, core, own, sems.at[2 * n]))
        copies.append(
            pltpu.make_async_copy(swapped.at[pl.ds((step - 1) * strip, strip)], his, sems.at[2 * n + 1])
        )
    return copies


def pair_kernel(first, count, frames, swapped, out, sems):
    copies = pair_copies(frames, swapped, Place().core, first, count, out, sems)
    for copy in copies:
        copy.start()
    for copy in copies:
        copy.wait()


def gather_first_kernel(ch, crow, pair, received, rest, xq, codes, msg_e, msg_o, rest_out, tmp, edges):
    place = Place()
    strip = BS * ch
    half = HALO * ch
    for n, piece in enumerate((pair, received)):
        side = place.side ^ n
        for m in range(2):
            at = side * 2 + m
            rows_first(piece, m * strip, xq, pl.multiple_of(at * strip, strip), tmp, ch)
            code_at = pl.multiple_of(at * crow, crow)
            codes[pl.ds(code_at, crow), :] = piece[pl.ds(2 * strip + m * crow, crow), :]
        edges[side] = piece[pl.ds(2 * (strip + crow), half), :]
    low = (QUAD * BS - HALO) * ch
    msg_e[pl.ds(0, half), :] = xq[pl.ds(pl.multiple_of(low - place.odd * low, half), half), :]
    msg_o[pl.ds(0, half), :] = xq[pl.ds(pl.multiple_of(place.odd * low, half), half), :]
    msg_e[pl.ds(half, half), :] = edges[1 - place.odd]
    msg_o[pl.ds(half, half), :] = edges[place.odd]
    msg_e[pl.ds(2 * half, codes.shape[0]), :] = codes[...]
    msg_o[pl.ds(2 * half, codes.shape[0]), :] = codes[...]


def gather_kernel(ch, at, pair, received, after, xq, tmp):
    strip = BS * ch
    side = Place().side
    for n, piece in enumerate((pair, received)):
        for m in range(2):
            start = ((side + n) % 2 * 2 + m) * strip
            rows_first(piece, (2 * at + m) * strip, xq, pl.multiple_of(start, strip), tmp, ch)


class Codes:
    def __init__(self, rows):
        width = rows[0].shape[1]
        self.rows = rows
        self.blocks = width // BS
        k_id = lax.broadcasted_iota(jnp.int32, (width, width), 0)
        l_id = lax.broadcasted_iota(jnp.int32, (width, width), 1)
        base = (k_id // BS - l_id // BS + self.blocks - 1).astype(F32)
        self.base = jnp.where(k_id % BS == l_id % BS, base, -1.0e4)
        self.slot = k_id.astype(F32)
        self.before = jnp.where((k_id % BS == 0) & (k_id // BS < l_id // BS), 1.0, 0.0).astype(BF)
        self.lane = (lax.broadcasted_iota(jnp.int32, (1, width), 1) % BS).astype(F32)
        self.zero = jnp.zeros((width, width), BF)
        self.ranks = {}

    def plain(self, dest, source):
        ds = source - dest
        if abs(ds) > REACH:
            return self.zero
        shift = float((ds + REACH) * 2 * self.blocks)
        return jnp.where(self.rows[dest + 2] - shift == self.base, 1.0, 0.0).astype(BF)

    def rank_all(self, wanted):
        rows = []
        for dest, source in wanted:
            low = float((source - dest + REACH) * 2 * self.blocks)
            code = self.rows[dest + 2]
            rows.append(jnp.where((code >= low) & (code < low + 2 * self.blocks), 1.0, 0.0))
        count = len(rows)
        rows += [rows[0]] * (-count % 16)
        stacked = jnp.concatenate(rows, axis=0)
        before = jnp.dot(stacked.astype(BF), self.before, preferred_element_type=F32)
        for n, key in enumerate(wanted):
            self.ranks[key] = jnp.where(
                stacked[n : n + 1] > 0, before[n : n + 1] * BS + self.lane, -1.0e4
            )

    def packed(self, dest, source, region):
        at = self.ranks[dest, source] + float(region * CAPACITY * BS)
        return jnp.where(self.slot == at, 1.0, 0.0).astype(BF)

    def pack(self, dest, source, region):
        return lax.dot_general(
            self.plain(dest, source),
            self.packed(dest, source, region),
            (((1,), (1,)), ((), ())),
            preferred_element_type=F32,
        )


FROM_ABOVE = (((0, -2), (-1, -2), (-1, -3)), ((1, -1), (0, -1), (0, -2)))
FROM_BELOW = (
    ((QUAD - 1, QUAD + 1), (QUAD, QUAD + 1), (QUAD, QUAD + 2)),
    ((QUAD - 2, QUAD), (QUAD - 1, QUAD), (QUAD - 1, QUAD + 1)),
)
TO_BELOW = tuple(tuple((d + QUAD, s + QUAD) for d, s in tile) for tile in FROM_ABOVE)
TO_ABOVE = tuple(tuple((d - QUAD, s - QUAD) for d, s in tile) for tile in FROM_BELOW)


def step_codes(ch, place, step, steps, codes, halo_e, halo_o):
    crow = codes.shape[0] // QUAD
    width = codes.shape[1]
    pick = place.core * (steps - 1) + step - 1
    row_id = lax.broadcasted_iota(jnp.int32, (crow, width), 0)

    def row(ref, start):
        block = ref[pl.ds(start, crow), :].astype(F32)
        return jnp.sum(jnp.where(row_id == pick, block, 0.0), axis=0, keepdims=True)

    odd = place.odd == 1
    half = HALO * ch

    def beside(strip, above):
        e = row(halo_e, 2 * half + strip * crow)
        o = row(halo_o, 2 * half + strip * crow)
        return jnp.where(odd, e, o) if above else jnp.where(odd, o, e)

    rows = [beside(QUAD - 2, True), beside(QUAD - 1, True)]
    rows += [row(codes, strip * crow) for strip in range(QUAD)]
    rows += [beside(0, False), beside(1, False)]
    return Codes(rows)


PARTS = (((-1,), True), ((0, 1), False), ((0, 1), True), ((2, 3), False), ((2, 3), True), ((QUAD,), False))


def tiles_of(dests, bottom):
    tiles = [source for source in range(QUAD) if any(abs(source - d) <= REACH for d in dests)]
    for side, near, tables in ((0, -1, FROM_ABOVE), (1, QUAD, FROM_BELOW)):
        if any(abs(near - d) <= REACH for d in dests):
            whole = bottom if side == 0 else not bottom
            tiles += [(side, 0), (side, 1)] if whole else [(side, 2)]
    return tiles


def receive_choice(code, dests, bottom, out):
    width = out.shape[0] // len(tiles_of(dests, bottom))
    for n, tile in enumerate(tiles_of(dests, bottom)):
        for m, dest in enumerate(dests):
            if isinstance(tile, int):
                value = code.plain(dest, tile)
            elif tile[1] == 0:
                value = code.plain(dest, -1 if tile[0] == 0 else QUAD)
            else:
                table = (FROM_ABOVE, FROM_BELOW)[tile[0]][tile[1] - 1]
                value = sum(
                    (code.packed(d, source, at) for at, (d, source) in enumerate(table) if d == dest), code.zero
                )
            out[pl.ds(n * width, width), pl.ds(m * width, width)] = value


SENT = tuple((side, tile) for side in range(2) for tile in range(2))


def sent_regions(side, tile):
    regions = (TO_ABOVE, TO_BELOW)[side][tile]
    return regions, sorted({source for _, source in regions})


def send_choice(code, side, tile, out):
    regions, sources = sent_regions(side, tile)
    width = out.shape[1]
    for n, source in enumerate(sources):
        total = sum(code.pack(d, source, at) for at, (d, origin) in enumerate(regions) if origin == source)
        out[pl.ds(n * width, width), :] = total.astype(BF)


def all_pairs(*tables):
    return [pair for table in tables for tile in table for pair in tile]


def choices_kernel(ch, step, steps, codes, code_e, code_o, after, *outs):
    place = Place()
    code = step_codes(ch, place, step, steps, codes, code_e, code_o)
    code.rank_all(all_pairs(FROM_ABOVE, FROM_BELOW))
    for part, out in zip(PARTS, outs):
        receive_choice(code, *part, out)
    if step + 1 < steps:
        code = step_codes(ch, place, step + 1, steps, codes, code_e, code_o)
        code.rank_all(all_pairs(TO_ABOVE, TO_BELOW))
        for item, out in zip(SENT, outs[len(PARTS) :]):
            send_choice(code, *item, out)


def choice_shapes(width):
    parts = [(len(tiles_of(*part)) * width, len(part[0]) * width) for part in PARTS]
    return parts, [(len(sent_regions(*item)[1]) * width, width) for item in SENT]


def align(ch, feat, recv, aligned, offset, part, choice, only=None):
    dests, bottom = part
    half = HALO * ch
    shift = half if bottom else 0
    width = feat.shape[1]
    left = [
        feat[pl.ds(tile * BS * ch + shift, half), :]
        if isinstance(tile, int)
        else recv[tile[0], pl.ds(tile[1] * half, half), :]
        for tile in tiles_of(dests, bottom)
    ]
    if only is None:
        right = choice[...]
    else:
        right = choice[:, only * width : (only + 1) * width]
        dests = (dests[only],)
    got = jnp.dot(jnp.concatenate(left, axis=1), right, preferred_element_type=F32).astype(BF)
    for n, d in enumerate(dests):
        aligned[pl.ds((d * BS + offset) * ch + shift, half), :] = got[:, n * width : (n + 1) * width]


def pack_messages(ch, fout, par, sent, choices, msg_e, msg_o):
    half = HALO * ch
    strip = BS * ch
    for side, near in ((0, 0), (1, QUAD - 1)):
        shift = half if side == 1 else 0
        sent[side, pl.ds(0, half), :] = fout[pl.ds(near * strip + shift, half), :]
    for (side, tile), choice in zip(SENT, choices):
        shift = half if (side == 1) == (tile == 0) else 0
        left = [fout[pl.ds(source * strip + shift, half), :] for source in sent_regions(side, tile)[1]]
        got = jnp.dot(jnp.concatenate(left, axis=1), choice[...], preferred_element_type=F32)
        sent[side, pl.ds((tile + 1) * half, half), :] = got.astype(BF)
    msg_e[...] = sent[1 - par]
    msg_o[...] = sent[par]


def step_kernel(ch, step, steps, *refs):
    strip = BS * ch
    half = HALO * ch
    last = step == steps - 1
    refs = list(refs)

    def take(count):
        taken = refs[:count]
        del refs[:count]
        return taken

    xq, halo_e, halo_o, join, conv = take(5)
    if step > 0:
        feat, feat_e, feat_o = take(3)
        choices = take(len(PARTS) + (0 if last else len(SENT)))
        before, back, out_a, out_b = take(4)
        if not last:
            (x_next,) = take(1)
    else:
        (codes,) = take(1)
    if not last:
        fout, msg_e, msg_o = take(3)
    own_out, part_out = take(2)
    if step > 0:
        out_f, out_g = take(2)
    tmp, act_a, act_b, held, xext = take(5)
    if step > 0:
        sems, aligned, recv = take(3)
    else:
        choices = take(len(SENT))
    if last:
        (fout,) = take(1)
    else:
        (sent,) = take(1)
    width = xq.shape[-1]
    place = Place()
    par = place.odd
    core = place.core
    quad_rows = QUAD * BS
    rows = 2 * BS if last else quad_rows
    right_side = place.side
    own = place.core if last else place.strip

    copies = []
    if step > 0:
        copies = result_copies(strip, step - 1, steps, before, back, out_f, out_g, sems)
        for n, copy in copies:
            pl.when(core == n)(copy.start)
    halo_at = (0, half)[step] if step < 2 else 3 * half

    above = pl.ds(pl.multiple_of((1 - par) * (quad_rows + HALO) * ch, half), half)
    below = pl.ds(pl.multiple_of(par * (quad_rows + HALO) * ch, half), half)
    xext[above, :] = halo_e[pl.ds(halo_at, half), :]
    xext[below, :] = halo_o[pl.ds(halo_at, half), :]
    xext[pl.ds(half, quad_rows * ch), :] = xq[...]
    if step > 0:
        recv[1 - par] = feat_e[pl.ds(0, 3 * half), :]
        recv[par] = feat_o[pl.ds(0, 3 * half), :]
        if last:

            @pl.when(right_side == 0)
            def _():
                for n in range(3):
                    align(ch, feat, recv, aligned, HALO, PARTS[n], choices[n])
                align(ch, feat, recv, aligned, HALO, PARTS[3], choices[3], 0)

            @pl.when(right_side == 1)
            def _():
                offset = HALO - 2 * BS
                align(ch, feat, recv, aligned, offset, PARTS[2], choices[2], 1)
                for n in range(3, 6):
                    align(ch, feat, recv, aligned, offset, PARTS[n], choices[n])

        else:
            for n, rows_part in enumerate(PARTS):
                align(ch, feat, recv, aligned, HALO, rows_part, choices[n])
            sent[0, pl.ds(3 * half, half), :] = x_next[pl.ds(0, half), :]
            sent[1, pl.ds(3 * half, half), :] = x_next[pl.ds((quad_rows - HALO) * ch, half), :]
    else:
        code = step_codes(ch, place, 1, steps, codes, halo_e, halo_o)
        code.rank_all(all_pairs(TO_ABOVE, TO_BELOW))
        for item, out in zip(SENT, choices):
            send_choice(code, *item, out)

    off = 8
    top_ok = jnp.logical_not(place.top)
    bottom_ok = jnp.logical_not(place.bottom)
    if last:
        top_ok = top_ok | (right_side == 1)
        bottom_ok = bottom_ok | (right_side == 0)
    start_row = right_side * (2 * BS) if last else 0
    lane = lax.broadcasted_iota(jnp.int32, (ch, width), 1)
    not_first = lane > 0
    not_last = lane < width - 1
    zero = jnp.zeros((ch, width), BF)

    def put(buf, row, act):
        if row < 0:
            act = jnp.where(top_ok, act, zero)
        if row >= rows:
            act = jnp.where(bottom_ok, act, zero)
        here = pl.ds((row + off) * ch, ch)
        buf[0, here, :] = jnp.where(not_first, pltpu.roll(act, 1, 1), zero)
        buf[1, here, :] = act
        buf[2, here, :] = jnp.where(not_last, pltpu.roll(act, width - 1, 1), zero)

    for buf in (act_a, act_b):
        for row in (-HALO - 1, rows + HALO):
            for n in range(3):
                buf[n, pl.ds((row + off) * ch, ch), :] = zero

    join_mat = join[...]
    for g in range((rows + 2 * HALO) // 4):
        first = g * 4 - HALO
        at = (start_row + g * 4) * ch
        inp = xext[pl.ds(pl.multiple_of(at, 4 * ch) if last else at, 4 * ch), :]
        if step == 0:
            right = jnp.concatenate([inp[: 2 * ch], inp[2 * ch :]], axis=1)
        else:
            al = aligned[pl.ds(g * 4 * ch, 4 * ch), :]
            sides = []
            for h in range(2):
                a, b = 2 * h * ch, (2 * h + 1) * ch
                sides.append(
                    jnp.concatenate([al[a : a + ch], inp[a : a + ch], al[b : b + ch], inp[b : b + ch]], axis=0)
                )
            right = jnp.concatenate(sides, axis=1)
        mixed = jnp.dot(join_mat, right, preferred_element_type=F32).astype(BF)
        for h in range(2):
            for q in range(2):
                row = first + 2 * h + q
                value = mixed[q * ch : (q + 1) * ch, h * width : (h + 1) * width]
                held[pl.ds((row + off) * ch, ch), :] = value
                put(act_a, row, leaky(value))

    layers = conv.shape[0]
    source, target = act_a, act_b
    for layer in range(layers):
        need = layers - 1 - layer
        reach = -(-need // 2) * 2
        start, stop = -reach, rows + reach
        if (stop - start) % 4:
            start, stop = -HALO, rows + HALO
        weight = conv[layer]
        for first in range(start, stop, 4):
            sides = [
                jnp.concatenate([source[n, pl.ds((first + 2 * h - 1 + off) * ch, 4 * ch), :] for n in range(3)], axis=0)
                for h in range(2)
            ]
            out = jnp.dot(weight, jnp.concatenate(sides, axis=1), preferred_element_type=F32)
            for h in range(2):
                for q in range(2):
                    row = first + 2 * h + q
                    here = pl.ds((row + off) * ch, ch)
                    total = held[here, :].astype(F32) + out[q * ch : (q + 1) * ch, h * width : (h + 1) * width]
                    value = total.astype(BF)
                    if layer < layers - 1:
                        held[here, :] = value
                        put(target, row, leaky(value))
                    else:
                        fout[pl.ds(row * ch, ch), :] = value
        source, target = target, source

    if not last:
        pack_messages(ch, fout, par, sent, choices[-len(SENT) :], msg_e, msg_o)
    channels_first(fout, pl.multiple_of(own * strip, strip), own_out, tmp, ch)
    channels_first(fout, pl.multiple_of((own ^ 1) * strip, strip), part_out, tmp, ch)
    for n, copy in copies:
        pl.when(core == n)(copy.wait)


def result_copies(strip, step, steps, own, back, out_f, out_g, sems):
    copies = []
    for n in range(2):
        forth, other = (out_f, out_g) if n == 0 else (out_g, out_f)
        at = step if n == 0 else steps - 1 - step
        other_at = steps - 1 - at
        copies.append((n, pltpu.make_async_copy(own, forth.at[pl.ds(at * strip, strip)], sems.at[0])))
        copies.append((n, pltpu.make_async_copy(back, other.at[pl.ds(other_at * strip, strip)], sems.at[1])))
    return copies


def finish_kernel(strip, steps, own, back, out_a, out_b, out_f, out_g, sems):
    core = Place().core
    copies = result_copies(strip, steps - 1, steps, own, back, out_f, out_g, sems)
    for n, copy in copies:
        pl.when(core == n)(copy.start)
    for n, copy in copies:
        pl.when(core == n)(copy.wait)


def weights_kernel(conv, join, wide, join_both, join_first):
    core = Place().core
    layers, ch = conv.shape[1], conv.shape[3]
    zero = jnp.zeros((ch, ch), BF)
    for layer in range(layers):
        for dx in range(3):
            taps = [conv[core, layer, 3 * dy + dx] for dy in range(3)]
            for q in range(2):
                line = [zero] * q + taps + [zero] * (1 - q)
                wide[layer, pl.ds(q * ch, ch), pl.ds(dx * 4 * ch, 4 * ch)] = jnp.concatenate(line, axis=1)
    both = join[core]
    none = jnp.zeros_like(both)
    join_both[pl.ds(0, ch), :] = jnp.concatenate([both, none], axis=1)
    join_both[pl.ds(ch, ch), :] = jnp.concatenate([none, both], axis=1)
    enter = both[:, ch:]
    join_first[pl.ds(0, ch), :] = jnp.concatenate([enter, zero], axis=1)
    join_first[pl.ds(ch, ch), :] = jnp.concatenate([zero, enter], axis=1)


VMEM = pl.BlockSpec(memory_space=pltpu.VMEM)
ANY = pl.BlockSpec(memory_space=pl.ANY)
HBM = pl.BlockSpec(memory_space=pltpu.HBM)


def call(kernel, name, args, outs, scratch=(), flops=0, in_any=(), out_any=(), aliases=None, in_hbm=()):
    args = [pltpu.with_memory_space_constraint(a, pltpu.HBM) if n in in_hbm else a for n, a in enumerate(args)]
    return pl.pallas_call(
        kernel,
        out_shape=[jax.ShapeDtypeStruct(o, BF) for o in outs],
        in_specs=[HBM if n in in_hbm else ANY if n in in_any else VMEM for n in range(len(args))],
        out_specs=[ANY if n in out_any else VMEM for n in range(len(outs))],
        scratch_shapes=list(scratch),
        input_output_aliases=aliases or {},
        compiler_params=pltpu.CompilerParams(vmem_limit_bytes=32 << 20),
        cost_estimate=pl.CostEstimate(
            flops=flops, bytes_accessed=sum(a.size * a.dtype.itemsize for a in args), transcendentals=0
        ),
        name=name,
    )(*args)


def pairings(count):
    groups = count // QUAD
    out = []
    for parity in range(2):
        pairs = []
        for i in range(count):
            g = i // QUAD
            other = g + 1 if g % 2 == parity else g - 1
            pairs.append((i, i % QUAD + other * QUAD if 0 <= other < groups else i ^ 1))
        out.append(pairs)
    return out


def on_device(frames, motion_forward, motion_backward, join_weight, conv_weight):
    steps, ch, strip_rows, width = frames.shape
    strip = strip_rows * ch
    half = HALO * ch
    crow = 16
    count = lax.axis_size("tiles")
    even, odd = pairings(count)

    def near(k):
        return [(i, i ^ k) for i in range(count)]

    def send(value, pairs):
        return lax.ppermute(value, "tiles", pairs)

    tmp = pltpu.VMEM((strip, width), F32)
    piece = (strip, width)
    rows = QUAD * BS
    messages = [(3 * half, width)] + [(4 * half, width)] * (steps - 2)
    feature = (rows * ch, width)
    whole = (steps * strip, width)
    flat = frames.reshape(steps, strip, width)
    mine, other = call(
        functools.partial(pack_first_kernel, ch, crow),
        "pack_first",
        (flat, motion_forward, motion_backward),
        [(strip + crow + half, width)] * 2,
        [
            pltpu.VMEM((2, *piece), BF),
            pltpu.VMEM((2, *motion_forward.shape), jnp.int32),
            tmp,
            pltpu.SemaphoreType.DMA((6,)),
        ],
        in_hbm=(0, 1, 2),
    )
    (pair,) = call(
        functools.partial(pair_first_kernel, ch, crow),
        "pair_first",
        (mine, send(other, near(1))),
        [(2 * (strip + crow) + half, width)],
    )
    received = send(pair, near(2))
    (rest,) = call(
        pack_rest_kernel,
        "pack_rest",
        (flat, pair),
        [((steps - 1) * strip, width)],
        [pltpu.SemaphoreType.DMA((steps - 1,))],
        in_hbm=(0,),
        in_any=(1,),
        out_any=(0,),
    )
    swapped = send(rest, near(1))
    many = 2 * (steps - 1)
    (pair_rest,) = call(
        functools.partial(pair_kernel, 1, steps - 1),
        "pair_rest",
        (flat, swapped),
        [(many * strip, width)],
        [pltpu.SemaphoreType.DMA((many,))],
        in_hbm=(0,),
        in_any=(1,),
        out_any=(0,),
    )
    layers = conv_weight.shape[1]
    conv, join_both, join_first = call(
        weights_kernel,
        "weights",
        (conv_weight, join_weight),
        [(layers, 2 * ch, 12 * ch), (2 * ch, 4 * ch), (2 * ch, 2 * ch)],
    )
    xq, codes, edge_e, edge_o, pair_rest = call(
        functools.partial(gather_first_kernel, ch, crow),
        "gather_first",
        (pair, received, pair_rest),
        [feature, (QUAD * crow, width)] + [(2 * half + QUAD * crow, width)] * 2 + [pair_rest.shape],
        [tmp, pltpu.VMEM((2, half, width), BF)],
        in_any=(2,),
        out_any=(4,),
        aliases={2: 4},
    )
    halo_e, halo_o = code_e, code_o = send(edge_e, even), send(edge_o, odd)
    received_rest = send(pair_rest, near(2))

    wide_act = pltpu.VMEM((3, (rows + 16) * ch, width), BF)
    flops = 2 * (rows + 2 * HALO) * width * ch * ch * 9 * layers
    part_shapes, sent_shapes = choice_shapes(width)
    for step in range(steps):
        last = step == steps - 1
        args = [xq, halo_e, halo_o, join_both if step else join_first, conv]
        outs = [] if last else [feature, messages[step], messages[step]]
        outs += [piece, piece]
        scratch = [tmp, wide_act, wide_act, pltpu.VMEM(((rows + 16) * ch, width), BF)]
        scratch += [pltpu.VMEM(((rows + 2 * HALO) * ch, width), BF)]
        if step:
            args += [feat, feat_e, feat_o, *choices, own, back, *outputs]
            many = len(args)
            in_any = (many - 4, many - 3, many - 2, many - 1)
            aliases = {many - 2: len(outs), many - 1: len(outs) + 1}
            out_any = (len(outs), len(outs) + 1)
            outs += [whole, whole]
            if not last:
                args += [x_next]
            scratch += [pltpu.SemaphoreType.DMA((2,))]
            scratch += [pltpu.VMEM(((rows + 2 * HALO) * ch, width), BF), pltpu.VMEM((2, 3 * half, width), BF)]
        else:
            args += [codes]
            in_any = out_any = ()
            aliases = {}
            scratch += [pltpu.VMEM(shape, BF) for shape in sent_shapes]
        scratch += [pltpu.VMEM((2 * strip, width) if last else (2, *messages[step]), BF)]
        results = call(
            functools.partial(step_kernel, ch, step, steps),
            "refine",
            args,
            outs,
            scratch,
            flops,
            in_any,
            out_any,
            aliases,
        )
        if not last:
            feat, msg_e, msg_o, *results = results
            feat_e, feat_o = send(msg_e, even), send(msg_o, odd)
            if step:
                halo_e, halo_o = feat_e, feat_o
            choices = call(
                functools.partial(choices_kernel, ch, step + 1, steps),
                "choices",
                (codes, code_e, code_o, msg_e),
                part_shapes + (sent_shapes if step + 2 < steps else []),
                in_any=(3,),
            )
        own, part, *results = results
        back = send(part, near(1))
        if step == 0:
            outputs = call(lambda after, a, b: None, "results", (part,), [whole, whole], in_any=(0,), out_any=(0, 1))

            def later(frame):
                return call(
                    functools.partial(gather_kernel, ch, frame - 1),
                    "gather",
                    (pair_rest, received_rest, msg_e),
                    [feature],
                    [tmp],
                    in_any=(2,),
                )[0]

            xq, x_next = later(1), later(2)
        else:
            outputs = results
            if not last:
                xq = x_next
                x_next = later(step + 2) if step + 2 < steps else None

    outputs = call(
        functools.partial(finish_kernel, strip, steps),
        "finish",
        [own, back, *outputs],
        [whole] * 2,
        [pltpu.SemaphoreType.DMA((2,))],
        in_any=(0, 1, 2, 3),
        out_any=(0, 1),
        aliases={2: 0, 3: 1},
    )
    return tuple(o.reshape(frames.shape) for o in outputs)


def solution(mesh):
    return jax.shard_map(
        on_device,
        mesh=mesh,
        in_specs=(
            P(None, None, ("clips", "tiles"), None),
            P(None, ("clips", "tiles")),
            P(None, ("clips", "tiles")),
            P(),
            P(),
        ),
        out_specs=(
            P(None, None, ("clips", "tiles"), None),
            P(None, None, ("clips", "tiles"), None),
        ),
        check_vma=False,
    )
```

profile of v0, /device:TPU:0, one launch (start us, length us, event | category | flops | bytes accessed | tf_op | source)
XLA Modules:
  0.0 66.9 jit_solution(6080461137835896709)
XLA Ops:
  0.6 1.3 %pack_first.1 = (bf16[784,128]{1,0:T(8,128)(2,1)S(1)}, bf16[784,128]{1,0:T(8,128)(2,1)S(1)}) custom-call(bf16[4,512,128]{2,1,0:T(8,128)(2,1)} %bitcast.5, s32[3,16]{1,0:T(4,128)} %motion_f.1, s32[3,16]{1,0:T(4,128)} %motion_b.1), custom_call_target="tpu_custom_call" | custom-call | bytes 524672 | tf_op jit(solution)/shard_map/pack_first/pallas_call | solution.py:585
  2.4 1.1 %collective-permute-done.swapped = bf16[784,128]{1,0:T(8,128)(2,1)S(1)} collective-permute-done((bf16[784,128]{1,0:T(8,128)(2,1)S(1)}, bf16[784,128]{1,0:T(8,128)(2,1)S(1)}, u32[]{:S(2)}, u32[]{:S(2)}) %collective-permute-start) | collective-permute-done | bytes 200736 | tf_op jit(solution)/shard_map/ppermute | solution.py:625
  3.5 1.1 %pack_rest.1 = bf16[1536,128]{1,0:T(8,128)(2,1)S(1)} custom-call(bf16[4,512,128]{2,1,0:T(8,128)(2,1)} %bitcast.6, bf16[1312,128]{1,0:T(8,128)(2,1)S(1)} %pair_first.1.after.pair), custom_call_target="tpu_custom_call" | custom-call | bytes 860160 | tf_op jit(solution)/shard_map/pack_rest/pallas_call | solution.py:585
  5.1 2.6 %collective-permute-start.1 = (bf16[1312,128]{1,0:T(8,128)(2,1)S(1)}, bf16[1312,128]{1,0:T(8,128)(2,1)S(1)}, u32[]{:S(2)}, u32[]{:S(2)}) collective-permute-start(bf16[1312,128]{1,0:T(8,128)(2,1)S(1)} %pair_first.1.after.pair), channel_id=1, source_target_pairs={{0,2},{1,3},{2,0},{3,1},{4,6},{5,7},{6,4},{7,5},{8,10},{9,11},{10,... | collective-permute-start | bytes 1007624 | tf_op jit(solution)/shard_map/ppermute | solution.py:625
  7.7 1.3 %pair_rest.1.rest = bf16[3072,128]{1,0:T(8,128)(2,1)S(1)} custom-call(bf16[4,512,128]{2,1,0:T(8,128)(2,1)} %bitcast.7, bf16[1536,128]{1,0:T(8,128)(2,1)S(1)} %collective-permute-done.2.swapped), custom_call_target="tpu_custom_call" | custom-call | bytes 917504 | tf_op jit(solution)/shard_map/pair_rest/pallas_call | solution.py:585
  9.0 7.1 %collective-permute-done.1.received = bf16[1312,128]{1,0:T(8,128)(2,1)S(1)} collective-permute-done((bf16[1312,128]{1,0:T(8,128)(2,1)S(1)}, bf16[1312,128]{1,0:T(8,128)(2,1)S(1)}, u32[]{:S(2)}, u32[]{:S(2)}) %collective-permute-start.1) | collective-permute-done | bytes 335904 | tf_op jit(solution)/shard_map/ppermute | solution.py:625
  16.4 1.8 %collective-permute-start.3 = (bf16[3072,128]{1,0:T(8,128)(2,1)S(1)}, bf16[3072,128]{1,0:T(8,128)(2,1)S(1)}, u32[]{:S(2)}, u32[]{:S(2)}) collective-permute-start(bf16[3072,128]{1,0:T(8,128)(2,1)S(1)} %get-tuple-element.67.pair), channel_id=1, source_target_pairs={{0,2},{1,3},{2,0},{3,1},{4,6},{5,7},{6,4},{7,5},{8,10},{9,11},{10,... | collective-permute-start | bytes 2359304 | tf_op jit(solution)/shard_map/ppermute | solution.py:625
  18.2 1.6 %collective-permute-start.4 = (bf16[576,128]{1,0:T(8,128)(2,1)S(1)}, bf16[576,128]{1,0:T(8,128)(2,1)S(1)}, u32[]{:S(2)}, u32[]{:S(2)}) collective-permute-start(bf16[576,128]{1,0:T(8,128)(2,1)S(1)} %get-tuple-element.69), channel_id=1, source_target_pairs={{0,4},{1,5},{2,6},{3,7},{4,0},{5,1},{6,2},{7,3},{8,12},{9,13},{10,... | collective-permute-start | bytes 442376 | tf_op jit(solution)/shard_map/ppermute | solution.py:625
  20.0 3.3 %collective-permute-done.4.refs_1_.code_e = bf16[576,128]{1,0:T(8,128)(2,1)S(1)} collective-permute-done((bf16[576,128]{1,0:T(8,128)(2,1)S(1)}, bf16[576,128]{1,0:T(8,128)(2,1)S(1)}, u32[]{:S(2)}, u32[]{:S(2)}) %collective-permute-start.4) | collective-permute-done | bytes 147488 | tf_op jit(solution)/shard_map/ppermute | solution.py:625
  23.3 3.2 %refine.4 = (bf16[2048,128]{1,0:T(8,128)(2,1)S(1)}, bf16[768,128]{1,0:T(8,128)(2,1)S(1)}, bf16[768,128]{1,0:T(8,128)(2,1)S(1)}, bf16[512,128]{1,0:T(8,128)(2,1)S(1)}, bf16[512,128]{1,0:T(8,128)(2,1)S(1)}) custom-call(bf16[2048,128]{1,0:T(8,128)(2,1)S(1)} %get-tuple-element.68.refs_0_, bf16[576,128]{1,0:T(8,128)(2,1)S(1)} %collective-permute-done.4.refs_1_.code_e, ...), custom_call_target="tpu_custom_call" | custom-call | flops 1509949440 | bytes 1654784 | tf_op jit(solution)/shard_map/refine/pallas_call | solution.py:585
  26.7 4.7 %collective-permute-start.6 = (bf16[768,128]{1,0:T(8,128)(2,1)S(1)}, bf16[768,128]{1,0:T(8,128)(2,1)S(1)}, u32[]{:S(2)}, u32[]{:S(2)}) collective-permute-start(bf16[768,128]{1,0:T(8,128)(2,1)S(1)} %get-tuple-element.74.after), channel_id=1, source_target_pairs={{0,4},{1,5},{2,6},{3,7},{4,0},{5,1},{6,2},{7,3},{8,12},{9,13},{10,... | collective-permute-start | bytes 589832 | tf_op jit(solution)/shard_map/ppermute | solution.py:625
  31.4 0.7 %choices.3 = (bf16[512,128]{1,0:T(8,128)(2,1)S(1)}, bf16[640,256]{1,0:T(8,128)(2,1)S(1)}, bf16[768,256]{1,0:T(8,128)(2,1)S(1)}, bf16[768,256]{1,0:T(8,128)(2,1)S...) custom-call(bf16[64,128]{1,0:T(8,128)(2,1)S(1)} %get-tuple-element.7, ...), custom_call_target="tpu_custom_call" | custom-call | bytes 507904 | tf_op jit(solution)/shard_map/choices/pallas_call | solution.py:585
  32.1 3.6 %collective-permute-done.3.received = bf16[3072,128]{1,0:T(8,128)(2,1)S(1)} collective-permute-done((bf16[3072,128]{1,0:T(8,128)(2,1)S(1)}, bf16[3072,128]{1,0:T(8,128)(2,1)S(1)}, u32[]{:S(2)}, u32[]{:S(2)}) %collective-permute-start.3) | collective-permute-done | bytes 786464 | tf_op jit(solution)/shard_map/ppermute | solution.py:625
  36.2 3.9 %refine.5 = (bf16[2048,128]{1,0:T(8,128)(2,1)S(1)}, bf16[1024,128]{1,0:T(8,128)(2,1)S(1)}, bf16[1024,128]{1,0:T(8,128)(2,1)S(1)}, bf16[512,128]{1,0:T(8,128)(2,1...) custom-call(bf16[2048,128]{1,0:T(8,128)(2,1)S(1)} %gather.3.refs_0_,, ...), custom_call_target="tpu_custom_call", output_to_operand_aliasing={{5}: (20, {}), {6}: (21, {})} | custom-call | flops 1509949440 | bytes 6389760 | tf_op jit(solution)/shard_map/refine/pallas_call | solution.py:585
  40.2 3.1 %collective-permute-start.9 = (bf16[1024,128]{1,0:T(8,128)(2,1)S(1)}, bf16[1024,128]{1,0:T(8,128)(2,1)S(1)}, u32[]{:S(2)}, u32[]{:S(2)}) collective-permute-start(bf16[1024,128]{1,0:T(8,128)(2,1)S(1)} %get-tuple-element.92.after), channel_id=1, source_target_pairs={{0,4},{1,5},{2,6},{3,7},{4,0},{5,1},{6,2},{7,3},{8,12},{9,13},{10,... | collective-permute-start | bytes 786440 | tf_op jit(solution)/shard_map/ppermute | solution.py:625
  43.6 0.7 %choices.4 = (bf16[512,128]{1,0:T(8,128)(2,1)S(1)}, bf16[640,256]{1,0:T(8,128)(2,1)S(1)}, bf16[768,256]{1,0:T(8,128)(2,1)S(1)}, bf16[768,256]{1,0:T(8,128)(2,1)S...) custom-call(bf16[64,128]{1,0:T(8,128)(2,1)S(1)} %get-tuple-element.7, ...), custom_call_target="tpu_custom_call" | custom-call | bytes 573440 | tf_op jit(solution)/shard_map/choices/pallas_call | solution.py:585
  44.7 4.2 %collective-permute-done.9.refs_1_.refs_6_ = bf16[1024,128]{1,0:T(8,128)(2,1)S(1)} collective-permute-done((bf16[1024,128]{1,0:T(8,128)(2,1)S(1)}, bf16[1024,128]{1,0:T(8,128)(2,1)S(1)}, u32[]{:S(2)}, u32[]{:S(2)}) %collective-permute-start.9) | collective-permute-done | bytes 262176 | tf_op jit(solution)/shard_map/ppermute | solution.py:625
  48.9 4.1 %refine.6 = (bf16[2048,128]{1,0:T(8,128)(2,1)S(1)}, bf16[1024,128]{1,0:T(8,128)(2,1)S(1)}, bf16[1024,128]{1,0:T(8,128)(2,1)S(1)}, bf16[512,128]{1,0:T(8,128)(2,1...) custom-call(bf16[2048,128]{1,0:T(8,128)(2,1)S(1)} %gather.4.refs_22_, ...), custom_call_target="tpu_custom_call", output_to_operand_aliasing={{5}: (20, {}), {6}: (21, {})} | custom-call | flops 1509949440 | bytes 6750208 | tf_op jit(solution)/shard_map/refine/pallas_call | solution.py:585
  53.2 3.0 %collective-permute-start.12 = (bf16[1024,128]{1,0:T(8,128)(2,1)S(1)}, bf16[1024,128]{1,0:T(8,128)(2,1)S(1)}, u32[]{:S(2)}, u32[]{:S(2)}) collective-permute-start(bf16[1024,128]{1,0:T(8,128)(2,1)S(1)} %get-tuple-element.109.after), channel_id=1, source_target_pairs={{0,4},{1,5},{2,6},{3,7},{4,0},{5,1},{6,2},{7,3},{8,12},{9,13},{10,... | collective-permute-start | bytes 786440 | tf_op jit(solution)/shard_map/ppermute | solution.py:625
  56.5 1.0 %collective-permute-done.14.refs_15_ = bf16[512,128]{1,0:T(8,128)(2,1)S(1)} collective-permute-done((bf16[512,128]{1,0:T(8,128)(2,1)S(1)}, bf16[512,128]{1,0:T(8,128)(2,1)S(1)}, u32[]{:S(2)}, u32[]{:S(2)}) %collective-permute-start.14) | collective-permute-done | bytes 131104 | tf_op jit(solution)/shard_map/ppermute | solution.py:625
  57.5 4.4 %collective-permute-done.12.refs_1_.refs_6_ = bf16[1024,128]{1,0:T(8,128)(2,1)S(1)} collective-permute-done((bf16[1024,128]{1,0:T(8,128)(2,1)S(1)}, bf16[1024,128]{1,0:T(8,128)(2,1)S(1)}, u32[]{:S(2)}, u32[]{:S(2)}) %collective-permute-start.12) | collective-permute-done | bytes 262176 | tf_op jit(solution)/shard_map/ppermute | solution.py:625
  61.9 2.8 %refine.7 = (bf16[512,128]{1,0:T(8,128)(2,1)S(1)}, bf16[512,128]{1,0:T(8,128)(2,1)S(1)}, bf16[2048,128]{1,0:T(8,128)(2,1)}, bf16[2048,128]{1,0:T(8,128)(2,1)}) custom-call(bf16[2048,128]{1,0:T(8,128)(2,1)S(1)} %gather.5.refs_22_.refs_0_, ...), custom_call_target="tpu_custom_call", output_to_operand_aliasing={{2}: (16, {}), {3}: (17, {})} | custom-call | flops 1509949440 | bytes 5963776 | tf_op jit(solution)/shard_map/refine/pallas_call | solution.py:585
  64.7 1.3 %collective-permute-done.15.back = bf16[512,128]{1,0:T(8,128)(2,1)S(1)} collective-permute-done((bf16[512,128]{1,0:T(8,128)(2,1)S(1)}, bf16[512,128]{1,0:T(8,128)(2,1)S(1)}, u32[]{:S(2)}, u32[]{:S(2)}) %collective-permute-start.15) | collective-permute-done | bytes 131104 | tf_op jit(solution)/shard_map/ppermute | solution.py:625
  66.1 0.7 %finish.1 = (bf16[2048,128]{1,0:T(8,128)(2,1)}, bf16[2048,128]{1,0:T(8,128)(2,1)}) custom-call(bf16[512,128]{1,0:T(8,128)(2,1)S(1)} %get-tuple-element.122.own, bf16[512,128]{1,0:T(8,128)(2,1)S(1)} %collective-permute-done.15.back, bf16[2048,128]{1,0:T(8,128)(2,1)} %get-tuple-element.124.out_a, ...), custom_call_target="tpu_custom_call", output_to_operand_aliasing={{0}: (2, {}), {1}: (3, {})} | custom-call | bytes 1310720 | tf_op jit(solution)/shard_map/finish/pallas_call | solution.py:585
  (30 shorter events, 3.2 us)
Async XLA Ops:
  1.9 1.6 %collective-permute-start = (bf16[784,128]{1,0:T(8,128)(2,1)S(1)}, bf16[784,128]{1,0:T(8,128)(2,1)S(1)}, u32[]{:S(2)}, u32[]{:S(2)}) collective-permute-start(bf16[784,128]{1,0:T(8,128)(2,1)S(1)} %get-tuple-element.66), channel_id=1, source_target_pairs={{0,1},{1,0},{2,3},{3,2},{4,5},{5,4},{6,7},{7,6},{8,9},{9,8},{10,11... | collective-permute-start | bytes 602120 | tf_op jit(solution)/shard_map/ppermute | solution.py:625
  4.6 15.2 %copy-start = (bf16[2,4,9,64,64]{4,3,2,1,0:T(8,128)(2,1)S(1)}, bf16[2,4,9,64,64]{4,3,2,1,0:T(8,128)(2,1)}, u32[]{:S(2)}) copy-start(bf16[2,4,9,64,64]{4,3,2,1,0:T(8,128)(2,1)} %conv.1) | copy-start | bytes 1769476
  4.6 15.2 %copy-start.1 = (bf16[2,64,128]{2,1,0:T(8,128)(2,1)S(1)}, bf16[2,64,128]{2,1,0:T(8,128)(2,1)}, u32[]{:S(2)}) copy-start(bf16[2,64,128]{2,1,0:T(8,128)(2,1)} %join.1) | copy-start | bytes 98308
  4.6 3.1 %collective-permute-start.2 = (bf16[1536,128]{1,0:T(8,128)(2,1)S(1)}, bf16[1536,128]{1,0:T(8,128)(2,1)S(1)}, u32[]{:S(2)}, u32[]{:S(2)}) collective-permute-start(bf16[1536,128]{1,0:T(8,128)(2,1)S(1)} %pack_rest.1), channel_id=1, source_target_pairs={{0,1},{1,0},{2,3},{3,2},{4,5},{5,4},{6,7},{7,6},{8,9},{9,8},{10,11... | collective-permute-start | bytes 1179656 | tf_op jit(solution)/shard_map/ppermute | solution.py:625
  5.1 11.0 %collective-permute-start.1 = (bf16[1312,128]{1,0:T(8,128)(2,1)S(1)}, bf16[1312,128]{1,0:T(8,128)(2,1)S(1)}, u32[]{:S(2)}, u32[]{:S(2)}) collective-permute-start(bf16[1312,128]{1,0:T(8,128)(2,1)S(1)} %pair_first.1.after.pair), channel_id=1, source_target_pairs={{0,2},{1,3},{2,0},{3,1},{4,6},{5,7},{6,4},{7,5},{8,10},{9,11},{10,... | collective-permute-start | bytes 1007624 | tf_op jit(solution)/shard_map/ppermute | solution.py:625
  16.4 19.3 %collective-permute-start.3 = (bf16[3072,128]{1,0:T(8,128)(2,1)S(1)}, bf16[3072,128]{1,0:T(8,128)(2,1)S(1)}, u32[]{:S(2)}, u32[]{:S(2)}) collective-permute-start(bf16[3072,128]{1,0:T(8,128)(2,1)S(1)} %get-tuple-element.67.pair), channel_id=1, source_target_pairs={{0,2},{1,3},{2,0},{3,1},{4,6},{5,7},{6,4},{7,5},{8,10},{9,11},{10,... | collective-permute-start | bytes 2359304 | tf_op jit(solution)/shard_map/ppermute | solution.py:625
  18.2 5.1 %collective-permute-start.4 = (bf16[576,128]{1,0:T(8,128)(2,1)S(1)}, bf16[576,128]{1,0:T(8,128)(2,1)S(1)}, u32[]{:S(2)}, u32[]{:S(2)}) collective-permute-start(bf16[576,128]{1,0:T(8,128)(2,1)S(1)} %get-tuple-element.69), channel_id=1, source_target_pairs={{0,4},{1,5},{2,6},{3,7},{4,0},{5,1},{6,2},{7,3},{8,12},{9,13},{10,... | collective-permute-start | bytes 442376 | tf_op jit(solution)/shard_map/ppermute | solution.py:625
  19.8 3.6 %collective-permute-start.5 = (bf16[576,128]{1,0:T(8,128)(2,1)S(1)}, bf16[576,128]{1,0:T(8,128)(2,1)S(1)}, u32[]{:S(2)}, u32[]{:S(2)}) collective-permute-start(bf16[576,128]{1,0:T(8,128)(2,1)S(1)} %get-tuple-element.70), channel_id=1, source_target_pairs={{0,1},{1,0},{2,3},{3,2},{4,8},{5,9},{6,10},{7,11},{8,4},{9,5},{10,... | collective-permute-start | bytes 442376 | tf_op jit(solution)/shard_map/ppermute | solution.py:625
  26.6 9.6 %collective-permute-start.7 = (bf16[768,128]{1,0:T(8,128)(2,1)S(1)}, bf16[768,128]{1,0:T(8,128)(2,1)S(1)}, u32[]{:S(2)}, u32[]{:S(2)}) collective-permute-start(bf16[768,128]{1,0:T(8,128)(2,1)S(1)} %get-tuple-element.77), channel_id=1, source_target_pairs={{0,1},{1,0},{2,3},{3,2},{4,8},{5,9},{6,10},{7,11},{8,4},{9,5},{10,... | collective-permute-start | bytes 589832 | tf_op jit(solution)/shard_map/ppermute | solution.py:625
  26.7 9.5 %collective-permute-start.6 = (bf16[768,128]{1,0:T(8,128)(2,1)S(1)}, bf16[768,128]{1,0:T(8,128)(2,1)S(1)}, u32[]{:S(2)}, u32[]{:S(2)}) collective-permute-start(bf16[768,128]{1,0:T(8,128)(2,1)S(1)} %get-tuple-element.74.after), channel_id=1, source_target_pairs={{0,4},{1,5},{2,6},{3,7},{4,0},{5,1},{6,2},{7,3},{8,12},{9,13},{10,... | collective-permute-start | bytes 589832 | tf_op jit(solution)/shard_map/ppermute | solution.py:625
  31.4 4.8 %collective-permute-start.8 = (bf16[512,128]{1,0:T(8,128)(2,1)S(1)}, bf16[512,128]{1,0:T(8,128)(2,1)S(1)}, u32[]{:S(2)}, u32[]{:S(2)}) collective-permute-start(bf16[512,128]{1,0:T(8,128)(2,1)S(1)} %get-tuple-element.89.after), channel_id=1, source_target_pairs={{0,1},{1,0},{2,3},{3,2},{4,5},{5,4},{6,7},{7,6},{8,9},{9,8},{10,11... | collective-permute-start | bytes 393224 | tf_op jit(solution)/shard_map/ppermute | solution.py:625
  40.1 4.6 %collective-permute-start.10 = (bf16[1024,128]{1,0:T(8,128)(2,1)S(1)}, bf16[1024,128]{1,0:T(8,128)(2,1)S(1)}, u32[]{:S(2)}, u32[]{:S(2)}) collective-permute-start(bf16[1024,128]{1,0:T(8,128)(2,1)S(1)} %get-tuple-element.93), channel_id=1, source_target_pairs={{0,1},{1,0},{2,3},{3,2},{4,8},{5,9},{6,10},{7,11},{8,4},{9,5},{10,... | collective-permute-start | bytes 786440 | tf_op jit(solution)/shard_map/ppermute | solution.py:625
  40.2 8.7 %collective-permute-start.9 = (bf16[1024,128]{1,0:T(8,128)(2,1)S(1)}, bf16[1024,128]{1,0:T(8,128)(2,1)S(1)}, u32[]{:S(2)}, u32[]{:S(2)}) collective-permute-start(bf16[1024,128]{1,0:T(8,128)(2,1)S(1)} %get-tuple-element.92.after), channel_id=1, source_target_pairs={{0,4},{1,5},{2,6},{3,7},{4,0},{5,1},{6,2},{7,3},{8,12},{9,13},{10,... | collective-permute-start | bytes 786440 | tf_op jit(solution)/shard_map/ppermute | solution.py:625
  43.4 1.3 %collective-permute-start.11 = (bf16[512,128]{1,0:T(8,128)(2,1)S(1)}, bf16[512,128]{1,0:T(8,128)(2,1)S(1)}, u32[]{:S(2)}, u32[]{:S(2)}) collective-permute-start(bf16[512,128]{1,0:T(8,128)(2,1)S(1)} %get-tuple-element.106), channel_id=1, source_target_pairs={{0,1},{1,0},{2,3},{3,2},{4,5},{5,4},{6,7},{7,6},{8,9},{9,8},{10,11... | collective-permute-start | bytes 393224 | tf_op jit(solution)/shard_map/ppermute | solution.py:625
  53.1 4.4 %collective-permute-start.13 = (bf16[1024,128]{1,0:T(8,128)(2,1)S(1)}, bf16[1024,128]{1,0:T(8,128)(2,1)S(1)}, u32[]{:S(2)}, u32[]{:S(2)}) collective-permute-start(bf16[1024,128]{1,0:T(8,128)(2,1)S(1)} %get-tuple-element.110), channel_id=1, source_target_pairs={{0,1},{1,0},{2,3},{3,2},{4,8},{5,9},{6,10},{7,11},{8,4},{9,5},{10,... | collective-permute-start | bytes 786440 | tf_op jit(solution)/shard_map/ppermute | solution.py:625
  53.2 8.7 %collective-permute-start.12 = (bf16[1024,128]{1,0:T(8,128)(2,1)S(1)}, bf16[1024,128]{1,0:T(8,128)(2,1)S(1)}, u32[]{:S(2)}, u32[]{:S(2)}) collective-permute-start(bf16[1024,128]{1,0:T(8,128)(2,1)S(1)} %get-tuple-element.109.after), channel_id=1, source_target_pairs={{0,4},{1,5},{2,6},{3,7},{4,0},{5,1},{6,2},{7,3},{8,12},{9,13},{10,... | collective-permute-start | bytes 786440 | tf_op jit(solution)/shard_map/ppermute | solution.py:625
  56.1 1.3 %collective-permute-start.14 = (bf16[512,128]{1,0:T(8,128)(2,1)S(1)}, bf16[512,128]{1,0:T(8,128)(2,1)S(1)}, u32[]{:S(2)}, u32[]{:S(2)}) collective-permute-start(bf16[512,128]{1,0:T(8,128)(2,1)S(1)} %get-tuple-element.119), channel_id=1, source_target_pairs={{0,1},{1,0},{2,3},{3,2},{4,5},{5,4},{6,7},{7,6},{8,9},{9,8},{10,11... | collective-permute-start | bytes 393224 | tf_op jit(solution)/shard_map/ppermute | solution.py:625
  64.7 1.4 %collective-permute-start.15 = (bf16[512,128]{1,0:T(8,128)(2,1)S(1)}, bf16[512,128]{1,0:T(8,128)(2,1)S(1)}, u32[]{:S(2)}, u32[]{:S(2)}) collective-permute-start(bf16[512,128]{1,0:T(8,128)(2,1)S(1)} %get-tuple-element.123), channel_id=1, source_target_pairs={{0,1},{1,0},{2,3},{3,2},{4,5},{5,4},{6,7},{7,6},{8,9},{9,8},{10,11... | collective-permute-start | bytes 393224 | tf_op jit(solution)/shard_map/ppermute | solution.py:625
where the time goes:
time: 67.1 us; the launch traced here: 66.9 us
  waiting for transfers between devices  26.4 us (39%)
  Pallas kernels  21.5 us (32%)
  starting transfers between devices  18.1 us (27%)
  between operations  0.96 us (1%)
    ppermute x16, waiting for transfers between devices, send(): return lax.ppermute(value, 'tiles', pairs)  26.4 us
    pallas_call x18, Pallas kernels, call(): pl.pallas_call(kernel, out_shape=[jax.ShapeDtypeStruct(o, BF) for o in ou...  21.5 us
    ppermute x16, starting transfers between devices, send(): return lax.ppermute(value, 'tiles', pairs)  18.1 us
  transfers between devices with their start and end apart: 16, of which 9 were waited for; matrix products, arithmetic and copies ran while one was open for 0% of the time, Pallas kernels for 11%

commit v1 on v0

--- a/solution.py
+++ b/solution.py
@@ -47,7 +47,7 @@
     dst[...] = tmp[...].astype(BF)
 
 
-def pack_first_kernel(ch, crow, frames, motion_f, motion_b, mine, other, following, motion_buf, tmp, sems):
+def pack_first_kernel(ch, crow, frames, motion_f, motion_b, mine, other, rest, following, motion_buf, tmp, sems):
     place = Place()
     steps, strip = frames.shape[:2]
     half = HALO * ch
@@ -61,7 +61,11 @@
         back = 1 - core if n else core
         copies.append(frame_copy(frames, 0, back, outs[n].at[pl.ds(0, strip)], sems.at[n]))
         copies.append(frame_copy(frames, 1, back, following.at[n], sems.at[2 + n]))
-    for copy in lists + copies:
+    later = [
+        frame_copy(frames, step, 1 - core, rest.at[pl.ds((step - 1) * strip, strip)], sems.at[5 + step])
+        for step in range(1, steps)
+    ]
+    for copy in lists + copies + later:
         copy.start()
     for copy in lists:
         copy.wait()
@@ -93,9 +97,11 @@
         for r in range(HALO):
             row = tmp[pl.ds(place.side * (BS - HALO) + r, ch, stride=BS), :]
             out[pl.ds(strip + crow + r * ch, ch), :] = row.astype(BF)
-
-
-def pair_first_kernel(ch, crow, mine, swapped, out):
+    for copy in later:
+        copy.wait()
+
+
+def pair_first_kernel(ch, crow, mine, swapped, rest_in, out, rest_out):
     place = Place()
     strip = BS * ch
     half = HALO * ch
@@ -112,20 +118,6 @@
 def frame_copy(frames, step, back, out, sem):
     steps = frames.shape[0]
     return pltpu.make_async_copy(frames.at[step + back * (steps - 1 - 2 * step)], out, sem)
-
-
-def pack_rest_kernel(frames, after, other, sems):
-    steps = frames.shape[0]
-    strip = frames.shape[1]
-    core = Place().core
-    copies = [
-        frame_copy(frames, step, 1 - core, other.at[pl.ds((step - 1) * strip, strip)], sems.at[step - 1])
-        for step in range(1, steps)
-    ]
-    for copy in copies:
-        copy.start()
-    for copy in copies:
-        copy.wait()
 
 
 def pair_copies(frames, swapped, core, first, count, out, sems):
@@ -142,15 +134,18 @@
     return copies
 
 
-def pair_kernel(first, count, frames, swapped, out, sems):
-    copies = pair_copies(frames, swapped, Place().core, first, count, out, sems)
+def pair_kernel(many, frames, swapped, near_out, far_out, sems):
+    steps = frames.shape[0]
+    core = Place().core
+    copies = pair_copies(frames, swapped, core, 1, many, near_out, sems)
+    copies += pair_copies(frames, swapped, core, 1 + many, steps - 1 - many, far_out, sems.at[pl.ds(2 * many, 2 * (steps - 1 - many))])
     for copy in copies:
         copy.start()
     for copy in copies:
         copy.wait()
 
 
-def gather_first_kernel(ch, crow, pair, received, rest, xq, codes, msg_e, msg_o, rest_out, tmp, edges):
+def gather_first_kernel(ch, crow, pair, received, near_in, xq, codes, msg_e, msg_o, near_out, tmp, edges):
     place = Place()
     strip = BS * ch
     half = HALO * ch
@@ -365,6 +360,150 @@
     msg_o[...] = sent[par]
 
 
+class Rows:
+    def __init__(self, ch, width, top_ok, bottom_ok, count):
+        lane = lax.broadcasted_iota(jnp.int32, (ch, width), 1)
+        self.not_first = lane > 0
+        self.not_last = lane < width - 1
+        self.zero = jnp.zeros((ch, width), BF)
+        self.top_ok = top_ok
+        self.bottom_ok = bottom_ok
+        self.count = count
+
+    def active(self, value, row):
+        act = leaky(value)
+        if row < 0:
+            act = jnp.where(self.top_ok, act, self.zero)
+        if row >= self.count:
+            act = jnp.where(self.bottom_ok, act, self.zero)
+        return (
+            jnp.where(self.not_first, pltpu.roll(act, 1, 1), self.zero),
+            act,
+            jnp.where(self.not_last, pltpu.roll(act, act.shape[1] - 1, 1), self.zero),
+        )
+
+    def put(self, buf, here, value, row):
+        for n, act in enumerate(self.active(value, row)):
+            buf[n, here, :] = act
+
+
+OFF = 8
+
+
+def here_of(row, ch, count=1):
+    return pl.ds((row + OFF) * ch, count * ch)
+
+
+def conv_layer(ch, weight, source, held, start, stop, emit):
+    width = held.shape[1]
+    for first in range(start, stop, 4):
+        sides = [
+            jnp.concatenate([source[n, here_of(first + 2 * h - 1, ch, 4), :] for n in range(3)], axis=0)
+            for h in range(2)
+        ]
+        out = jnp.dot(weight, jnp.concatenate(sides, axis=1), preferred_element_type=F32)
+        for h in range(2):
+            for q in range(2):
+                row = first + 2 * h + q
+                total = held[here_of(row, ch), :].astype(F32)
+                total += out[q * ch : (q + 1) * ch, h * width : (h + 1) * width]
+                emit(row, total.astype(BF))
+
+
+def join_first_rows(ch, join_mat, inp):
+    width = inp.shape[1]
+    mixed = jnp.dot(
+        join_mat, jnp.concatenate([inp[: 2 * ch], inp[2 * ch :]], axis=1), preferred_element_type=F32
+    ).astype(BF)
+    return [mixed[q * ch : (q + 1) * ch, h * width : (h + 1) * width] for h in range(2) for q in range(2)]
+
+
+def inner_kernel(ch, xq, join, conv, feat, saved, saved_held, act_a, act_b, held):
+    rows = QUAD * BS
+    layers = conv.shape[0]
+    space = Rows(ch, xq.shape[1], True, True, rows)
+    for buf in (act_a, act_b):
+        for row in (-1, rows):
+            for n in range(3):
+                buf[n, here_of(row, ch), :] = space.zero
+    join_mat = join[...]
+    for first in range(0, rows, 4):
+        for n, value in enumerate(join_first_rows(ch, join_mat, xq[pl.ds(first * ch, 4 * ch), :])):
+            held[here_of(first + n, ch), :] = value
+            space.put(act_a, here_of(first + n, ch), value, first + n)
+    source, target = act_a, act_b
+    for layer in range(layers):
+        for side, row, both in ((0, layer, layer), (1, rows - 1 - layer, rows - 2 - layer)):
+            for n in range(3):
+                saved[layer, side, n] = source[n, here_of(both, ch, 2), :]
+            saved_held[layer, side] = held[here_of(row, ch), :]
+        edge = (layer + 1) // 2 * 2
+
+        def emit(row, value, layer=layer, target=target):
+            if layer < layers - 1:
+                held[here_of(row, ch), :] = value
+                space.put(target, here_of(row, ch), value, row)
+            else:
+                feat[pl.ds(row * ch, ch), :] = value
+
+        conv_layer(ch, conv[layer], source, held, edge, rows - edge, emit)
+        source, target = target, source
+
+
+def outer_kernel(ch, steps, *refs):
+    feat_in, saved, saved_held, halo_e, halo_o, join, conv, codes, far_in, *refs = refs
+    fout, msg_e, msg_o, own_out, part_out, far_out, tmp, sent, *choices = refs
+    half = HALO * ch
+    strip = BS * ch
+    rows = QUAD * BS
+    place = Place()
+    layers = conv.shape[0]
+    width = feat_in.shape[1]
+    space = Rows(ch, width, jnp.logical_not(place.top), jnp.logical_not(place.bottom), rows)
+    code = step_codes(ch, place, 1, steps, codes, halo_e, halo_o)
+    code.rank_all(all_pairs(TO_ABOVE, TO_BELOW))
+    for item, out in zip(SENT, choices):
+        send_choice(code, *item, out)
+    fout[pl.ds(half, (rows - 2 * HALO) * ch), :] = feat_in[pl.ds(half, (rows - 2 * HALO) * ch), :]
+    odd = place.odd == 1
+    one, two = halo_e[pl.ds(0, half), :].astype(F32), halo_o[pl.ds(0, half), :].astype(F32)
+    halos = [jnp.where(odd, one, two).astype(BF), jnp.where(odd, two, one).astype(BF)]
+    join_mat = join[...]
+    values = [join_first_rows(ch, join_mat, halo) for halo in halos]
+    starts = [-HALO, rows]
+    for layer in range(layers):
+        weight = conv[layer]
+        for side in range(2):
+            acts = [space.active(value, starts[side] + n) for n, value in enumerate(values[side])]
+            kept = [
+                tuple(saved[layer, side, n, pl.ds(m * ch, ch), :] for n in range(3)) for m in range(2)
+            ]
+            beside = saved_held[layer, side]
+            if side == 0:
+                window, base = acts + kept, values[side][1:] + [beside]
+                starts[side] += 1
+            else:
+                window, base = kept + acts, [beside] + values[side][:3]
+                starts[side] -= 1
+            halves = [
+                jnp.concatenate([window[2 * h + m][n] for n in range(3) for m in range(4)], axis=0) for h in range(2)
+            ]
+            out = jnp.dot(weight, jnp.concatenate(halves, axis=1), preferred_element_type=F32)
+            values[side] = [
+                (
+                    base[2 * h + q].astype(F32) + out[q * ch : (q + 1) * ch, h * width : (h + 1) * width]
+                ).astype(BF)
+                for h in range(2)
+                for q in range(2)
+            ]
+    for side in range(2):
+        for n, value in enumerate(values[side]):
+            fout[pl.ds((starts[side] + n) * ch, ch), :] = value
+    pack_messages(ch, fout, place.odd, sent, choices, msg_e, msg_o)
+    channels_first(fout, pl.multiple_of(place.strip * strip, strip), own_out, tmp, ch)
+    channels_first(fout, pl.multiple_of((place.strip ^ 1) * strip, strip), part_out, tmp, ch)
+
+
 def step_kernel(ch, step, steps, *refs):
     strip = BS * ch
     half = HALO * ch
@@ -377,24 +516,13 @@
         return taken
 
     xq, halo_e, halo_o, join, conv = take(5)
-    if step > 0:
-        feat, feat_e, feat_o = take(3)
-        choices = take(len(PARTS) + (0 if last else len(SENT)))
-        before, back, out_a, out_b = take(4)
-        if not last:
-            (x_next,) = take(1)
-    else:
-        (codes,) = take(1)
+    feat, feat_e, feat_o = take(3)
+    choices = take(len(PARTS) + (0 if last else len(SENT)))
+    before, back, out_a, out_b = take(4)
     if not last:
-        fout, msg_e, msg_o = take(3)
-    own_out, part_out = take(2)
-    if step > 0:
-        out_f, out_g = take(2)
-    tmp, act_a, act_b, held, xext = take(5)
-    if step > 0:
-        sems, aligned, recv = take(3)
-    else:
-        choices = take(len(SENT))
+        x_next, fout, msg_e, msg_o = take(4)
+    own_out, part_out, out_f, out_g = take(4)
+    tmp, act_a, act_b, held, xext, sems, aligned, recv = take(8)
     if last:
         (fout,) = take(1)
     else:
@@ -408,97 +536,67 @@
     right_side = place.side
     own = place.core if last else place.strip
 
-    copies = []
-    if step > 0:
-        copies = result_copies(strip, step - 1, steps, before, back, out_f, out_g, sems)
-        for n, copy in copies:
-            pl.when(core == n)(copy.start)
-    halo_at = (0, half)[step] if step < 2 else 3 * half
-
+    copies = result_copies(strip, step - 1, steps, before, back, out_f, out_g, sems)
+    for n, copy in copies:
+        pl.when(core == n)(copy.start)
+    halo_at = half if step == 1 else 3 * half
     above = pl.ds(pl.multiple_of((1 - par) * (quad_rows + HALO) * ch, half), half)
     below = pl.ds(pl.multiple_of(par * (quad_rows + HALO) * ch, half), half)
     xext[above, :] = halo_e[pl.ds(halo_at, half), :]
     xext[below, :] = halo_o[pl.ds(halo_at, half), :]
     xext[pl.ds(half, quad_rows * ch), :] = xq[...]
-    if step > 0:
-        recv[1 - par] = feat_e[pl.ds(0, 3 * half), :]
-        recv[par] = feat_o[pl.ds(0, 3 * half), :]
-        if last:
-
-            @pl.when(right_side == 0)
-            def _():
-                for n in range(3):
-                    align(ch, feat, recv, aligned, HALO, PARTS[n], choices[n])
-                align(ch, feat, recv, aligned, HALO, PARTS[3], choices[3], 0)
-
-            @pl.when(right_side == 1)
-            def _():
-                offset = HALO - 2 * BS
-                align(ch, feat, recv, aligned, offset, PARTS[2], choices[2], 1)
-                for n in range(3, 6):
-                    align(ch, feat, recv, aligned, offset, PARTS[n], choices[n])
-
-        else:
-            for n, rows_part in enumerate(PARTS):
-                align(ch, feat, recv, aligned, HALO, rows_part, choices[n])
-            sent[0, pl.ds(3 * half, half), :] = x_next[pl.ds(0, half), :]
-            sent[1, pl.ds(3 * half, half), :] = x_next[pl.ds((quad_rows - HALO) * ch, half), :]
+    recv[1 - par] = feat_e[pl.ds(0, 3 * half), :]
+    recv[par] = feat_o[pl.ds(0, 3 * half), :]
+    if last:
+
+        @pl.when(right_side == 0)
+        def _():
+            for n in range(3):
+                align(ch, feat, recv, aligned, HALO, PARTS[n], choices[n])
+            align(ch, feat, recv, aligned, HALO, PARTS[3], choices[3], 0)
+
+        @pl.when(right_side == 1)
+        def _():
+            offset = HALO - 2 * BS
+            align(ch, feat, recv, aligned, offset, PARTS[2], choices[2], 1)
+            for n in range(3, 6):
+                align(ch, feat, recv, aligned, offset, PARTS[n], choices[n])
+
     else:
-        code = step_codes(ch, place, 1, steps, codes, halo_e, halo_o)
-        code.rank_all(all_pairs(TO_ABOVE, TO_BELOW))
-        for item, out in zip(SENT, choices):
-            send_choice(code, *item, out)
-
-    off = 8
+        for n, rows_part in enumerate(PARTS):
+            align(ch, feat, recv, aligned, HALO, rows_part, choices[n])
+        sent[0, pl.ds(3 * half, half), :] = x_next[pl.ds(0, half), :]
+        sent[1, pl.ds(3 * half, half), :] = x_next[pl.ds((quad_rows - HALO) * ch, half), :]
+
     top_ok = jnp.logical_not(place.top)
     bottom_ok = jnp.logical_not(place.bottom)
     if last:
         top_ok = top_ok | (right_side == 1)
         bottom_ok = bottom_ok | (right_side == 0)
     start_row = right_side * (2 * BS) if last else 0
-    lane = lax.broadcasted_iota(jnp.int32, (ch, width), 1)
-    not_first = lane > 0
-    not_last = lane < width - 1
-    zero = jnp.zeros((ch, width), BF)
-
-    def put(buf, row, act):
-        if row < 0:
-            act = jnp.where(top_ok, act, zero)
-        if row >= rows:
-            act = jnp.where(bottom_ok, act, zero)
-        here = pl.ds((row + off) * ch, ch)
-        buf[0, here, :] = jnp.where(not_first, pltpu.roll(act, 1, 1), zero)
-        buf[1, here, :] = act
-        buf[2, here, :] = jnp.where(not_last, pltpu.roll(act, width - 1, 1), zero)
-
+    space = Rows(ch, width, top_ok, bottom_ok, rows)
     for buf in (act_a, act_b):
         for row in (-HALO - 1, rows + HALO):
             for n in range(3):
-                buf[n, pl.ds((row + off) * ch, ch), :] = zero
+                buf[n, here_of(row, ch), :] = space.zero
 
     join_mat = join[...]
     for g in range((rows + 2 * HALO) // 4):
         first = g * 4 - HALO
         at = (start_row + g * 4) * ch
         inp = xext[pl.ds(pl.multiple_of(at, 4 * ch) if last else at, 4 * ch), :]
-        if step == 0:
-            right = jnp.concatenate([inp[: 2 * ch], inp[2 * ch :]], axis=1)
-        else:
-            al = aligned[pl.ds(g * 4 * ch, 4 * ch), :]
-            sides = []
-            for h in range(2):
-                a, b = 2 * h * ch, (2 * h + 1) * ch
-                sides.append(
-                    jnp.concatenate([al[a : a + ch], inp[a : a + ch], al[b : b + ch], inp[b : b + ch]], axis=0)
-                )
-            right = jnp.concatenate(sides, axis=1)
-        mixed = jnp.dot(join_mat, right, preferred_element_type=F32).astype(BF)
+        al = aligned[pl.ds(g * 4 * ch, 4 * ch), :]
+        sides = []
+        for h in range(2):
+            a, b = 2 * h * ch, (2 * h + 1) * ch
+            sides.append(jnp.concatenate([al[a : a + ch], inp[a : a + ch], al[b : b + ch], inp[b : b + ch]], axis=0))
+        mixed = jnp.dot(join_mat, jnp.concatenate(sides, axis=1), preferred_element_type=F32).astype(BF)
         for h in range(2):
             for q in range(2):
                 row = first + 2 * h + q
                 value = mixed[q * ch : (q + 1) * ch, h * width : (h + 1) * width]
-                held[pl.ds((row + off) * ch, ch), :] = value
-                put(act_a, row, leaky(value))
+                held[here_of(row, ch), :] = value
+                space.put(act_a, here_of(row, ch), value, row)
 
     layers = conv.shape[0]
     source, target = act_a, act_b
@@ -508,24 +606,15 @@
         start, stop = -reach, rows + reach
         if (stop - start) % 4:
             start, stop = -HALO, rows + HALO
-        weight = conv[layer]
-        for first in range(start, stop, 4):
-            sides = [
-                jnp.concatenate([source[n, pl.ds((first + 2 * h - 1 + off) * ch, 4 * ch), :] for n in range(3)], axis=0)
-                for h in range(2)
-            ]
-            out = jnp.dot(weight, jnp.concatenate(sides, axis=1), preferred_element_type=F32)
-            for h in range(2):
-                for q in range(2):
-                    row = first + 2 * h + q
-                    here = pl.ds((row + off) * ch, ch)
-                    total = held[here, :].astype(F32) + out[q * ch : (q + 1) * ch, h * width : (h + 1) * width]
-                    value = total.astype(BF)
-                    if layer < layers - 1:
-                        held[here, :] = value
-                        put(target, row, leaky(value))
-                    else:
-                        fout[pl.ds(row * ch, ch), :] = value
+
+        def emit(row, value, layer=layer, target=target):
+            if layer < layers - 1:
+                held[here_of(row, ch), :] = value
+                space.put(target, here_of(row, ch), value, row)
+            else:
+                fout[pl.ds(row * ch, ch), :] = value
+
+        conv_layer(ch, conv[layer], source, held, start, stop, emit)
         source, target = target, source
 
     if not last:
@@ -580,7 +669,7 @@
 HBM = pl.BlockSpec(memory_space=pltpu.HBM)
 
 
-def call(kernel, name, args, outs, scratch=(), flops=0, in_any=(), out_any=(), aliases=None, in_hbm=()):
+def call(kernel, name, args, outs, scratch=(), flops=0, in_any=(), out_any=(), aliases=None, in_hbm=(), free=False):
     args = [pltpu.with_memory_space_constraint(a, pltpu.HBM) if n in in_hbm else a for n, a in enumerate(args)]
     return pl.pallas_call(
         kernel,
@@ -591,7 +680,9 @@
         input_output_aliases=aliases or {},
         compiler_params=pltpu.CompilerParams(vmem_limit_bytes=32 << 20),
         cost_estimate=pl.CostEstimate(
-            flops=flops, bytes_accessed=sum(a.size * a.dtype.itemsize for a in args), transcendentals=0
+            flops=flops,
+            bytes_accessed=0 if free else sum(a.size * a.dtype.itemsize for a in args),
+            transcendentals=0,
         ),
         name=name,
     )(*args)
@@ -631,47 +722,42 @@
     feature = (rows * ch, width)
     whole = (steps * strip, width)
     flat = frames.reshape(steps, strip, width)
-    mine, other = call(
+    later = ((steps - 1) * strip, width)
+    mine, other, rest = call(
         functools.partial(pack_first_kernel, ch, crow),
         "pack_first",
         (flat, motion_forward, motion_backward),
-        [(strip + crow + half, width)] * 2,
+        [(strip + crow + half, width)] * 2 + [later],
         [
             pltpu.VMEM((2, *piece), BF),
             pltpu.VMEM((2, *motion_forward.shape), jnp.int32),
             tmp,
-            pltpu.SemaphoreType.DMA((6,)),
+            pltpu.SemaphoreType.DMA((5 + steps,)),
         ],
         in_hbm=(0, 1, 2),
+        out_any=(2,),
     )
-    (pair,) = call(
+    pair, rest = call(
         functools.partial(pair_first_kernel, ch, crow),
         "pair_first",
-        (mine, send(other, near(1))),
-        [(2 * (strip + crow) + half, width)],
+        (mine, send(other, near(1)), rest),
+        [(2 * (strip + crow) + half, width), later],
+        in_any=(2,),
+        out_any=(1,),
+        aliases={2: 1},
     )
     received = send(pair, near(2))
-    (rest,) = call(
-        pack_rest_kernel,
-        "pack_rest",
-        (flat, pair),
-        [((steps - 1) * strip, width)],
-        [pltpu.SemaphoreType.DMA((steps - 1,))],
+    swapped = send(rest, near(1))
+    soon = min(2, steps - 1)
+    pair_near, pair_far = call(
+        functools.partial(pair_kernel, soon),
+        "pair_rest",
+        (flat, swapped),
+        [(2 * soon * strip, width), (2 * (steps - 1 - soon) * strip, width)],
+        [pltpu.SemaphoreType.DMA((2 * (steps - 1),))],
         in_hbm=(0,),
         in_any=(1,),
-        out_any=(0,),
-    )
-    swapped = send(rest, near(1))
-    many = 2 * (steps - 1)
-    (pair_rest,) = call(
-        functools.partial(pair_kernel, 1, steps - 1),
-        "pair_rest",
-        (flat, swapped),
-        [(many * strip, width)],
-        [pltpu.SemaphoreType.DMA((many,))],
-        in_hbm=(0,),
-        in_any=(1,),
-        out_any=(0,),
+        out_any=(0, 1),
     )
     layers = conv_weight.shape[1]
     conv, join_both, join_first = call(
@@ -679,91 +765,100 @@
         "weights",
         (conv_weight, join_weight),
         [(layers, 2 * ch, 12 * ch), (2 * ch, 4 * ch), (2 * ch, 2 * ch)],
+        free=True,
     )
-    xq, codes, edge_e, edge_o, pair_rest = call(
+    xq, codes, edge_e, edge_o, pair_near = call(
         functools.partial(gather_first_kernel, ch, crow),
         "gather_first",
-        (pair, received, pair_rest),
-        [feature, (QUAD * crow, width)] + [(2 * half + QUAD * crow, width)] * 2 + [pair_rest.shape],
+        (pair, received, pair_near),
+        [feature, (QUAD * crow, width)] + [(2 * half + QUAD * crow, width)] * 2 + [pair_near.shape],
         [tmp, pltpu.VMEM((2, half, width), BF)],
         in_any=(2,),
         out_any=(4,),
         aliases={2: 4},
     )
     halo_e, halo_o = code_e, code_o = send(edge_e, even), send(edge_o, odd)
-    received_rest = send(pair_rest, near(2))
 
     wide_act = pltpu.VMEM((3, (rows + 16) * ch, width), BF)
     flops = 2 * (rows + 2 * HALO) * width * ch * ch * 9 * layers
     part_shapes, sent_shapes = choice_shapes(width)
-    for step in range(steps):
+    acts = [wide_act, wide_act, pltpu.VMEM(((rows + 16) * ch, width), BF)]
+    inner, saved, saved_held = call(
+        functools.partial(inner_kernel, ch),
+        "refine_inner",
+        (xq, join_first, conv),
+        [feature, (layers, 2, 3, 2 * ch, width), (layers, 2, ch, width)],
+        acts,
+        flops,
+    )
+    received_near = send(pair_near, near(2))
+    feat, msg_e, msg_o, own, part, pair_far = call(
+        functools.partial(outer_kernel, ch, steps),
+        "refine_outer",
+        (inner, saved, saved_held, halo_e, halo_o, join_first, conv, codes, pair_far),
+        [feature, messages[0], messages[0], piece, piece, pair_far.shape],
+        [tmp, pltpu.VMEM((2, *messages[0]), BF)] + [pltpu.VMEM(shape, BF) for shape in sent_shapes],
+        flops // 4,
+        in_any=(8,),
+        out_any=(5,),
+        aliases={8: 5},
+    )
+    feat_e, feat_o = send(msg_e, even), send(msg_o, odd)
+    back = send(part, near(1))
+    received_far = send(pair_far, near(2))
+    outputs = call(lambda after, a, b: None, "results", (part,), [whole, whole], in_any=(0,), out_any=(0, 1), free=True)
+
+    def choices_of(step):
+        return call(
+            functools.partial(choices_kernel, ch, step, steps),
+            "choices",
+            (codes, code_e, code_o, msg_e),
+            part_shapes + (sent_shapes if step + 1 < steps else []),
+            in_any=(3,),
+        )
+
+    def frame_of(step):
+        near_one = step <= soon
+        source = (pair_near, received_near) if near_one else (pair_far, received_far)
+        return call(
+            functools.partial(gather_kernel, ch, step - 1 if near_one else step - 1 - soon),
+            "gather",
+            (*source, msg_e),
+            [feature],
+            [tmp],
+            in_any=(2,),
+        )[0]
+
+    x_now = frame_of(1)
+    for step in range(1, steps):
         last = step == steps - 1
-        args = [xq, halo_e, halo_o, join_both if step else join_first, conv]
+        choices = choices_of(step)
+        args = [x_now, halo_e, halo_o, join_both, conv, feat, feat_e, feat_o, *choices, own, back, *outputs]
+        many = len(args)
         outs = [] if last else [feature, messages[step], messages[step]]
-        outs += [piece, piece]
-        scratch = [tmp, wide_act, wide_act, pltpu.VMEM(((rows + 16) * ch, width), BF)]
-        scratch += [pltpu.VMEM(((rows + 2 * HALO) * ch, width), BF)]
-        if step:
-            args += [feat, feat_e, feat_o, *choices, own, back, *outputs]
-            many = len(args)
-            in_any = (many - 4, many - 3, many - 2, many - 1)
-            aliases = {many - 2: len(outs), many - 1: len(outs) + 1}
-            out_any = (len(outs), len(outs) + 1)
-            outs += [whole, whole]
-            if not last:
-                args += [x_next]
-            scratch += [pltpu.SemaphoreType.DMA((2,))]
-            scratch += [pltpu.VMEM(((rows + 2 * HALO) * ch, width), BF), pltpu.VMEM((2, 3 * half, width), BF)]
-        else:
-            args += [codes]
-            in_any = out_any = ()
-            aliases = {}
-            scratch += [pltpu.VMEM(shape, BF) for shape in sent_shapes]
+        outs += [piece, piece, whole, whole]
+        scratch = [tmp, *acts, pltpu.VMEM(((rows + 2 * HALO) * ch, width), BF), pltpu.SemaphoreType.DMA((2,))]
+        scratch += [pltpu.VMEM(((rows + 2 * HALO) * ch, width), BF), pltpu.VMEM((2, 3 * half, width), BF)]
         scratch += [pltpu.VMEM((2 * strip, width) if last else (2, *messages[step]), BF)]
-        results = call(
+        if not last:
+            x_now = frame_of(step + 1)
+            args += [x_now]
+        *results, own, part, out_f, out_g = call(
             functools.partial(step_kernel, ch, step, steps),
             "refine",
             args,
             outs,
             scratch,
             flops,
-            in_any,
-            out_any,
-            aliases,
+            in_any=(many - 4, many - 3, many - 2, many - 1),
+            out_any=(len(outs) - 2, len(outs) - 1),
+            aliases={many - 2: len(outs) - 2, many - 1: len(outs) - 1},
         )
+        outputs = out_f, out_g
         if not last:
-            feat, msg_e, msg_o, *results = results
-            feat_e, feat_o = send(msg_e, even), send(msg_o, odd)
-            if step:
-                halo_e, halo_o = feat_e, feat_o
-            choices = call(
-                functools.partial(choices_kernel, ch, step + 1, steps),
-                "choices",
-                (codes, code_e, code_o, msg_e),
-                part_shapes + (sent_shapes if step + 2 < steps else []),
-                in_any=(3,),
-            )
-        own, part, *results = results
+            feat, msg_e, msg_o = results
+            halo_e, halo_o = feat_e, feat_o = send(msg_e, even), send(msg_o, odd)
         back = send(part, near(1))
-        if step == 0:
-            outputs = call(lambda after, a, b: None, "results", (part,), [whole, whole], in_any=(0,), out_any=(0, 1))
-
-            def later(frame):
-                return call(
-                    functools.partial(gather_kernel, ch, frame - 1),
-                    "gather",
-                    (pair_rest, received_rest, msg_e),
-                    [feature],
-                    [tmp],
-                    in_any=(2,),
-                )[0]
-
-            xq, x_next = later(1), later(2)
-        else:
-            outputs = results
-            if not last:
-                xq = x_next
-                x_next = later(step + 2) if step + 2 < steps else None
 
     outputs = call(
         functools.partial(finish_kernel, strip, steps),

time: 67.1 us -> 57.8 us (0.86)
  waiting for transfers between devices: 26.4 us -> 18.9 us
  starting transfers between devices: 18.1 us -> 15.9 us
    ppermute x16 -> x17, waiting for transfers between devices: 26.4 us -> 18.9 us  [send(): return lax.ppermute(value, 'tiles', pairs)]
    ppermute x16 -> x17, starting transfers between devices: 18.1 us -> 15.9 us  [send(): return lax.ppermute(value, 'tiles', pairs)]
  transfers between devices with their start and end apart: 16 -> 17, of which waited for: 9 -> 9; matrix products, arithmetic and copies ran while one was open for 0% -> 0% of each run, Pallas kernels for 11% -> 22%
where the time goes in v1:
time: 57.8 us; the launch traced here: 57.6 us
  Pallas kernels  21.9 us (38%)
  waiting for transfers between devices  18.9 us (33%)
  starting transfers between devices  15.9 us (28%)
  between operations  0.94 us (2%)
    pallas_call x18, Pallas kernels, call(): pl.pallas_call(kernel, out_shape=[jax.ShapeDtypeStruct(o, BF) for o in ou...  21.9 us
    ppermute x17, waiting for transfers between devices, send(): return lax.ppermute(value, 'tiles', pairs)  18.9 us
    ppermute x17, starting transfers between devices, send(): return lax.ppermute(value, 'tiles', pairs)  15.9 us
  transfers between devices with their start and end apart: 17, of which 9 were waited for; matrix products, arithmetic and copies ran while one was open for 0% of the time, Pallas kernels for 22%

profile of v1, /device:TPU:0, one launch (start us, length us, event | category | flops | bytes accessed | tf_op | source)
XLA Modules:
  0.0 57.6 jit_solution(12450724954709569476)
XLA Ops:
  0.6 1.3 %pack_first.1 = (bf16[784,128]{1,0:T(8,128)(2,1)S(1)}, bf16[784,128]{1,0:T(8,128)(2,1)S(1)}, bf16[1536,128]{1,0:T(8,128)(2,1)S(1)}) custom-call(bf16[4,512,128]{2,1,0:T(8,128)(2,1)} %bitcast.5, s32[3,16]{1,0:T(4,128)} %motion_f.1, s32[3,16]{1,0:T(4,128)} %motion_b.1), custom_call_target="tpu_custom_call" | custom-call | bytes 524672 | tf_op jit(solution)/shard_map/pack_first/pallas_call | solution.py:674
  2.5 1.1 %collective-permute-done.swapped = bf16[784,128]{1,0:T(8,128)(2,1)S(1)} collective-permute-done((bf16[784,128]{1,0:T(8,128)(2,1)S(1)}, bf16[784,128]{1,0:T(8,128)(2,1)S(1)}, u32[]{:S(2)}, u32[]{:S(2)}) %collective-permute-start) | collective-permute-done | bytes 200736 | tf_op jit(solution)/shard_map/ppermute | solution.py:716
  4.1 2.6 %collective-permute-start.1 = (bf16[1312,128]{1,0:T(8,128)(2,1)S(1)}, bf16[1312,128]{1,0:T(8,128)(2,1)S(1)}, u32[]{:S(2)}, u32[]{:S(2)}) collective-permute-start(bf16[1312,128]{1,0:T(8,128)(2,1)S(1)} %get-tuple-element.77.pair), channel_id=1, source_target_pairs={{0,2},{1,3},{2,0},{3,1},{4,6},{5,7},{6,4},{7,5},{8,10},{9,11},{10,... | collective-permute-start | bytes 1007624 | tf_op jit(solution)/shard_map/ppermute | solution.py:716
  6.7 1.3 %pair_rest.1 = (bf16[2048,128]{1,0:T(8,128)(2,1)S(1)}, bf16[1024,128]{1,0:T(8,128)(2,1)S(1)}) custom-call(bf16[4,512,128]{2,1,0:T(8,128)(2,1)} %bitcast.6, bf16[1536,128]{1,0:T(8,128)(2,1)S(1)} %collective-permute-done.2.swapped), custom_call_target="tpu_custom_call" | custom-call | bytes 917504 | tf_op jit(solution)/shard_map/pair_rest/pallas_call | solution.py:674
  8.0 7.1 %collective-permute-done.1.received = bf16[1312,128]{1,0:T(8,128)(2,1)S(1)} collective-permute-done((bf16[1312,128]{1,0:T(8,128)(2,1)S(1)}, bf16[1312,128]{1,0:T(8,128)(2,1)S(1)}, u32[]{:S(2)}, u32[]{:S(2)}) %collective-permute-start.1) | collective-permute-done | bytes 335904 | tf_op jit(solution)/shard_map/ppermute | solution.py:716
  15.4 1.8 %collective-permute-start.6 = (bf16[2048,128]{1,0:T(8,128)(2,1)S(1)}, bf16[2048,128]{1,0:T(8,128)(2,1)S(1)}, u32[]{:S(2)}, u32[]{:S(2)}) collective-permute-start(bf16[2048,128]{1,0:T(8,128)(2,1)S(1)} %get-tuple-element.91.pair), channel_id=1, source_target_pairs={{0,2},{1,3},{2,0},{3,1},{4,6},{5,7},{6,4},{7,5},{8,10},{9,11},{10,... | collective-permute-start | bytes 1572872 | tf_op jit(solution)/shard_map/ppermute | solution.py:716
  17.2 1.6 %collective-permute-start.3 = (bf16[576,128]{1,0:T(8,128)(2,1)S(1)}, bf16[576,128]{1,0:T(8,128)(2,1)S(1)}, u32[]{:S(2)}, u32[]{:S(2)}) collective-permute-start(bf16[576,128]{1,0:T(8,128)(2,1)S(1)} %get-tuple-element.86), channel_id=1, source_target_pairs={{0,4},{1,5},{2,6},{3,7},{4,0},{5,1},{6,2},{7,3},{8,12},{9,13},{10,... | collective-permute-start | bytes 442376 | tf_op jit(solution)/shard_map/ppermute | solution.py:716
  19.0 2.3 %refine_inner.1 = (bf16[2048,128]{1,0:T(8,128)(2,1)S(1)}, bf16[4,2,3,128,128]{4,3,2,1,0:T(8,128)(2,1)S(1)}, bf16[4,2,64,128]{3,2,1,0:T(8,128)(2,1)S(1)}) custom-call(bf16[2048,128]{1,0:T(8,128)(2,1)S(1)} %get-tuple-element.80.xq, bf16[128,128]{1,0:T(8,128)(2,1)S(1)} %get-tuple-element.81.join.refs_5_, ...), custom_call_target="tpu_custom_call" | custom-call | flops 1509949440 | bytes 1343488 | tf_op jit(solution)/shard_map/refine_inner/pallas_call | solution.py:674
  21.4 1.0 %collective-permute-done.3.refs_3_.code_e.refs_1_ = bf16[576,128]{1,0:T(8,128)(2,1)S(1)} collective-permute-done((bf16[576,128]{1,0:T(8,128)(2,1)S(1)}, bf16[576,128]{1,0:T(8,128)(2,1)S(1)}, u32[]{:S(2)}, u32[]{:S(2)}) %collective-permute-start.3) | collective-permute-done | bytes 147488 | tf_op jit(solution)/shard_map/ppermute | solution.py:716
  22.4 2.2 %refine_outer.1 = (bf16[2048,128]{1,0:T(8,128)(2,1)S(1)}, bf16[768,128]{1,0:T(8,128)(2,1)S(1)}, bf16[768,128]{1,0:T(8,128)(2,1)S(1)}, bf16[512,128]{1,0:T(8,128)...) custom-call(bf16[2048,128]{1,0:T(8,128)(2,1)S(1)} %get-tuple-element.83.re, ...), custom_call_target="tpu_custom_call", output_to_operand_aliasing={{5}: (8, {})} | custom-call | flops 377487360 | bytes 2834432 | tf_op jit(solution)/shard_map/refine_outer/pallas_call | solution.py:674
  24.6 2.8 %collective-permute-start.7 = (bf16[768,128]{1,0:T(8,128)(2,1)S(1)}, bf16[768,128]{1,0:T(8,128)(2,1)S(1)}, u32[]{:S(2)}, u32[]{:S(2)}) collective-permute-start(bf16[768,128]{1,0:T(8,128)(2,1)S(1)} %get-tuple-element.92.after), channel_id=1, source_target_pairs={{0,4},{1,5},{2,6},{3,7},{4,0},{5,1},{6,2},{7,3},{8,12},{9,13},{10,... | collective-permute-start | bytes 589832 | tf_op jit(solution)/shard_map/ppermute | solution.py:716
  28.4 0.7 %choices.3 = (bf16[512,128]{1,0:T(8,128)(2,1)S(1)}, bf16[640,256]{1,0:T(8,128)(2,1)S(1)}, bf16[768,256]{1,0:T(8,128)(2,1)S(1)}, bf16[768,256]{1,0:T(8,128)(2,1)S...) custom-call(bf16[64,128]{1,0:T(8,128)(2,1)S(1)} %get-tuple-element.8, ...), custom_call_target="tpu_custom_call" | custom-call | bytes 507904 | tf_op jit(solution)/shard_map/choices/pallas_call | solution.py:674
  29.6 1.4 %collective-permute-done.7.refs_6_ = bf16[768,128]{1,0:T(8,128)(2,1)S(1)} collective-permute-done((bf16[768,128]{1,0:T(8,128)(2,1)S(1)}, bf16[768,128]{1,0:T(8,128)(2,1)S(1)}, u32[]{:S(2)}, u32[]{:S(2)}) %collective-permute-start.7) | collective-permute-done | bytes 196640 | tf_op jit(solution)/shard_map/ppermute | solution.py:716
  31.0 3.9 %refine.3 = (bf16[2048,128]{1,0:T(8,128)(2,1)S(1)}, bf16[1024,128]{1,0:T(8,128)(2,1)S(1)}, bf16[1024,128]{1,0:T(8,128)(2,1)S(1)}, bf16[512,128]{1,0:T(8,128)(2,1...) custom-call(bf16[2048,128]{1,0:T(8,128)(2,1)S(1)} %gather.3.refs_0_,, ...), custom_call_target="tpu_custom_call", output_to_operand_aliasing={{5}: (20, {}), {6}: (21, {})} | custom-call | flops 1509949440 | bytes 6389760 | tf_op jit(solution)/shard_map/refine/pallas_call | solution.py:674
  34.9 2.2 %collective-permute-start.10 = (bf16[1024,128]{1,0:T(8,128)(2,1)S(1)}, bf16[1024,128]{1,0:T(8,128)(2,1)S(1)}, u32[]{:S(2)}, u32[]{:S(2)}) collective-permute-start(bf16[1024,128]{1,0:T(8,128)(2,1)S(1)} %get-tuple-element.110.after), channel_id=1, source_target_pairs={{0,4},{1,5},{2,6},{3,7},{4,0},{5,1},{6,2},{7,3},{8,12},{9,13},{10,... | collective-permute-start | bytes 786440 | tf_op jit(solution)/shard_map/ppermute | solution.py:716
  37.6 0.7 %choices.4 = (bf16[512,128]{1,0:T(8,128)(2,1)S(1)}, bf16[640,256]{1,0:T(8,128)(2,1)S(1)}, bf16[768,256]{1,0:T(8,128)(2,1)S(1)}, bf16[768,256]{1,0:T(8,128)(2,1)S...) custom-call(bf16[64,128]{1,0:T(8,128)(2,1)S(1)} %get-tuple-element.8, ...), custom_call_target="tpu_custom_call" | custom-call | bytes 573440 | tf_op jit(solution)/shard_map/choices/pallas_call | solution.py:674
  38.8 3.2 %collective-permute-done.10.refs_1_.refs_6_ = bf16[1024,128]{1,0:T(8,128)(2,1)S(1)} collective-permute-done((bf16[1024,128]{1,0:T(8,128)(2,1)S(1)}, bf16[1024,128]{1,0:T(8,128)(2,1)S(1)}, u32[]{:S(2)}, u32[]{:S(2)}) %collective-permute-start.10) | collective-permute-done | bytes 262176 | tf_op jit(solution)/shard_map/ppermute | solution.py:716
  42.0 4.2 %refine.4 = (bf16[2048,128]{1,0:T(8,128)(2,1)S(1)}, bf16[1024,128]{1,0:T(8,128)(2,1)S(1)}, bf16[1024,128]{1,0:T(8,128)(2,1)S(1)}, bf16[512,128]{1,0:T(8,128)(2,1...) custom-call(bf16[2048,128]{1,0:T(8,128)(2,1)S(1)} %gather.4.refs_22_, ...), custom_call_target="tpu_custom_call", output_to_operand_aliasing={{5}: (20, {}), {6}: (21, {})} | custom-call | flops 1509949440 | bytes 6750208 | tf_op jit(solution)/shard_map/refine/pallas_call | solution.py:674
  46.2 1.9 %collective-permute-start.13 = (bf16[1024,128]{1,0:T(8,128)(2,1)S(1)}, bf16[1024,128]{1,0:T(8,128)(2,1)S(1)}, u32[]{:S(2)}, u32[]{:S(2)}) collective-permute-start(bf16[1024,128]{1,0:T(8,128)(2,1)S(1)} %get-tuple-element.127.after), channel_id=1, source_target_pairs={{0,4},{1,5},{2,6},{3,7},{4,0},{5,1},{6,2},{7,3},{8,12},{9,13},{10,... | collective-permute-start | bytes 786440 | tf_op jit(solution)/shard_map/ppermute | solution.py:716
  48.9 0.8 %collective-permute-done.15.refs_15_ = bf16[512,128]{1,0:T(8,128)(2,1)S(1)} collective-permute-done((bf16[512,128]{1,0:T(8,128)(2,1)S(1)}, bf16[512,128]{1,0:T(8,128)(2,1)S(1)}, u32[]{:S(2)}, u32[]{:S(2)}) %collective-permute-start.15) | collective-permute-done | bytes 131104 | tf_op jit(solution)/shard_map/ppermute | solution.py:716
  49.8 2.8 %collective-permute-done.13.refs_1_.refs_6_ = bf16[1024,128]{1,0:T(8,128)(2,1)S(1)} collective-permute-done((bf16[1024,128]{1,0:T(8,128)(2,1)S(1)}, bf16[1024,128]{1,0:T(8,128)(2,1)S(1)}, u32[]{:S(2)}, u32[]{:S(2)}) %collective-permute-start.13) | collective-permute-done | bytes 262176 | tf_op jit(solution)/shard_map/ppermute | solution.py:716
  52.6 2.8 %refine.5 = (bf16[512,128]{1,0:T(8,128)(2,1)S(1)}, bf16[512,128]{1,0:T(8,128)(2,1)S(1)}, bf16[2048,128]{1,0:T(8,128)(2,1)}, bf16[2048,128]{1,0:T(8,128)(2,1)}) custom-call(bf16[2048,128]{1,0:T(8,128)(2,1)S(1)} %gather.5.refs_22_.refs_0_, ...), custom_call_target="tpu_custom_call", output_to_operand_aliasing={{2}: (16, {}), {3}: (17, {})} | custom-call | flops 1509949440 | bytes 5963776 | tf_op jit(solution)/shard_map/refine/pallas_call | solution.py:674
  55.4 1.3 %collective-permute-done.16.back = bf16[512,128]{1,0:T(8,128)(2,1)S(1)} collective-permute-done((bf16[512,128]{1,0:T(8,128)(2,1)S(1)}, bf16[512,128]{1,0:T(8,128)(2,1)S(1)}, u32[]{:S(2)}, u32[]{:S(2)}) %collective-permute-start.16) | collective-permute-done | bytes 131104 | tf_op jit(solution)/shard_map/ppermute | solution.py:716
  56.8 0.7 %finish.1 = (bf16[2048,128]{1,0:T(8,128)(2,1)}, bf16[2048,128]{1,0:T(8,128)(2,1)}) custom-call(bf16[512,128]{1,0:T(8,128)(2,1)S(1)} %get-tuple-element.140.own, bf16[512,128]{1,0:T(8,128)(2,1)S(1)} %collective-permute-done.16.back, bf16[2048,128]{1,0:T(8,128)(2,1)} %get-tuple-element.142.out_a, ...), custom_call_target="tpu_custom_call", output_to_operand_aliasing={{0}: (2, {}), {1}: (3, {})} | custom-call | bytes 1310720 | tf_op jit(solution)/shard_map/finish/pallas_call | solution.py:674
  (32 shorter events, 4.9 us)
Async XLA Ops:
  2.0 1.6 %collective-permute-start = (bf16[784,128]{1,0:T(8,128)(2,1)S(1)}, bf16[784,128]{1,0:T(8,128)(2,1)S(1)}, u32[]{:S(2)}, u32[]{:S(2)}) collective-permute-start(bf16[784,128]{1,0:T(8,128)(2,1)S(1)} %get-tuple-element.75), channel_id=1, source_target_pairs={{0,1},{1,0},{2,3},{3,2},{4,5},{5,4},{6,7},{7,6},{8,9},{9,8},{10,11... | collective-permute-start | bytes 602120 | tf_op jit(solution)/shard_map/ppermute | solution.py:716
  3.6 15.2 %copy-start = (bf16[2,4,9,64,64]{4,3,2,1,0:T(8,128)(2,1)S(1)}, bf16[2,4,9,64,64]{4,3,2,1,0:T(8,128)(2,1)}, u32[]{:S(2)}) copy-start(bf16[2,4,9,64,64]{4,3,2,1,0:T(8,128)(2,1)} %conv.1) | copy-start | bytes 1769476
  3.6 15.2 %copy-start.1 = (bf16[2,64,128]{2,1,0:T(8,128)(2,1)S(1)}, bf16[2,64,128]{2,1,0:T(8,128)(2,1)}, u32[]{:S(2)}) copy-start(bf16[2,64,128]{2,1,0:T(8,128)(2,1)} %join.1) | copy-start | bytes 98308
  3.6 3.1 %collective-permute-start.2 = (bf16[1536,128]{1,0:T(8,128)(2,1)S(1)}, bf16[1536,128]{1,0:T(8,128)(2,1)S(1)}, u32[]{:S(2)}, u32[]{:S(2)}) collective-permute-start(bf16[1536,128]{1,0:T(8,128)(2,1)S(1)} %get-tuple-element.78), channel_id=1, source_target_pairs={{0,1},{1,0},{2,3},{3,2},{4,5},{5,4},{6,7},{7,6},{8,9},{9,8},{10,11... | collective-permute-start | bytes 1179656 | tf_op jit(solution)/shard_map/ppermute | solution.py:716
  4.1 11.0 %collective-permute-start.1 = (bf16[1312,128]{1,0:T(8,128)(2,1)S(1)}, bf16[1312,128]{1,0:T(8,128)(2,1)S(1)}, u32[]{:S(2)}, u32[]{:S(2)}) collective-permute-start(bf16[1312,128]{1,0:T(8,128)(2,1)S(1)} %get-tuple-element.77.pair), channel_id=1, source_target_pairs={{0,2},{1,3},{2,0},{3,1},{4,6},{5,7},{6,4},{7,5},{8,10},{9,11},{10,... | collective-permute-start | bytes 1007624 | tf_op jit(solution)/shard_map/ppermute | solution.py:716
  15.4 13.7 %collective-permute-start.6 = (bf16[2048,128]{1,0:T(8,128)(2,1)S(1)}, bf16[2048,128]{1,0:T(8,128)(2,1)S(1)}, u32[]{:S(2)}, u32[]{:S(2)}) collective-permute-start(bf16[2048,128]{1,0:T(8,128)(2,1)S(1)} %get-tuple-element.91.pair), channel_id=1, source_target_pairs={{0,2},{1,3},{2,0},{3,1},{4,6},{5,7},{6,4},{7,5},{8,10},{9,11},{10,... | collective-permute-start | bytes 1572872 | tf_op jit(solution)/shard_map/ppermute | solution.py:716
  17.2 5.1 %collective-permute-start.3 = (bf16[576,128]{1,0:T(8,128)(2,1)S(1)}, bf16[576,128]{1,0:T(8,128)(2,1)S(1)}, u32[]{:S(2)}, u32[]{:S(2)}) collective-permute-start(bf16[576,128]{1,0:T(8,128)(2,1)S(1)} %get-tuple-element.86), channel_id=1, source_target_pairs={{0,4},{1,5},{2,6},{3,7},{4,0},{5,1},{6,2},{7,3},{8,12},{9,13},{10,... | collective-permute-start | bytes 442376 | tf_op jit(solution)/shard_map/ppermute | solution.py:716
  18.8 3.6 %collective-permute-start.4 = (bf16[576,128]{1,0:T(8,128)(2,1)S(1)}, bf16[576,128]{1,0:T(8,128)(2,1)S(1)}, u32[]{:S(2)}, u32[]{:S(2)}) collective-permute-start(bf16[576,128]{1,0:T(8,128)(2,1)S(1)} %get-tuple-element.87), channel_id=1, source_target_pairs={{0,1},{1,0},{2,3},{3,2},{4,8},{5,9},{6,10},{7,11},{8,4},{9,5},{10,... | collective-permute-start | bytes 442376 | tf_op jit(solution)/shard_map/ppermute | solution.py:716
  24.6 6.4 %collective-permute-start.7 = (bf16[768,128]{1,0:T(8,128)(2,1)S(1)}, bf16[768,128]{1,0:T(8,128)(2,1)S(1)}, u32[]{:S(2)}, u32[]{:S(2)}) collective-permute-start(bf16[768,128]{1,0:T(8,128)(2,1)S(1)} %get-tuple-element.92.after), channel_id=1, source_target_pairs={{0,4},{1,5},{2,6},{3,7},{4,0},{5,1},{6,2},{7,3},{8,12},{9,13},{10,... | collective-permute-start | bytes 589832 | tf_op jit(solution)/shard_map/ppermute | solution.py:716
  27.3 3.7 %collective-permute-start.8 = (bf16[768,128]{1,0:T(8,128)(2,1)S(1)}, bf16[768,128]{1,0:T(8,128)(2,1)S(1)}, u32[]{:S(2)}, u32[]{:S(2)}) collective-permute-start(bf16[768,128]{1,0:T(8,128)(2,1)S(1)} %get-tuple-element.95), channel_id=1, source_target_pairs={{0,1},{1,0},{2,3},{3,2},{4,8},{5,9},{6,10},{7,11},{8,4},{9,5},{10,... | collective-permute-start | bytes 589832 | tf_op jit(solution)/shard_map/ppermute | solution.py:716
  27.3 2.3 %collective-permute-start.9 = (bf16[512,128]{1,0:T(8,128)(2,1)S(1)}, bf16[512,128]{1,0:T(8,128)(2,1)S(1)}, u32[]{:S(2)}, u32[]{:S(2)}) collective-permute-start(bf16[512,128]{1,0:T(8,128)(2,1)S(1)} %get-tuple-element.107.after), channel_id=1, source_target_pairs={{0,1},{1,0},{2,3},{3,2},{4,5},{5,4},{6,7},{7,6},{8,9},{9,8},{10,11... | collective-permute-start | bytes 393224 | tf_op jit(solution)/shard_map/ppermute | solution.py:716
  27.8 10.5 %collective-permute-start.5 = (bf16[1024,128]{1,0:T(8,128)(2,1)S(1)}, bf16[1024,128]{1,0:T(8,128)(2,1)S(1)}, u32[]{:S(2)}, u32[]{:S(2)}) collective-permute-start(bf16[1024,128]{1,0:T(8,128)(2,1)S(1)} %get-tuple-element.90.pair), channel_id=1, source_target_pairs={{0,2},{1,3},{2,0},{3,1},{4,6},{5,7},{6,4},{7,5},{8,10},{9,11},{10,... | collective-permute-start | bytes 786440 | tf_op jit(solution)/shard_map/ppermute | solution.py:716
  34.9 7.1 %collective-permute-start.10 = (bf16[1024,128]{1,0:T(8,128)(2,1)S(1)}, bf16[1024,128]{1,0:T(8,128)(2,1)S(1)}, u32[]{:S(2)}, u32[]{:S(2)}) collective-permute-start(bf16[1024,128]{1,0:T(8,128)(2,1)S(1)} %get-tuple-element.110.after), channel_id=1, source_target_pairs={{0,4},{1,5},{2,6},{3,7},{4,0},{5,1},{6,2},{7,3},{8,12},{9,13},{10,... | collective-permute-start | bytes 786440 | tf_op jit(solution)/shard_map/ppermute | solution.py:716
  37.1 4.9 %collective-permute-start.11 = (bf16[1024,128]{1,0:T(8,128)(2,1)S(1)}, bf16[1024,128]{1,0:T(8,128)(2,1)S(1)}, u32[]{:S(2)}, u32[]{:S(2)}) collective-permute-start(bf16[1024,128]{1,0:T(8,128)(2,1)S(1)} %get-tuple-element.111), channel_id=1, source_target_pairs={{0,1},{1,0},{2,3},{3,2},{4,8},{5,9},{6,10},{7,11},{8,4},{9,5},{10,... | collective-permute-start | bytes 786440 | tf_op jit(solution)/shard_map/ppermute | solution.py:716
  37.1 1.7 %collective-permute-start.12 = (bf16[512,128]{1,0:T(8,128)(2,1)S(1)}, bf16[512,128]{1,0:T(8,128)(2,1)S(1)}, u32[]{:S(2)}, u32[]{:S(2)}) collective-permute-start(bf16[512,128]{1,0:T(8,128)(2,1)S(1)} %get-tuple-element.124), channel_id=1, source_target_pairs={{0,1},{1,0},{2,3},{3,2},{4,5},{5,4},{6,7},{7,6},{8,9},{9,8},{10,11... | collective-permute-start | bytes 393224 | tf_op jit(solution)/shard_map/ppermute | solution.py:716
  46.2 6.4 %collective-permute-start.13 = (bf16[1024,128]{1,0:T(8,128)(2,1)S(1)}, bf16[1024,128]{1,0:T(8,128)(2,1)S(1)}, u32[]{:S(2)}, u32[]{:S(2)}) collective-permute-start(bf16[1024,128]{1,0:T(8,128)(2,1)S(1)} %get-tuple-element.127.after), channel_id=1, source_target_pairs={{0,4},{1,5},{2,6},{3,7},{4,0},{5,1},{6,2},{7,3},{8,12},{9,13},{10,... | collective-permute-start | bytes 786440 | tf_op jit(solution)/shard_map/ppermute | solution.py:716
  48.0 4.6 %collective-permute-start.14 = (bf16[1024,128]{1,0:T(8,128)(2,1)S(1)}, bf16[1024,128]{1,0:T(8,128)(2,1)S(1)}, u32[]{:S(2)}, u32[]{:S(2)}) collective-permute-start(bf16[1024,128]{1,0:T(8,128)(2,1)S(1)} %get-tuple-element.128), channel_id=1, source_target_pairs={{0,1},{1,0},{2,3},{3,2},{4,8},{5,9},{6,10},{7,11},{8,4},{9,5},{10,... | collective-permute-start | bytes 786440 | tf_op jit(solution)/shard_map/ppermute | solution.py:716
  48.0 1.7 %collective-permute-start.15 = (bf16[512,128]{1,0:T(8,128)(2,1)S(1)}, bf16[512,128]{1,0:T(8,128)(2,1)S(1)}, u32[]{:S(2)}, u32[]{:S(2)}) collective-permute-start(bf16[512,128]{1,0:T(8,128)(2,1)S(1)} %get-tuple-element.137), channel_id=1, source_target_pairs={{0,1},{1,0},{2,3},{3,2},{4,5},{5,4},{6,7},{7,6},{8,9},{9,8},{10,11... | collective-permute-start | bytes 393224 | tf_op jit(solution)/shard_map/ppermute | solution.py:716
  55.4 1.4 %collective-permute-start.16 = (bf16[512,128]{1,0:T(8,128)(2,1)S(1)}, bf16[512,128]{1,0:T(8,128)(2,1)S(1)}, u32[]{:S(2)}, u32[]{:S(2)}) collective-permute-start(bf16[512,128]{1,0:T(8,128)(2,1)S(1)} %get-tuple-element.141), channel_id=1, source_target_pairs={{0,1},{1,0},{2,3},{3,2},{4,5},{5,4},{6,7},{7,6},{8,9},{9,8},{10,11... | collective-permute-start | bytes 393224 | tf_op jit(solution)/shard_map/ppermute | solution.py:716

commit v2 on v1

--- a/solution.py
+++ b/solution.py
@@ -101,18 +101,29 @@
         copy.wait()
 
 
-def pair_first_kernel(ch, crow, mine, swapped, rest_in, out, rest_out):
+def pair_first_kernel(ch, crow, mine, swapped, rest_in, out, edge, rest_out, tmp):
     place = Place()
     strip = BS * ch
     half = HALO * ch
     for n, piece in enumerate((mine, swapped)):
         at = place.core ^ n
         out[pl.ds(pl.multiple_of(at * strip, strip), strip), :] = piece[pl.ds(0, strip), :]
-        out[pl.ds(pl.multiple_of(2 * strip + at * crow, crow), crow), :] = piece[pl.ds(strip, crow), :]
+        for ref, start in ((out, 2 * strip), (edge, 2 * half)):
+            ref[pl.ds(pl.multiple_of(start + at * crow, crow), crow), :] = piece[pl.ds(strip, crow), :]
 
         @pl.when(at == place.side)
         def _(piece=piece):
-            out[pl.ds(2 * (strip + crow), half), :] = piece[pl.ds(strip + crow, half), :]
+            tmp[...] = piece[pl.ds(0, strip), :].astype(F32)
+            for r in range(HALO):
+                row = tmp[pl.ds(place.side * (BS - HALO) + r, ch, stride=BS), :]
+                edge[pl.ds(r * ch, ch), :] = row.astype(BF)
+            edge[pl.ds(half, half), :] = piece[pl.ds(strip + crow, half), :]
+
+
+def above_below(place, along, cross):
+    left = place.side == 0
+    along, cross = along.astype(F32), cross.astype(F32)
+    return jnp.where(left, cross, along).astype(BF), jnp.where(left, along, cross).astype(BF)
 
 
 def frame_copy(frames, step, back, out, sem):
@@ -134,21 +145,46 @@
     return copies
 
 
-def pair_kernel(many, frames, swapped, near_out, far_out, sems):
-    steps = frames.shape[0]
-    core = Place().core
-    copies = pair_copies(frames, swapped, core, 1, many, near_out, sems)
-    copies += pair_copies(frames, swapped, core, 1 + many, steps - 1 - many, far_out, sems.at[pl.ds(2 * many, 2 * (steps - 1 - many))])
+def edge_rows(place, ch, pair, outer, out, start, tmp):
+    strip = BS * ch
+    one, two = pair[pl.ds(0, strip), :].astype(F32), pair[pl.ds(strip, strip), :].astype(F32)
+    left = place.side == 0
+    if outer:
+        tmp[...] = jnp.where(left, one, two)
+        first = place.side * (BS - HALO)
+    else:
+        tmp[...] = jnp.where(left, two, one)
+        first = (1 - place.side) * (BS - HALO)
+    for r in range(HALO):
+        out[pl.ds(start + r * ch, ch), :] = tmp[pl.ds(first + r, ch, stride=BS), :].astype(BF)
+
+
+def pair_kernel(ch, frames, swapped, near_out, far_out, last_out, tmp, sems):
+    place = Place()
+    steps, strip = frames.shape[:2]
+    half = HALO * ch
+    between = range(2, steps - 1)
+    pairs = {1: near_out.at[pl.ds(0, 2 * strip)], steps - 1: last_out}
+    for n, step in enumerate(between):
+        pairs[step] = far_out.at[pl.ds(2 * n * strip, 2 * strip)]
+    copies = []
+    for step, out in pairs.items():
+        copies += pair_copies(frames, swapped, place.core, step, 1, out, sems.at[pl.ds(2 * step, 2)])
     for copy in copies:
         copy.start()
     for copy in copies:
         copy.wait()
-
-
-def gather_first_kernel(ch, crow, pair, received, near_in, xq, codes, msg_e, msg_o, near_out, tmp, edges):
+    edge_rows(place, ch, pairs[2], True, near_out, 2 * strip, tmp)
+    at = 2 * len(between) * strip
+    for step in range(3, steps):
+        edge_rows(place, ch, pairs[step], True, far_out, at, tmp)
+        at += half
+    edge_rows(place, ch, last_out, False, far_out, at, tmp)
+
+
+def gather_first_kernel(ch, crow, pair, received, near_in, conv, xq, codes, near_out, tmp):
     place = Place()
     strip = BS * ch
-    half = HALO * ch
     for n, piece in enumerate((pair, received)):
         side = place.side ^ n
         for m in range(2):
@@ -156,23 +192,24 @@
             rows_first(piece, m * strip, xq, pl.multiple_of(at * strip, strip), tmp, ch)
             code_at = pl.multiple_of(at * crow, crow)
             codes[pl.ds(code_at, crow), :] = piece[pl.ds(2 * strip + m * crow, crow), :]
-        edges[side] = piece[pl.ds(2 * (strip + crow), half), :]
-    low = (QUAD * BS - HALO) * ch
-    msg_e[pl.ds(0, half), :] = xq[pl.ds(pl.multiple_of(low - place.odd * low, half), half), :]
-    msg_o[pl.ds(0, half), :] = xq[pl.ds(pl.multiple_of(place.odd * low, half), half), :]
-    msg_e[pl.ds(half, half), :] = edges[1 - place.odd]
-    msg_o[pl.ds(half, half), :] = edges[place.odd]
-    msg_e[pl.ds(2 * half, codes.shape[0]), :] = codes[...]
-    msg_o[pl.ds(2 * half, codes.shape[0]), :] = codes[...]
-
-
-def gather_kernel(ch, at, pair, received, after, xq, tmp):
+
+
+def gather_kernel(ch, pair_at, edge_at, pair, received, after, xq, edges, tmp):
     strip = BS * ch
+    half = HALO * ch
     side = Place().side
     for n, piece in enumerate((pair, received)):
         for m in range(2):
             start = ((side + n) % 2 * 2 + m) * strip
-            rows_first(piece, (2 * at + m) * strip, xq, pl.multiple_of(start, strip), tmp, ch)
+            rows_first(piece, pair_at + m * strip, xq, pl.multiple_of(start, strip), tmp, ch)
+        edges[side ^ n] = piece[pl.ds(edge_at, half), :]
+
+
+def gather_last_kernel(ch, inner_at, pair, received, after, xq, inner, tmp):
+    strip = BS * ch
+    for m in range(2):
+        rows_first(pair, m * strip, xq, m * strip, tmp, ch)
+    inner[...] = received[pl.ds(inner_at, HALO * ch), :]
 
 
 class Codes:
@@ -225,36 +262,31 @@
         )
 
 
-FROM_ABOVE = (((0, -2), (-1, -2), (-1, -3)), ((1, -1), (0, -1), (0, -2)))
+FROM_ABOVE = (((0, -2), (-1, -2), (-1, -3), (1, -1)), ((0, -1), (0, -2)))
 FROM_BELOW = (
-    ((QUAD - 1, QUAD + 1), (QUAD, QUAD + 1), (QUAD, QUAD + 2)),
-    ((QUAD - 2, QUAD), (QUAD - 1, QUAD), (QUAD - 1, QUAD + 1)),
+    ((QUAD - 1, QUAD + 1), (QUAD, QUAD + 1), (QUAD, QUAD + 2), (QUAD - 2, QUAD)),
+    ((QUAD - 1, QUAD), (QUAD - 1, QUAD + 1)),
 )
 TO_BELOW = tuple(tuple((d + QUAD, s + QUAD) for d, s in tile) for tile in FROM_ABOVE)
 TO_ABOVE = tuple(tuple((d - QUAD, s - QUAD) for d, s in tile) for tile in FROM_BELOW)
 
 
-def step_codes(ch, place, step, steps, codes, halo_e, halo_o):
+def step_codes(ch, place, step, steps, codes, along, cross):
     crow = codes.shape[0] // QUAD
     width = codes.shape[1]
     pick = place.core * (steps - 1) + step - 1
     row_id = lax.broadcasted_iota(jnp.int32, (crow, width), 0)
-
-    def row(ref, start):
-        block = ref[pl.ds(start, crow), :].astype(F32)
-        return jnp.sum(jnp.where(row_id == pick, block, 0.0), axis=0, keepdims=True)
-
-    odd = place.odd == 1
-    half = HALO * ch
-
-    def beside(strip, above):
-        e = row(halo_e, 2 * half + strip * crow)
-        o = row(halo_o, 2 * half + strip * crow)
-        return jnp.where(odd, e, o) if above else jnp.where(odd, o, e)
-
-    rows = [beside(QUAD - 2, True), beside(QUAD - 1, True)]
-    rows += [row(codes, strip * crow) for strip in range(QUAD)]
-    rows += [beside(0, False), beside(1, False)]
+    start = 2 * HALO * ch
+    above, below = above_below(
+        place, along[pl.ds(start, 2 * crow), :], cross[pl.ds(start, 2 * crow), :]
+    )
+
+    def row(block):
+        return jnp.sum(jnp.where(row_id == pick, block.astype(F32), 0.0), axis=0, keepdims=True)
+
+    rows = [row(above[n * crow : (n + 1) * crow]) for n in range(2)]
+    rows += [row(codes[pl.ds(strip * crow, crow), :]) for strip in range(QUAD)]
+    rows += [row(below[n * crow : (n + 1) * crow]) for n in range(2)]
     return Codes(rows)
 
 
@@ -266,7 +298,7 @@
     for side, near, tables in ((0, -1, FROM_ABOVE), (1, QUAD, FROM_BELOW)):
         if any(abs(near - d) <= REACH for d in dests):
             whole = bottom if side == 0 else not bottom
-            tiles += [(side, 0), (side, 1)] if whole else [(side, 2)]
+            tiles += [(side, 0), (side, 1)] if whole else [(side, 1), (side, 2)]
     return tiles
 
 
@@ -279,10 +311,11 @@
             elif tile[1] == 0:
                 value = code.plain(dest, -1 if tile[0] == 0 else QUAD)
             else:
-                table = (FROM_ABOVE, FROM_BELOW)[tile[0]][tile[1] - 1]
-                value = sum(
-                    (code.packed(d, source, at) for at, (d, source) in enumerate(table) if d == dest), code.zero
-                )
+                side, kind = tile
+                regions = list(enumerate((FROM_ABOVE, FROM_BELOW)[side][kind - 1]))
+                if kind == 1:
+                    regions = regions[:3] if bottom == (side == 0) else regions[3:]
+                value = sum((code.packed(d, source, at) for at, (d, source) in regions if d == dest), code.zero)
             out[pl.ds(n * width, width), pl.ds(m * width, width)] = value
 
 
@@ -290,30 +323,32 @@
 
 
 def sent_regions(side, tile):
-    regions = (TO_ABOVE, TO_BELOW)[side][tile]
-    return regions, sorted({source for _, source in regions})
+    picks = {}
+    for at, (dest, source) in enumerate((TO_ABOVE, TO_BELOW)[side][tile]):
+        lower = (side == 1) == (tile == 0 and at < 3)
+        picks.setdefault((source, lower), []).append((at, dest))
+    return picks
 
 
 def send_choice(code, side, tile, out):
-    regions, sources = sent_regions(side, tile)
     width = out.shape[1]
-    for n, source in enumerate(sources):
-        total = sum(code.pack(d, source, at) for at, (d, origin) in enumerate(regions) if origin == source)
+    for n, ((source, _), regions) in enumerate(sent_regions(side, tile).items()):
+        total = sum(code.pack(dest, source, at) for at, dest in regions)
         out[pl.ds(n * width, width), :] = total.astype(BF)
 
 
 def all_pairs(*tables):
-    return [pair for table in tables for tile in table for pair in tile]
-
-
-def choices_kernel(ch, step, steps, codes, code_e, code_o, after, *outs):
+    return sorted({pair for table in tables for tile in table for pair in tile})
+
+
+def choices_kernel(ch, step, steps, codes, along, cross, after, *outs):
     place = Place()
-    code = step_codes(ch, place, step, steps, codes, code_e, code_o)
+    code = step_codes(ch, place, step, steps, codes, along, cross)
     code.rank_all(all_pairs(FROM_ABOVE, FROM_BELOW))
     for part, out in zip(PARTS, outs):
         receive_choice(code, *part, out)
     if step + 1 < steps:
-        code = step_codes(ch, place, step + 1, steps, codes, code_e, code_o)
+        code = step_codes(ch, place, step + 1, steps, codes, along, cross)
         code.rank_all(all_pairs(TO_ABOVE, TO_BELOW))
         for item, out in zip(SENT, outs[len(PARTS) :]):
             send_choice(code, *item, out)
@@ -321,7 +356,7 @@
 
 def choice_shapes(width):
     parts = [(len(tiles_of(*part)) * width, len(part[0]) * width) for part in PARTS]
-    return parts, [(len(sent_regions(*item)[1]) * width, width) for item in SENT]
+    return parts, [(len(sent_regions(*item)) * width, width) for item in SENT]
 
 
 def align(ch, feat, recv, aligned, offset, part, choice, only=None):
@@ -348,16 +383,32 @@
 def pack_messages(ch, fout, par, sent, choices, msg_e, msg_o):
     half = HALO * ch
     strip = BS * ch
+    width = fout.shape[1]
     for side, near in ((0, 0), (1, QUAD - 1)):
         shift = half if side == 1 else 0
         sent[side, pl.ds(0, half), :] = fout[pl.ds(near * strip + shift, half), :]
     for (side, tile), choice in zip(SENT, choices):
-        shift = half if (side == 1) == (tile == 0) else 0
-        left = [fout[pl.ds(source * strip + shift, half), :] for source in sent_regions(side, tile)[1]]
-        got = jnp.dot(jnp.concatenate(left, axis=1), choice[...], preferred_element_type=F32)
-        sent[side, pl.ds((tile + 1) * half, half), :] = got.astype(BF)
+        left = [
+            fout[pl.ds(source * strip + (half if lower else 0), half), :] for source, lower in sent_regions(side, tile)
+        ]
+        got = jnp.dot(jnp.concatenate(left, axis=1), choice[...], preferred_element_type=F32).astype(BF)
+        if tile == 0:
+            sent[side, pl.ds(half, half), :] = got
+        else:
+            lane = lax.broadcasted_iota(jnp.int32, (half // 2, width), 1)
+            folded = jnp.where(lane < width // 2, got[: half // 2], pltpu.roll(got[half // 2 :], width // 2, 1))
+            sent[side, pl.ds(2 * half, half // 2), :] = folded
     msg_e[...] = sent[1 - par]
     msg_o[...] = sent[par]
+
+
+def unpack_message(ch, message, recv, side):
+    half = HALO * ch
+    width = message.shape[1]
+    recv[side, pl.ds(0, 2 * half), :] = message[pl.ds(0, 2 * half), :]
+    folded = message[pl.ds(2 * half, half // 2), :]
+    recv[side, pl.ds(2 * half, half // 2), :] = folded
+    recv[side, pl.ds(2 * half + half // 2, half // 2), :] = pltpu.roll(folded, width // 2, 1)
 
 
 class Rows:
@@ -416,6 +467,34 @@
         join_mat, jnp.concatenate([inp[: 2 * ch], inp[2 * ch :]], axis=1), preferred_element_type=F32
     ).astype(BF)
     return [mixed[q * ch : (q + 1) * ch, h * width : (h + 1) * width] for h in range(2) for q in range(2)]
+
+
+def clear_outside(space, ch, rows, bufs):
+    for buf in bufs:
+        for row in (-HALO - 1, rows + HALO):
+            for n in range(3):
+                buf[n, here_of(row, ch), :] = space.zero
+
+
+def conv_layers(ch, conv, space, rows, act_a, act_b, held, fout):
+    layers = conv.shape[0]
+    source, target = act_a, act_b
+    for layer in range(layers):
+        need = layers - 1 - layer
+        reach = -(-need // 2) * 2
+        start, stop = -reach, rows + reach
+        if (stop - start) % 4:
+            start, stop = -HALO, rows + HALO
+
+        def emit(row, value, layer=layer, target=target):
+            if layer < layers - 1:
+                held[here_of(row, ch), :] = value
+                space.put(target, here_of(row, ch), value, row)
+            else:
+                fout[pl.ds(row * ch, ch), :] = value
+
+        conv_layer(ch, conv[layer], source, held, start, stop, emit)
+        source, target = target, source
 
 
 def inner_kernel(ch, xq, join, conv, feat, saved, saved_held, act_a, act_b, held):
@@ -451,7 +530,7 @@
 
 
 def outer_kernel(ch, steps, *refs):
-    feat_in, saved, saved_held, halo_e, halo_o, join, conv, codes, far_in, *refs = refs
+    feat_in, saved, saved_held, along, cross, join, conv, codes, far_in, *refs = refs
     fout, msg_e, msg_o, own_out, part_out, far_out, tmp, sent, *choices = refs
     half = HALO * ch
     strip = BS * ch
@@ -460,14 +539,12 @@
     layers = conv.shape[0]
     width = feat_in.shape[1]
     space = Rows(ch, width, jnp.logical_not(place.top), jnp.logical_not(place.bottom), rows)
-    code = step_codes(ch, place, 1, steps, codes, halo_e, halo_o)
+    code = step_codes(ch, place, 1, steps, codes, along, cross)
     code.rank_all(all_pairs(TO_ABOVE, TO_BELOW))
     for item, out in zip(SENT, choices):
         send_choice(code, *item, out)
     fout[pl.ds(half, (rows - 2 * HALO) * ch), :] = feat_in[pl.ds(half, (rows - 2 * HALO) * ch), :]
-    odd = place.odd == 1
-    one, two = halo_e[pl.ds(0, half), :].astype(F32), halo_o[pl.ds(0, half), :].astype(F32)
-    halos = [jnp.where(odd, one, two).astype(BF), jnp.where(odd, two, one).astype(BF)]
+    halos = above_below(place, along[pl.ds(0, half), :], cross[pl.ds(0, half), :])
     join_mat = join[...]
     values = [join_first_rows(ch, join_mat, halo) for halo in halos]
     starts = [-HALO, rows]
@@ -518,11 +595,16 @@
     xq, halo_e, halo_o, join, conv = take(5)
     feat, feat_e, feat_o = take(3)
     choices = take(len(PARTS) + (0 if last else len(SENT)))
-    before, back, out_a, out_b = take(4)
-    if not last:
-        x_next, fout, msg_e, msg_o = take(4)
+    before, out_a, out_b = take(3)
+    backs = take(steps - 1 if last else 0)
+    held_back = take(step if step == steps - 2 else 0)
+    if last:
+        (x_inner,) = take(1)
+    else:
+        next_edges, fout, msg_e, msg_o = take(4)
     own_out, part_out, out_f, out_g = take(4)
-    tmp, act_a, act_b, held, xext, sems, aligned, recv = take(8)
+    take(len(held_back))
+    tmp, act_a, act_b, held, sems, aligned, recv = take(7)
     if last:
         (fout,) = take(1)
     else:
@@ -536,17 +618,26 @@
     right_side = place.side
     own = place.core if last else place.strip
 
-    copies = result_copies(strip, step - 1, steps, before, back, out_f, out_g, sems)
+    copies = own_copies(strip, step - 1, steps, before, out_f, out_g, sems.at[0])
+    for n, back in enumerate(backs):
+        copies += back_copies(strip, n, steps, back, out_f, out_g, sems.at[1 + n])
     for n, copy in copies:
         pl.when(core == n)(copy.start)
-    halo_at = half if step == 1 else 3 * half
-    above = pl.ds(pl.multiple_of((1 - par) * (quad_rows + HALO) * ch, half), half)
-    below = pl.ds(pl.multiple_of(par * (quad_rows + HALO) * ch, half), half)
-    xext[above, :] = halo_e[pl.ds(halo_at, half), :]
-    xext[below, :] = halo_o[pl.ds(halo_at, half), :]
-    xext[pl.ds(half, quad_rows * ch), :] = xq[...]
-    recv[1 - par] = feat_e[pl.ds(0, 3 * half), :]
-    recv[par] = feat_o[pl.ds(0, 3 * half), :]
+    halo_at = 5 * half // 2
+    if step == 1:
+        over, under = above_below(place, halo_e[pl.ds(half, half), :], halo_o[pl.ds(half, half), :])
+    else:
+        one, two = halo_e[pl.ds(halo_at, half), :].astype(F32), halo_o[pl.ds(halo_at, half), :].astype(F32)
+        over = jnp.where(par == 1, one, two).astype(BF)
+        under = jnp.where(par == 1, two, one).astype(BF)
+    if last:
+        inner = x_inner[...].astype(F32)
+        over, under = (
+            jnp.where(right_side == 0, over.astype(F32), inner).astype(BF),
+            jnp.where(right_side == 0, inner, under.astype(F32)).astype(BF),
+        )
+    unpack_message(ch, feat_e, recv, 1 - par)
+    unpack_message(ch, feat_o, recv, par)
     if last:
 
         @pl.when(right_side == 0)
@@ -565,26 +656,20 @@
     else:
         for n, rows_part in enumerate(PARTS):
             align(ch, feat, recv, aligned, HALO, rows_part, choices[n])
-        sent[0, pl.ds(3 * half, half), :] = x_next[pl.ds(0, half), :]
-        sent[1, pl.ds(3 * half, half), :] = x_next[pl.ds((quad_rows - HALO) * ch, half), :]
+        for n in range(2):
+            sent[n, pl.ds(halo_at, half), :] = next_edges[n]
 
     top_ok = jnp.logical_not(place.top)
     bottom_ok = jnp.logical_not(place.bottom)
     if last:
         top_ok = top_ok | (right_side == 1)
         bottom_ok = bottom_ok | (right_side == 0)
-    start_row = right_side * (2 * BS) if last else 0
     space = Rows(ch, width, top_ok, bottom_ok, rows)
-    for buf in (act_a, act_b):
-        for row in (-HALO - 1, rows + HALO):
-            for n in range(3):
-                buf[n, here_of(row, ch), :] = space.zero
-
+    clear_outside(space, ch, rows, (act_a, act_b))
     join_mat = join[...]
     for g in range((rows + 2 * HALO) // 4):
         first = g * 4 - HALO
-        at = (start_row + g * 4) * ch
-        inp = xext[pl.ds(pl.multiple_of(at, 4 * ch) if last else at, 4 * ch), :]
+        inp = over if first < 0 else under if first >= rows else xq[pl.ds(first * ch, 4 * ch), :]
         al = aligned[pl.ds(g * 4 * ch, 4 * ch), :]
         sides = []
         for h in range(2):
@@ -598,25 +683,7 @@
                 held[here_of(row, ch), :] = value
                 space.put(act_a, here_of(row, ch), value, row)
 
-    layers = conv.shape[0]
-    source, target = act_a, act_b
-    for layer in range(layers):
-        need = layers - 1 - layer
-        reach = -(-need // 2) * 2
-        start, stop = -reach, rows + reach
-        if (stop - start) % 4:
-            start, stop = -HALO, rows + HALO
-
-        def emit(row, value, layer=layer, target=target):
-            if layer < layers - 1:
-                held[here_of(row, ch), :] = value
-                space.put(target, here_of(row, ch), value, row)
-            else:
-                fout[pl.ds(row * ch, ch), :] = value
-
-        conv_layer(ch, conv[layer], source, held, start, stop, emit)
-        source, target = target, source
-
+    conv_layers(ch, conv, space, rows, act_a, act_b, held, fout)
     if not last:
         pack_messages(ch, fout, par, sent, choices[-len(SENT) :], msg_e, msg_o)
     channels_first(fout, pl.multiple_of(own * strip, strip), own_out, tmp, ch)
@@ -625,20 +692,24 @@
         pl.when(core == n)(copy.wait)
 
 
-def result_copies(strip, step, steps, own, back, out_f, out_g, sems):
-    copies = []
-    for n in range(2):
-        forth, other = (out_f, out_g) if n == 0 else (out_g, out_f)
-        at = step if n == 0 else steps - 1 - step
-        other_at = steps - 1 - at
-        copies.append((n, pltpu.make_async_copy(own, forth.at[pl.ds(at * strip, strip)], sems.at[0])))
-        copies.append((n, pltpu.make_async_copy(back, other.at[pl.ds(other_at * strip, strip)], sems.at[1])))
-    return copies
+def own_copies(strip, step, steps, own, out_f, out_g, sem):
+    return [
+        (0, pltpu.make_async_copy(own, out_f.at[pl.ds(step * strip, strip)], sem)),
+        (1, pltpu.make_async_copy(own, out_g.at[pl.ds((steps - 1 - step) * strip, strip)], sem)),
+    ]
+
+
+def back_copies(strip, step, steps, back, out_f, out_g, sem):
+    return [
+        (0, pltpu.make_async_copy(back, out_g.at[pl.ds((steps - 1 - step) * strip, strip)], sem)),
+        (1, pltpu.make_async_copy(back, out_f.at[pl.ds(step * strip, strip)], sem)),
+    ]
 
 
 def finish_kernel(strip, steps, own, back, out_a, out_b, out_f, out_g, sems):
     core = Place().core
-    copies = result_copies(strip, steps - 1, steps, own, back, out_f, out_g, sems)
+    copies = own_copies(strip, steps - 1, steps, own, out_f, out_g, sems.at[0])
+    copies += back_copies(strip, steps - 1, steps, back, out_f, out_g, sems.at[1])
     for n, copy in copies:
         pl.when(core == n)(copy.start)
     for n, copy in copies:
@@ -688,7 +759,20 @@
     )(*args)
 
 
-def pairings(count):
+def sooner(value):
+    return pl.pallas_call(
+        lambda given, out: None,
+        out_shape=jax.ShapeDtypeStruct(value.shape, value.dtype),
+        in_specs=[ANY],
+        out_specs=ANY,
+        input_output_aliases={0: 0},
+        compiler_params=pltpu.CompilerParams(vmem_limit_bytes=1 << 20),
+        cost_estimate=pl.CostEstimate(flops=0, bytes_accessed=2 << 20, transcendentals=0),
+        name="sooner",
+    )(value)
+
+
+def pairings(count, idle):
     groups = count // QUAD
     out = []
     for parity in range(2):
@@ -696,9 +780,23 @@
         for i in range(count):
             g = i // QUAD
             other = g + 1 if g % 2 == parity else g - 1
-            pairs.append((i, i % QUAD + other * QUAD if 0 <= other < groups else i ^ 1))
+            pairs.append((i, i % QUAD + other * QUAD if 0 <= other < groups else i ^ idle))
         out.append(pairs)
     return out
+
+
+def edge_pairings(count):
+    groups = count // QUAD
+    along, cross = [], []
+    for i in range(count):
+        g, side, core = i // QUAD, i % QUAD // 2, i % 2
+        if side == 0:
+            along += [(i, i - QUAD)] if g > 0 else []
+            cross.append((i, i - QUAD + 2 if g > 0 else i ^ 1))
+        else:
+            along += [(i, i + QUAD)] if g < groups - 1 else []
+            cross.append((i, i + QUAD - 2 if g < groups - 1 else i ^ 1))
+    return along, cross
 
 
 def on_device(frames, motion_forward, motion_backward, join_weight, conv_weight):
@@ -707,7 +805,8 @@
     half = HALO * ch
     crow = 16
     count = lax.axis_size("tiles")
-    even, odd = pairings(count)
+    even, odd = pairings(count, 1)
+    along_pairs, cross_pairs = edge_pairings(count)
 
     def near(k):
         return [(i, i ^ k) for i in range(count)]
@@ -718,7 +817,7 @@
     tmp = pltpu.VMEM((strip, width), F32)
     piece = (strip, width)
     rows = QUAD * BS
-    messages = [(3 * half, width)] + [(4 * half, width)] * (steps - 2)
+    messages = [(5 * half // 2, width)] + [(7 * half // 2, width)] * (steps - 2)
     feature = (rows * ch, width)
     whole = (steps * strip, width)
     flat = frames.reshape(steps, strip, width)
@@ -737,27 +836,28 @@
         in_hbm=(0, 1, 2),
         out_any=(2,),
     )
-    pair, rest = call(
+    pair, edge, rest = call(
         functools.partial(pair_first_kernel, ch, crow),
         "pair_first",
         (mine, send(other, near(1)), rest),
-        [(2 * (strip + crow) + half, width), later],
+        [(2 * (strip + crow), width), (2 * (half + crow), width), later],
+        [tmp],
         in_any=(2,),
-        out_any=(1,),
-        aliases={2: 1},
+        out_any=(2,),
+        aliases={2: 2},
     )
     received = send(pair, near(2))
+    along, cross = sooner(send(edge, along_pairs)), send(edge, cross_pairs)
     swapped = send(rest, near(1))
-    soon = min(2, steps - 1)
-    pair_near, pair_far = call(
-        functools.partial(pair_kernel, soon),
+    far_pairs = 2 * (steps - 3) * strip
+    pair_near, pair_far, pair_last = call(
+        functools.partial(pair_kernel, ch),
         "pair_rest",
         (flat, swapped),
-        [(2 * soon * strip, width), (2 * (steps - 1 - soon) * strip, width)],
-        [pltpu.SemaphoreType.DMA((2 * (steps - 1),))],
+        [(2 * strip + half, width), (far_pairs + (steps - 2) * half, width), (2 * strip, width)],
+        [tmp, pltpu.SemaphoreType.DMA((2 * steps,))],
         in_hbm=(0,),
         in_any=(1,),
-        out_any=(0, 1),
     )
     layers = conv_weight.shape[1]
     conv, join_both, join_first = call(
@@ -767,35 +867,36 @@
         [(layers, 2 * ch, 12 * ch), (2 * ch, 4 * ch), (2 * ch, 2 * ch)],
         free=True,
     )
-    xq, codes, edge_e, edge_o, pair_near = call(
+    xq, codes, pair_near = call(
         functools.partial(gather_first_kernel, ch, crow),
         "gather_first",
-        (pair, received, pair_near),
-        [feature, (QUAD * crow, width)] + [(2 * half + QUAD * crow, width)] * 2 + [pair_near.shape],
-        [tmp, pltpu.VMEM((2, half, width), BF)],
-        in_any=(2,),
-        out_any=(4,),
-        aliases={2: 4},
+        (pair, received, pair_near, conv),
+        [feature, (QUAD * crow, width), pair_near.shape],
+        [tmp],
+        in_any=(2, 3),
+        free=True,
+        out_any=(2,),
+        aliases={2: 2},
     )
-    halo_e, halo_o = code_e, code_o = send(edge_e, even), send(edge_o, odd)
+    halo_e, halo_o = along, cross
 
     wide_act = pltpu.VMEM((3, (rows + 16) * ch, width), BF)
     flops = 2 * (rows + 2 * HALO) * width * ch * ch * 9 * layers
     part_shapes, sent_shapes = choice_shapes(width)
     acts = [wide_act, wide_act, pltpu.VMEM(((rows + 16) * ch, width), BF)]
+    received_near = send(pair_near, near(2))
     inner, saved, saved_held = call(
         functools.partial(inner_kernel, ch),
         "refine_inner",
         (xq, join_first, conv),
         [feature, (layers, 2, 3, 2 * ch, width), (layers, 2, ch, width)],
         acts,
-        flops,
+        free=True,
     )
-    received_near = send(pair_near, near(2))
     feat, msg_e, msg_o, own, part, pair_far = call(
         functools.partial(outer_kernel, ch, steps),
         "refine_outer",
-        (inner, saved, saved_held, halo_e, halo_o, join_first, conv, codes, pair_far),
+        (inner, saved, saved_held, along, cross, join_first, conv, codes, pair_far),
         [feature, messages[0], messages[0], piece, piece, pair_far.shape],
         [tmp, pltpu.VMEM((2, *messages[0]), BF)] + [pltpu.VMEM(shape, BF) for shape in sent_shapes],
         flops // 4,
@@ -803,8 +904,8 @@
         out_any=(5,),
         aliases={8: 5},
     )
-    feat_e, feat_o = send(msg_e, even), send(msg_o, odd)
-    back = send(part, near(1))
+    feat_e, feat_o = sooner(send(msg_e, even)), send(msg_o, odd)
+    parts = [part]
     received_far = send(pair_far, near(2))
     outputs = call(lambda after, a, b: None, "results", (part,), [whole, whole], in_any=(0,), out_any=(0, 1), free=True)
 
@@ -812,53 +913,67 @@
         return call(
             functools.partial(choices_kernel, ch, step, steps),
             "choices",
-            (codes, code_e, code_o, msg_e),
+            (codes, along, cross, msg_e),
             part_shapes + (sent_shapes if step + 1 < steps else []),
             in_any=(3,),
         )
 
     def frame_of(step):
-        near_one = step <= soon
-        source = (pair_near, received_near) if near_one else (pair_far, received_far)
-        return call(
-            functools.partial(gather_kernel, ch, step - 1 if near_one else step - 1 - soon),
-            "gather",
-            (*source, msg_e),
-            [feature],
-            [tmp],
-            in_any=(2,),
-        )[0]
-
-    x_now = frame_of(1)
+        if step == steps - 1:
+            kernel = functools.partial(gather_last_kernel, ch, far_pairs + (steps - 3) * half)
+            args, outs = (pair_last, received_far, msg_e), [(2 * strip, width), (half, width)]
+        elif step == 1:
+            kernel = functools.partial(gather_kernel, ch, 0, 2 * strip)
+            args, outs = (pair_near, received_near, msg_e), [feature, (2, half, width)]
+        else:
+            kernel = functools.partial(gather_kernel, ch, 2 * (step - 2) * strip, far_pairs + (step - 2) * half)
+            args, outs = (pair_far, received_far, msg_e), [feature, (2, half, width)]
+        return call(kernel, "gather", args, outs, [tmp], in_any=(2,))
+
     for step in range(1, steps):
         last = step == steps - 1
         choices = choices_of(step)
-        args = [x_now, halo_e, halo_o, join_both, conv, feat, feat_e, feat_o, *choices, own, back, *outputs]
+        x_now, beside = frame_of(step)
+        args = [x_now, halo_e, halo_o, join_both, conv, feat, feat_e, feat_o, *choices, own, *outputs]
         many = len(args)
         outs = [] if last else [feature, messages[step], messages[step]]
         outs += [piece, piece, whole, whole]
-        scratch = [tmp, *acts, pltpu.VMEM(((rows + 2 * HALO) * ch, width), BF), pltpu.SemaphoreType.DMA((2,))]
+        in_any = [many - 3, many - 2, many - 1]
+        out_any = [len(outs) - 2, len(outs) - 1]
+        aliases = {many - 2: len(outs) - 2, many - 1: len(outs) - 1}
+        if last:
+            backs = [send(part, near(1)) for part in parts]
+            in_any += range(many, many + len(backs))
+            args += backs
+        elif step == steps - 2:
+            for n, part in enumerate(parts):
+                aliases[len(args)] = len(outs)
+                in_any.append(len(args))
+                out_any.append(len(outs))
+                args.append(part)
+                outs.append(piece)
+        args += [beside]
+        scratch = [tmp, *acts, pltpu.SemaphoreType.DMA((steps,))]
         scratch += [pltpu.VMEM(((rows + 2 * HALO) * ch, width), BF), pltpu.VMEM((2, 3 * half, width), BF)]
         scratch += [pltpu.VMEM((2 * strip, width) if last else (2, *messages[step]), BF)]
-        if not last:
-            x_now = frame_of(step + 1)
-            args += [x_now]
-        *results, own, part, out_f, out_g = call(
+        results = call(
             functools.partial(step_kernel, ch, step, steps),
             "refine",
             args,
             outs,
             scratch,
             flops,
-            in_any=(many - 4, many - 3, many - 2, many - 1),
-            out_any=(len(outs) - 2, len(outs) - 1),
-            aliases={many - 2: len(outs) - 2, many - 1: len(outs) - 1},
+            in_any=in_any,
+            out_any=out_any,
+            aliases=aliases,
         )
+        if not last:
+            feat, msg_e, msg_o, *results = results
+            halo_e, halo_o = feat_e, feat_o = sooner(send(msg_e, even)), send(msg_o, odd)
+        own, part, out_f, out_g, *held_back = results
         outputs = out_f, out_g
-        if not last:
-            feat, msg_e, msg_o = results
-            halo_e, halo_o = feat_e, feat_o = send(msg_e, even), send(msg_o, odd)
-        back = send(part, near(1))
+        parts = (held_back or parts) + [part]
+    back = send(part, near(1))
 
     outputs = call(
         functools.partial(finish_kernel, strip, steps),

time: 57.8 us -> 52.9 us (0.915)
  waiting for transfers between devices: 18.9 us -> 14.2 us
  starting transfers between devices: 15.9 us -> 14.9 us
  Pallas kernels: 21.9 us -> 22.7 us
    ppermute x17, waiting for transfers between devices: 18.9 us -> 14.2 us  [send(): return lax.ppermute(value, 'tiles', pairs)]
    ppermute x17, starting transfers between devices: 15.9 us -> 14.9 us  [send(): return lax.ppermute(value, 'tiles', pairs)]
    pallas_call x18, Pallas kernels: 21.9 us -> 22.7 us  [call(): pl.pallas_call(kernel, out_shape=[jax.ShapeDtypeStruct(o, BF) for o in ou...]
  transfers between devices with their start and end apart: 17 -> 17, of which waited for: 9 -> 7; matrix products, arithmetic and copies ran while one was open for 0% -> 0% of each run, Pallas kernels for 22% -> 25%
where the time goes in v2:
time: 52.9 us; the launch traced here: 52.7 us
  Pallas kernels  22.7 us (43%)
  starting transfers between devices  14.9 us (28%)
  waiting for transfers between devices  14.2 us (27%)
  between operations  0.96 us (2%)
    pallas_call x18, Pallas kernels, call(): pl.pallas_call(kernel, out_shape=[jax.ShapeDtypeStruct(o, BF) for o in ou...  22.7 us
    ppermute x17, starting transfers between devices, send(): return lax.ppermute(value, 'tiles', pairs)  14.9 us
    ppermute x17, waiting for transfers between devices, send(): return lax.ppermute(value, 'tiles', pairs)  14.2 us
  transfers between devices with their start and end apart: 17, of which 7 were waited for; matrix products, arithmetic and copies ran while one was open for 0% of the time, Pallas kernels for 25%

profile of v2, /device:TPU:0, one launch (start us, length us, event | category | flops | bytes accessed | tf_op | source)
XLA Modules:
  0.0 52.7 jit_solution(14800774550480074616)
XLA Ops:
  0.7 1.4 %pack_first.1 = (bf16[784,128]{1,0:T(8,128)(2,1)S(1)}, bf16[784,128]{1,0:T(8,128)(2,1)S(1)}, bf16[1536,128]{1,0:T(8,128)(2,1)S(1)}) custom-call(bf16[4,512,128]{2,1,0:T(8,128)(2,1)} %bitcast.5, s32[3,16]{1,0:T(4,128)} %motion_f.1, s32[3,16]{1,0:T(4,128)} %motion_b.1), custom_call_target="tpu_custom_call" | custom-call | bytes 524672 | tf_op jit(solution)/shard_map/pack_first/pallas_call | solution.py:745
  2.6 1.1 %collective-permute-done.swapped = bf16[784,128]{1,0:T(8,128)(2,1)S(1)} collective-permute-done((bf16[784,128]{1,0:T(8,128)(2,1)S(1)}, bf16[784,128]{1,0:T(8,128)(2,1)S(1)}, u32[]{:S(2)}, u32[]{:S(2)}) %collective-permute-start) | collective-permute-done | bytes 200736 | tf_op jit(solution)/shard_map/ppermute | solution.py:815
  4.2 2.6 %collective-permute-start.2 = (bf16[1056,128]{1,0:T(8,128)(2,1)S(1)}, bf16[1056,128]{1,0:T(8,128)(2,1)S(1)}, u32[]{:S(2)}, u32[]{:S(2)}) collective-permute-start(bf16[1056,128]{1,0:T(8,128)(2,1)S(1)} %get-tuple-element.87.pair), channel_id=1, source_target_pairs={{0,2},{1,3},{2,0},{3,1},{4,6},{5,7},{6,4},{7,5},{8,10},{9,11},{10,... | collective-permute-start | bytes 811016 | tf_op jit(solution)/shard_map/ppermute | solution.py:815
  6.8 1.3 %collective-permute-start.3 = (bf16[544,128]{1,0:T(8,128)(2,1)S(1)}, bf16[544,128]{1,0:T(8,128)(2,1)S(1)}, u32[]{:S(2)}, u32[]{:S(2)}) collective-permute-start(bf16[544,128]{1,0:T(8,128)(2,1)S(1)} %get-tuple-element.95), channel_id=1, source_target_pairs={{2,6},{3,7},{4,0},{5,1},{6,10},{7,11},{8,4},{9,5},{10,14},{11,15},... | collective-permute-start | bytes 417800 | tf_op jit(solution)/shard_map/ppermute | solution.py:815
  8.5 1.5 %pair_rest.1 = (bf16[1280,128]{1,0:T(8,128)(2,1)S(1)}, bf16[1536,128]{1,0:T(8,128)(2,1)S(1)}, bf16[1024,128]{1,0:T(8,128)(2,1)S(1)}) custom-call(bf16[4,512,128]{2,1,0:T(8,128)(2,1)} %bitcast.6, bf16[1536,128]{1,0:T(8,128)(2,1)S(1)} %collective-permute-done.1.swapped), custom_call_target="tpu_custom_call" | custom-call | bytes 917504 | tf_op jit(solution)/shard_map/pair_rest/pallas_call | solution.py:745
  10.1 3.8 %collective-permute-done.2.received = bf16[1056,128]{1,0:T(8,128)(2,1)S(1)} collective-permute-done((bf16[1056,128]{1,0:T(8,128)(2,1)S(1)}, bf16[1056,128]{1,0:T(8,128)(2,1)S(1)}, u32[]{:S(2)}, u32[]{:S(2)}) %collective-permute-start.2) | collective-permute-done | bytes 270368 | tf_op jit(solution)/shard_map/ppermute | solution.py:815
  14.1 2.4 %collective-permute-start.6 = (bf16[1280,128]{1,0:T(8,128)(2,1)S(1)}, bf16[1280,128]{1,0:T(8,128)(2,1)S(1)}, u32[]{:S(2)}, u32[]{:S(2)}) collective-permute-start(bf16[1280,128]{1,0:T(8,128)(2,1)S(1)} %get-tuple-element.99.pair), channel_id=1, source_target_pairs={{0,2},{1,3},{2,0},{3,1},{4,6},{5,7},{6,4},{7,5},{8,10},{9,11},{10,... | collective-permute-start | bytes 983048 | tf_op jit(solution)/shard_map/ppermute | solution.py:815
  16.5 2.4 %refine_inner.1 = (bf16[2048,128]{1,0:T(8,128)(2,1)S(1)}, bf16[4,2,3,128,128]{4,3,2,1,0:T(8,128)(2,1)S(1)}, bf16[4,2,64,128]{3,2,1,0:T(8,128)(2,1)S(1)}) custom-call(bf16[2048,128]{1,0:T(8,128)(2,1)S(1)} %get-tuple-element.90.xq, bf16[128,128]{1,0:T(8,128)(2,1)S(1)} %get-tuple-element.91.join.refs_5_, ...), custom_call_target="tpu_custom_call" | custom-call | tf_op jit(solution)/shard_map/refine_inner/pallas_call | solution.py:745
  18.9 2.3 %refine_outer.1 = (bf16[2048,128]{1,0:T(8,128)(2,1)S(1)}, bf16[640,128]{1,0:T(8,128)(2,1)S(1)}, bf16[640,128]{1,0:T(8,128)(2,1)S(1)}, bf16[512,128]{1,0:T(8,128)...) custom-call(bf16[2048,128]{1,0:T(8,128)(2,1)S(1)} %get-tuple-element.92.re, ...), custom_call_target="tpu_custom_call", output_to_operand_aliasing={{5}: (8, {})} | custom-call | flops 377487360 | bytes 2949120 | tf_op jit(solution)/shard_map/refine_outer/pallas_call | solution.py:745
  21.2 1.6 %collective-permute-start.7 = (bf16[640,128]{1,0:T(8,128)(2,1)S(1)}, bf16[640,128]{1,0:T(8,128)(2,1)S(1)}, u32[]{:S(2)}, u32[]{:S(2)}) collective-permute-start(bf16[640,128]{1,0:T(8,128)(2,1)S(1)} %get-tuple-element.100.after), channel_id=1, source_target_pairs={{0,4},{1,5},{2,6},{3,7},{4,0},{5,1},{6,2},{7,3},{8,12},{9,13},{10,... | collective-permute-start | bytes 491528 | tf_op jit(solution)/shard_map/ppermute | solution.py:815
  22.8 0.6 %collective-permute-start.5 = (bf16[1536,128]{1,0:T(8,128)(2,1)S(1)}, bf16[1536,128]{1,0:T(8,128)(2,1)S(1)}, u32[]{:S(2)}, u32[]{:S(2)}) collective-permute-start(bf16[1536,128]{1,0:T(8,128)(2,1)S(1)} %get-tuple-element.98.pair), channel_id=1, source_target_pairs={{0,2},{1,3},{2,0},{3,1},{4,6},{5,7},{6,4},{7,5},{8,10},{9,11},{10,... | collective-permute-start | bytes 1179656 | tf_op jit(solution)/shard_map/ppermute | solution.py:815
  23.4 0.8 %choices.3 = (bf16[512,128]{1,0:T(8,128)(2,1)S(1)}, bf16[768,256]{1,0:T(8,128)(2,1)S(1)}, bf16[768,256]{1,0:T(8,128)(2,1)S(1)}, bf16[768,256]{1,0:T(8,128)(2,1)S...) custom-call(bf16[64,128]{1,0:T(8,128)(2,1)S(1)} %get-tuple-element.9, ...), custom_call_target="tpu_custom_call" | custom-call | bytes 458752 | tf_op jit(solution)/shard_map/choices/pallas_call | solution.py:745
  24.1 2.4 %collective-permute-done.7.given = bf16[640,128]{1,0:T(8,128)(2,1)S(1)} collective-permute-done((bf16[640,128]{1,0:T(8,128)(2,1)S(1)}, bf16[640,128]{1,0:T(8,128)(2,1)S(1)}, u32[]{:S(2)}, u32[]{:S(2)}) %collective-permute-start.7) | collective-permute-done | bytes 163872 | tf_op jit(solution)/shard_map/ppermute | solution.py:815
  26.8 4.1 %refine.3 = (bf16[2048,128]{1,0:T(8,128)(2,1)S(1)}, bf16[896,128]{1,0:T(8,128)(2,1)S(1)}, bf16[896,128]{1,0:T(8,128)(2,1)S(1)}, bf16[512,128]{1,0:T(8,128)(2,1)S...) custom-call(bf16[2048,128]{1,0:T(8,128)(2,1)S(1)} %get-tuple-element, ...), custom_call_target="tpu_custom_call", output_to_operand_aliasing={{5}: (19, {}), {6}: (20, {})} | custom-call | flops 1509949440 | bytes 5980160 | tf_op jit(solution)/shard_map/refine/pallas_call | solution.py:745
  30.9 1.9 %collective-permute-start.9 = (bf16[896,128]{1,0:T(8,128)(2,1)S(1)}, bf16[896,128]{1,0:T(8,128)(2,1)S(1)}, u32[]{:S(2)}, u32[]{:S(2)}) collective-permute-start(bf16[896,128]{1,0:T(8,128)(2,1)S(1)} %get-tuple-element.120.after), channel_id=1, source_target_pairs={{0,4},{1,5},{2,6},{3,7},{4,0},{5,1},{6,2},{7,3},{8,12},{9,13},{10,... | collective-permute-start | bytes 688136 | tf_op jit(solution)/shard_map/ppermute | solution.py:815
  32.9 0.8 %choices.4 = (bf16[512,128]{1,0:T(8,128)(2,1)S(1)}, bf16[768,256]{1,0:T(8,128)(2,1)S(1)}, bf16[768,256]{1,0:T(8,128)(2,1)S(1)}, bf16[768,256]{1,0:T(8,128)(2,1)S...) custom-call(bf16[64,128]{1,0:T(8,128)(2,1)S(1)} %get-tuple-element.9, ...), custom_call_target="tpu_custom_call" | custom-call | bytes 524288 | tf_op jit(solution)/shard_map/choices/pallas_call | solution.py:745
  33.7 0.7 %collective-permute-done.5.received = bf16[1536,128]{1,0:T(8,128)(2,1)S(1)} collective-permute-done((bf16[1536,128]{1,0:T(8,128)(2,1)S(1)}, bf16[1536,128]{1,0:T(8,128)(2,1)S(1)}, u32[]{:S(2)}, u32[]{:S(2)}) %collective-permute-start.5) | collective-permute-done | bytes 393248 | tf_op jit(solution)/shard_map/ppermute | solution.py:815
  34.6 2.5 %collective-permute-done.9.given = bf16[896,128]{1,0:T(8,128)(2,1)S(1)} collective-permute-done((bf16[896,128]{1,0:T(8,128)(2,1)S(1)}, bf16[896,128]{1,0:T(8,128)(2,1)S(1)}, u32[]{:S(2)}, u32[]{:S(2)}) %collective-permute-start.9) | collective-permute-done | bytes 229408 | tf_op jit(solution)/shard_map/ppermute | solution.py:815
  37.0 4.3 %refine.4 = (bf16[2048,128]{1,0:T(8,128)(2,1)S(1)}, bf16[896,128]{1,0:T(8,128)(2,1)S(1)}, bf16[896,128]{1,0:T(8,128)(2,1)S(1)}, bf16[512,128]{1,0:T(8,128)(2,1)S...) custom-call(bf16[2048,128]{1,0:T(8,128)(2,1)S(1)} %get-tuple-element, ...), custom_call_target="tpu_custom_call", output_to_operand_aliasing={{5}: (19, {}), {6}: (20, {}), {7}: (21, {}), {8}: (22, {})} | custom-call | flops 1509949440 | bytes 6553600 | tf_op jit(solution)/shard_map/refine/pallas_call | solution.py:745
  41.4 2.2 %collective-permute-start.11 = (bf16[896,128]{1,0:T(8,128)(2,1)S(1)}, bf16[896,128]{1,0:T(8,128)(2,1)S(1)}, u32[]{:S(2)}, u32[]{:S(2)}) collective-permute-start(bf16[896,128]{1,0:T(8,128)(2,1)S(1)} %get-tuple-element.139.after), channel_id=1, source_target_pairs={{0,4},{1,5},{2,6},{3,7},{4,0},{5,1},{6,2},{7,3},{8,12},{9,13},{10,... | collective-permute-start | bytes 688136 | tf_op jit(solution)/shard_map/ppermute | solution.py:815
  45.1 2.5 %collective-permute-done.11.given = bf16[896,128]{1,0:T(8,128)(2,1)S(1)} collective-permute-done((bf16[896,128]{1,0:T(8,128)(2,1)S(1)}, bf16[896,128]{1,0:T(8,128)(2,1)S(1)}, u32[]{:S(2)}, u32[]{:S(2)}) %collective-permute-start.11) | collective-permute-done | bytes 229408 | tf_op jit(solution)/shard_map/ppermute | solution.py:815
  47.6 2.8 %refine.5 = (bf16[512,128]{1,0:T(8,128)(2,1)S(1)}, bf16[512,128]{1,0:T(8,128)(2,1)S(1)}, bf16[2048,128]{1,0:T(8,128)(2,1)}, bf16[2048,128]{1,0:T(8,128)(2,1)}) custom-call(bf16[1024,128]{1,0:T(8,128)(2,1)S(1)} %get-tuple-element.140.refs_0_, bf16[896,128]{1,0:T(8,128)(2,1)S(1)} %sooner.7.refs_1_.refs_6_, ...), custom_call_target="tpu_custom_call", output_to_operand_aliasing={{2}: (15, {}), {3}: (16, {})} | custom-call | flops 1509949440 | bytes 6029312 | tf_op jit(solution)/shard_map/refine/pallas_call | solution.py:745
  50.5 1.3 %collective-permute-done.16.back = bf16[512,128]{1,0:T(8,128)(2,1)S(1)} collective-permute-done((bf16[512,128]{1,0:T(8,128)(2,1)S(1)}, bf16[512,128]{1,0:T(8,128)(2,1)S(1)}, u32[]{:S(2)}, u32[]{:S(2)}) %collective-permute-start.16) | collective-permute-done | bytes 131104 | tf_op jit(solution)/shard_map/ppermute | solution.py:815
  51.9 0.7 %finish.1 = (bf16[2048,128]{1,0:T(8,128)(2,1)}, bf16[2048,128]{1,0:T(8,128)(2,1)}) custom-call(bf16[512,128]{1,0:T(8,128)(2,1)S(1)} %get-tuple-element.156.own, bf16[512,128]{1,0:T(8,128)(2,1)S(1)} %collective-permute-done.16.back, bf16[2048,128]{1,0:T(8,128)(2,1)} %get-tuple-element.158.out_a, ...), custom_call_target="tpu_custom_call", output_to_operand_aliasing={{0}: (2, {}), {1}: (3, {})} | custom-call | bytes 1310720 | tf_op jit(solution)/shard_map/finish/pallas_call | solution.py:745
  (36 shorter events, 3.7 us)
Async XLA Ops:
  0.6 7.6 %copy-start = (bf16[2,4,9,64,64]{4,3,2,1,0:T(8,128)(2,1)S(1)}, bf16[2,4,9,64,64]{4,3,2,1,0:T(8,128)(2,1)}, u32[]{:S(2)}) copy-start(bf16[2,4,9,64,64]{4,3,2,1,0:T(8,128)(2,1)} %conv.1) | copy-start | bytes 1769476
  0.6 7.6 %copy-start.1 = (bf16[2,64,128]{2,1,0:T(8,128)(2,1)S(1)}, bf16[2,64,128]{2,1,0:T(8,128)(2,1)}, u32[]{:S(2)}) copy-start(bf16[2,64,128]{2,1,0:T(8,128)(2,1)} %join.1) | copy-start | bytes 98308
  2.1 1.6 %collective-permute-start = (bf16[784,128]{1,0:T(8,128)(2,1)S(1)}, bf16[784,128]{1,0:T(8,128)(2,1)S(1)}, u32[]{:S(2)}, u32[]{:S(2)}) collective-permute-start(bf16[784,128]{1,0:T(8,128)(2,1)S(1)} %get-tuple-element.83), channel_id=1, source_target_pairs={{0,1},{1,0},{2,3},{3,2},{4,5},{5,4},{6,7},{7,6},{8,9},{9,8},{10,11... | collective-permute-start | bytes 602120 | tf_op jit(solution)/shard_map/ppermute | solution.py:815
  3.8 4.7 %collective-permute-start.1 = (bf16[1536,128]{1,0:T(8,128)(2,1)S(1)}, bf16[1536,128]{1,0:T(8,128)(2,1)S(1)}, u32[]{:S(2)}, u32[]{:S(2)}) collective-permute-start(bf16[1536,128]{1,0:T(8,128)(2,1)S(1)} %get-tuple-element.85), channel_id=1, source_target_pairs={{0,1},{1,0},{2,3},{3,2},{4,5},{5,4},{6,7},{7,6},{8,9},{9,8},{10,11... | collective-permute-start | bytes 1179656 | tf_op jit(solution)/shard_map/ppermute | solution.py:815
  4.2 9.6 %collective-permute-start.2 = (bf16[1056,128]{1,0:T(8,128)(2,1)S(1)}, bf16[1056,128]{1,0:T(8,128)(2,1)S(1)}, u32[]{:S(2)}, u32[]{:S(2)}) collective-permute-start(bf16[1056,128]{1,0:T(8,128)(2,1)S(1)} %get-tuple-element.87.pair), channel_id=1, source_target_pairs={{0,2},{1,3},{2,0},{3,1},{4,6},{5,7},{6,4},{7,5},{8,10},{9,11},{10,... | collective-permute-start | bytes 811016 | tf_op jit(solution)/shard_map/ppermute | solution.py:815
  6.8 9.7 %collective-permute-start.3 = (bf16[544,128]{1,0:T(8,128)(2,1)S(1)}, bf16[544,128]{1,0:T(8,128)(2,1)S(1)}, u32[]{:S(2)}, u32[]{:S(2)}) collective-permute-start(bf16[544,128]{1,0:T(8,128)(2,1)S(1)} %get-tuple-element.95), channel_id=1, source_target_pairs={{2,6},{3,7},{4,0},{5,1},{6,10},{7,11},{8,4},{9,5},{10,14},{11,15},... | collective-permute-start | bytes 417800 | tf_op jit(solution)/shard_map/ppermute | solution.py:815
  8.1 10.7 %collective-permute-start.4 = (bf16[544,128]{1,0:T(8,128)(2,1)S(1)}, bf16[544,128]{1,0:T(8,128)(2,1)S(1)}, u32[]{:S(2)}, u32[]{:S(2)}) collective-permute-start(bf16[544,128]{1,0:T(8,128)(2,1)S(1)} %get-tuple-element.95), channel_id=1, source_target_pairs={{0,1},{1,0},{2,4},{3,5},{4,2},{5,3},{6,8},{7,9},{8,6},{9,7},{10,12... | collective-permute-start | bytes 417800 | tf_op jit(solution)/shard_map/ppermute | solution.py:815
  14.1 12.5 %collective-permute-start.6 = (bf16[1280,128]{1,0:T(8,128)(2,1)S(1)}, bf16[1280,128]{1,0:T(8,128)(2,1)S(1)}, u32[]{:S(2)}, u32[]{:S(2)}) collective-permute-start(bf16[1280,128]{1,0:T(8,128)(2,1)S(1)} %get-tuple-element.99.pair), channel_id=1, source_target_pairs={{0,2},{1,3},{2,0},{3,1},{4,6},{5,7},{6,4},{7,5},{8,10},{9,11},{10,... | collective-permute-start | bytes 983048 | tf_op jit(solution)/shard_map/ppermute | solution.py:815
  21.2 5.4 %collective-permute-start.7 = (bf16[640,128]{1,0:T(8,128)(2,1)S(1)}, bf16[640,128]{1,0:T(8,128)(2,1)S(1)}, u32[]{:S(2)}, u32[]{:S(2)}) collective-permute-start(bf16[640,128]{1,0:T(8,128)(2,1)S(1)} %get-tuple-element.100.after), channel_id=1, source_target_pairs={{0,4},{1,5},{2,6},{3,7},{4,0},{5,1},{6,2},{7,3},{8,12},{9,13},{10,... | collective-permute-start | bytes 491528 | tf_op jit(solution)/shard_map/ppermute | solution.py:815
  22.8 4.0 %collective-permute-start.8 = (bf16[640,128]{1,0:T(8,128)(2,1)S(1)}, bf16[640,128]{1,0:T(8,128)(2,1)S(1)}, u32[]{:S(2)}, u32[]{:S(2)}) collective-permute-start(bf16[640,128]{1,0:T(8,128)(2,1)S(1)} %get-tuple-element.104), channel_id=1, source_target_pairs={{0,1},{1,0},{2,3},{3,2},{4,8},{5,9},{6,10},{7,11},{8,4},{9,5},{10,... | collective-permute-start | bytes 491528 | tf_op jit(solution)/shard_map/ppermute | solution.py:815
  22.8 11.5 %collective-permute-start.5 = (bf16[1536,128]{1,0:T(8,128)(2,1)S(1)}, bf16[1536,128]{1,0:T(8,128)(2,1)S(1)}, u32[]{:S(2)}, u32[]{:S(2)}) collective-permute-start(bf16[1536,128]{1,0:T(8,128)(2,1)S(1)} %get-tuple-element.98.pair), channel_id=1, source_target_pairs={{0,2},{1,3},{2,0},{3,1},{4,6},{5,7},{6,4},{7,5},{8,10},{9,11},{10,... | collective-permute-start | bytes 1179656 | tf_op jit(solution)/shard_map/ppermute | solution.py:815
  30.9 6.1 %collective-permute-start.9 = (bf16[896,128]{1,0:T(8,128)(2,1)S(1)}, bf16[896,128]{1,0:T(8,128)(2,1)S(1)}, u32[]{:S(2)}, u32[]{:S(2)}) collective-permute-start(bf16[896,128]{1,0:T(8,128)(2,1)S(1)} %get-tuple-element.120.after), channel_id=1, source_target_pairs={{0,4},{1,5},{2,6},{3,7},{4,0},{5,1},{6,2},{7,3},{8,12},{9,13},{10,... | collective-permute-start | bytes 688136 | tf_op jit(solution)/shard_map/ppermute | solution.py:815
  32.9 4.2 %collective-permute-start.10 = (bf16[896,128]{1,0:T(8,128)(2,1)S(1)}, bf16[896,128]{1,0:T(8,128)(2,1)S(1)}, u32[]{:S(2)}, u32[]{:S(2)}) collective-permute-start(bf16[896,128]{1,0:T(8,128)(2,1)S(1)} %get-tuple-element.122), channel_id=1, source_target_pairs={{0,1},{1,0},{2,3},{3,2},{4,8},{5,9},{6,10},{7,11},{8,4},{9,5},{10,... | collective-permute-start | bytes 688136 | tf_op jit(solution)/shard_map/ppermute | solution.py:815
  41.4 6.2 %collective-permute-start.11 = (bf16[896,128]{1,0:T(8,128)(2,1)S(1)}, bf16[896,128]{1,0:T(8,128)(2,1)S(1)}, u32[]{:S(2)}, u32[]{:S(2)}) collective-permute-start(bf16[896,128]{1,0:T(8,128)(2,1)S(1)} %get-tuple-element.139.after), channel_id=1, source_target_pairs={{0,4},{1,5},{2,6},{3,7},{4,0},{5,1},{6,2},{7,3},{8,12},{9,13},{10,... | collective-permute-start | bytes 688136 | tf_op jit(solution)/shard_map/ppermute | solution.py:815
  43.6 4.0 %collective-permute-start.12 = (bf16[896,128]{1,0:T(8,128)(2,1)S(1)}, bf16[896,128]{1,0:T(8,128)(2,1)S(1)}, u32[]{:S(2)}, u32[]{:S(2)}) collective-permute-start(bf16[896,128]{1,0:T(8,128)(2,1)S(1)} %get-tuple-element.141), channel_id=1, source_target_pairs={{0,1},{1,0},{2,3},{3,2},{4,8},{5,9},{6,10},{7,11},{8,4},{9,5},{10,... | collective-permute-start | bytes 688136 | tf_op jit(solution)/shard_map/ppermute | solution.py:815
  43.6 4.0 %collective-permute-start.13 = (bf16[512,128]{1,0:T(8,128)(2,1)S(1)}, bf16[512,128]{1,0:T(8,128)(2,1)S(1)}, u32[]{:S(2)}, u32[]{:S(2)}) collective-permute-start(bf16[512,128]{1,0:T(8,128)(2,1)S(1)} %get-tuple-element.152), channel_id=1, source_target_pairs={{0,1},{1,0},{2,3},{3,2},{4,5},{5,4},{6,7},{7,6},{8,9},{9,8},{10,11... | collective-permute-start | bytes 393224 | tf_op jit(solution)/shard_map/ppermute | solution.py:815
  44.1 3.5 %collective-permute-start.14 = (bf16[512,128]{1,0:T(8,128)(2,1)S(1)}, bf16[512,128]{1,0:T(8,128)(2,1)S(1)}, u32[]{:S(2)}, u32[]{:S(2)}) collective-permute-start(bf16[512,128]{1,0:T(8,128)(2,1)S(1)} %get-tuple-element.153), channel_id=1, source_target_pairs={{0,1},{1,0},{2,3},{3,2},{4,5},{5,4},{6,7},{7,6},{8,9},{9,8},{10,11... | collective-permute-start | bytes 393224 | tf_op jit(solution)/shard_map/ppermute | solution.py:815
  44.1 3.5 %collective-permute-start.15 = (bf16[512,128]{1,0:T(8,128)(2,1)S(1)}, bf16[512,128]{1,0:T(8,128)(2,1)S(1)}, u32[]{:S(2)}, u32[]{:S(2)}) collective-permute-start(bf16[512,128]{1,0:T(8,128)(2,1)S(1)} %get-tuple-element.154), channel_id=1, source_target_pairs={{0,1},{1,0},{2,3},{3,2},{4,5},{5,4},{6,7},{7,6},{8,9},{9,8},{10,11... | collective-permute-start | bytes 393224 | tf_op jit(solution)/shard_map/ppermute | solution.py:815
  50.4 1.4 %collective-permute-start.16 = (bf16[512,128]{1,0:T(8,128)(2,1)S(1)}, bf16[512,128]{1,0:T(8,128)(2,1)S(1)}, u32[]{:S(2)}, u32[]{:S(2)}) collective-permute-start(bf16[512,128]{1,0:T(8,128)(2,1)S(1)} %get-tuple-element.157), channel_id=1, source_target_pairs={{0,1},{1,0},{2,3},{3,2},{4,5},{5,4},{6,7},{7,6},{8,9},{9,8},{10,11... | collective-permute-start | bytes 393224 | tf_op jit(solution)/shard_map/ppermute | solution.py:815

commit v3 on v2

--- a/solution.py
+++ b/solution.py
@@ -47,7 +47,7 @@
     dst[...] = tmp[...].astype(BF)
 
 
-def pack_first_kernel(ch, crow, frames, motion_f, motion_b, mine, other, rest, following, motion_buf, tmp, sems):
+def pack_first_kernel(ch, crow, frames, motion_f, motion_b, mine, mine_edge, other, rest, following, motion_buf, tmp, sems):
     place = Place()
     steps, strip = frames.shape[:2]
     half = HALO * ch
@@ -92,32 +92,34 @@
         out[pl.ds(strip, crow), :] = code
     for copy in copies:
         copy.wait()
-    for n, out in enumerate(outs):
-        tmp[...] = following[n].astype(F32)
-        for r in range(HALO):
-            row = tmp[pl.ds(place.side * (BS - HALO) + r, ch, stride=BS), :]
-            out[pl.ds(strip + crow + r * ch, ch), :] = row.astype(BF)
+    for n, (out, start) in enumerate(((mine_edge, 0), (other, strip + crow))):
+        edge_of(place.side == 0, ch, following[n], out, start, tmp)
     for copy in later:
         copy.wait()
 
 
-def pair_first_kernel(ch, crow, mine, swapped, rest_in, out, edge, rest_out, tmp):
+def edge_of(top, ch, strip_values, out, start, tmp):
+    tmp[...] = strip_values.astype(F32)
+    for r in range(HALO):
+        one, two = tmp[pl.ds(r, ch, stride=BS), :], tmp[pl.ds(BS - HALO + r, ch, stride=BS), :]
+        out[pl.ds(start + r * ch, ch), :] = jnp.where(top, one, two).astype(BF)
+
+
+def pair_first_kernel(ch, crow, mine, mine_edge, partner, rest_in, out, edge, edge_too, rest_out, tmp):
     place = Place()
     strip = BS * ch
     half = HALO * ch
-    for n, piece in enumerate((mine, swapped)):
+    own = place.core == place.side
+    first = jnp.where(own, mine[pl.ds(0, strip), :].astype(F32), partner[pl.ds(0, strip), :].astype(F32))
+    edge_of(place.side == 0, ch, first, edge, 0, tmp)
+    second = partner[pl.ds(strip + crow, half), :].astype(F32)
+    edge[pl.ds(half, half), :] = jnp.where(own, mine_edge[...].astype(F32), second).astype(BF)
+    for n, piece in enumerate((mine, partner)):
         at = place.core ^ n
         out[pl.ds(pl.multiple_of(at * strip, strip), strip), :] = piece[pl.ds(0, strip), :]
         for ref, start in ((out, 2 * strip), (edge, 2 * half)):
             ref[pl.ds(pl.multiple_of(start + at * crow, crow), crow), :] = piece[pl.ds(strip, crow), :]
-
-        @pl.when(at == place.side)
-        def _(piece=piece):
-            tmp[...] = piece[pl.ds(0, strip), :].astype(F32)
-            for r in range(HALO):
-                row = tmp[pl.ds(place.side * (BS - HALO) + r, ch, stride=BS), :]
-                edge[pl.ds(r * ch, ch), :] = row.astype(BF)
-            edge[pl.ds(half, half), :] = piece[pl.ds(strip + crow, half), :]
+    edge_too[...] = edge[...]
 
 
 def above_below(place, along, cross):
@@ -150,16 +152,12 @@
     one, two = pair[pl.ds(0, strip), :].astype(F32), pair[pl.ds(strip, strip), :].astype(F32)
     left = place.side == 0
     if outer:
-        tmp[...] = jnp.where(left, one, two)
-        first = place.side * (BS - HALO)
+        edge_of(left, ch, jnp.where(left, one, two), out, start, tmp)
     else:
-        tmp[...] = jnp.where(left, two, one)
-        first = (1 - place.side) * (BS - HALO)
-    for r in range(HALO):
-        out[pl.ds(start + r * ch, ch), :] = tmp[pl.ds(first + r, ch, stride=BS), :].astype(BF)
-
-
-def pair_kernel(ch, frames, swapped, near_out, far_out, last_out, tmp, sems):
+        edge_of(jnp.logical_not(left), ch, jnp.where(left, two, one), out, start, tmp)
+
+
+def pair_kernel(ch, frames, swapped, edge_in, near_out, far_out, last_out, edge_out, tmp, sems):
     place = Place()
     steps, strip = frames.shape[:2]
     half = HALO * ch
@@ -182,7 +180,7 @@
     edge_rows(place, ch, last_out, False, far_out, at, tmp)
 
 
-def gather_first_kernel(ch, crow, pair, received, near_in, conv, xq, codes, near_out, tmp):
+def gather_first_kernel(ch, crow, pair, received, conv, near_in, xq, codes, near_out, tmp):
     place = Place()
     strip = BS * ch
     for n, piece in enumerate((pair, received)):
@@ -194,7 +192,7 @@
             codes[pl.ds(code_at, crow), :] = piece[pl.ds(2 * strip + m * crow, crow), :]
 
 
-def gather_kernel(ch, pair_at, edge_at, pair, received, after, xq, edges, tmp):
+def gather_kernel(ch, pair_at, edge_at, pair, received, feat, xq, edges, own_out, part_out, tmp):
     strip = BS * ch
     half = HALO * ch
     side = Place().side
@@ -203,13 +201,22 @@
             start = ((side + n) % 2 * 2 + m) * strip
             rows_first(piece, pair_at + m * strip, xq, pl.multiple_of(start, strip), tmp, ch)
         edges[side ^ n] = piece[pl.ds(edge_at, half), :]
-
-
-def gather_last_kernel(ch, inner_at, pair, received, after, xq, inner, tmp):
+    split_results(ch, feat, own_out, part_out, tmp)
+
+
+def split_results(ch, feat, own_out, part_out, tmp):
+    strip = BS * ch
+    own = Place().strip
+    channels_first(feat, pl.multiple_of(own * strip, strip), own_out, tmp, ch)
+    channels_first(feat, pl.multiple_of((own ^ 1) * strip, strip), part_out, tmp, ch)
+
+
+def gather_last_kernel(ch, inner_at, pair, received, feat, xq, inner, own_out, part_out, tmp):
     strip = BS * ch
     for m in range(2):
         rows_first(pair, m * strip, xq, m * strip, tmp, ch)
     inner[...] = received[pl.ds(inner_at, HALO * ch), :]
+    split_results(ch, feat, own_out, part_out, tmp)
 
 
 class Codes:
@@ -302,9 +309,12 @@
     return tiles
 
 
-def receive_choice(code, dests, bottom, out):
-    width = out.shape[0] // len(tiles_of(dests, bottom))
-    for n, tile in enumerate(tiles_of(dests, bottom)):
+def receive_choice(code, dests, bottom, near, far):
+    width = code.zero.shape[0]
+    tiles = tiles_of(dests, bottom)
+    own = sum(isinstance(tile, int) for tile in tiles)
+    for n, tile in enumerate(tiles):
+        out, at = (near, n) if n < own else (far, n - own)
         for m, dest in enumerate(dests):
             if isinstance(tile, int):
                 value = code.plain(dest, tile)
@@ -315,8 +325,8 @@
                 regions = list(enumerate((FROM_ABOVE, FROM_BELOW)[side][kind - 1]))
                 if kind == 1:
                     regions = regions[:3] if bottom == (side == 0) else regions[3:]
-                value = sum((code.packed(d, source, at) for at, (d, source) in regions if d == dest), code.zero)
-            out[pl.ds(n * width, width), pl.ds(m * width, width)] = value
+                value = sum((code.packed(d, source, at_) for at_, (d, source) in regions if d == dest), code.zero)
+            out[pl.ds(at * width, width), pl.ds(m * width, width)] = value
 
 
 SENT = tuple((side, tile) for side in range(2) for tile in range(2))
@@ -341,12 +351,20 @@
     return sorted({pair for table in tables for tile in table for pair in tile})
 
 
-def choices_kernel(ch, step, steps, codes, along, cross, after, *outs):
+def choices_kernel(ch, step, steps, codes, along, cross, feat, local, *refs):
+    outs, near = refs[: -len(PARTS)], refs[-len(PARTS) :]
     place = Place()
     code = step_codes(ch, place, step, steps, codes, along, cross)
     code.rank_all(all_pairs(FROM_ABOVE, FROM_BELOW))
-    for part, out in zip(PARTS, outs):
-        receive_choice(code, *part, out)
+    half = HALO * ch
+    width = feat.shape[1]
+    for (dests, bottom), mine, out in zip(PARTS, near, outs):
+        receive_choice(code, dests, bottom, mine, out)
+        shift = half if bottom else 0
+        left = [feat[pl.ds(t * BS * ch + shift, half), :] for t in tiles_of(dests, bottom) if isinstance(t, int)]
+        got = jnp.dot(jnp.concatenate(left, axis=1), mine[...], preferred_element_type=F32).astype(BF)
+        for n, dest in enumerate(dests):
+            local[pl.ds((dest * BS + HALO) * ch + shift, half), :] = got[:, n * width : (n + 1) * width]
     if step + 1 < steps:
         code = step_codes(ch, place, step + 1, steps, codes, along, cross)
         code.rank_all(all_pairs(TO_ABOVE, TO_BELOW))
@@ -355,29 +373,33 @@
 
 
 def choice_shapes(width):
-    parts = [(len(tiles_of(*part)) * width, len(part[0]) * width) for part in PARTS]
-    return parts, [(len(sent_regions(*item)) * width, width) for item in SENT]
-
-
-def align(ch, feat, recv, aligned, offset, part, choice, only=None):
+    near, far = [], []
+    for dests, bottom in PARTS:
+        tiles = tiles_of(dests, bottom)
+        own = sum(isinstance(tile, int) for tile in tiles)
+        near.append((own * width, len(dests) * width))
+        far.append(((len(tiles) - own) * width, len(dests) * width))
+    return near, far, [(len(sent_regions(*item)) * width, width) for item in SENT]
+
+
+def align(ch, local, recv, aligned, offset, part, choice, only=None):
     dests, bottom = part
     half = HALO * ch
     shift = half if bottom else 0
-    width = feat.shape[1]
+    width = local.shape[1]
     left = [
-        feat[pl.ds(tile * BS * ch + shift, half), :]
-        if isinstance(tile, int)
-        else recv[tile[0], pl.ds(tile[1] * half, half), :]
-        for tile in tiles_of(dests, bottom)
+        recv[tile[0], pl.ds(tile[1] * half, half), :] for tile in tiles_of(dests, bottom) if not isinstance(tile, int)
     ]
     if only is None:
         right = choice[...]
     else:
         right = choice[:, only * width : (only + 1) * width]
         dests = (dests[only],)
-    got = jnp.dot(jnp.concatenate(left, axis=1), right, preferred_element_type=F32).astype(BF)
+    got = jnp.dot(jnp.concatenate(left, axis=1), right, preferred_element_type=F32)
     for n, d in enumerate(dests):
-        aligned[pl.ds((d * BS + offset) * ch + shift, half), :] = got[:, n * width : (n + 1) * width]
+        near = local[pl.ds((d * BS + HALO) * ch + shift, half), :].astype(F32)
+        both = got[:, n * width : (n + 1) * width] + near
+        aligned[pl.ds((d * BS + offset) * ch + shift, half), :] = both.astype(BF)
 
 
 def pack_messages(ch, fout, par, sent, choices, msg_e, msg_o):
@@ -531,9 +553,8 @@
 
 def outer_kernel(ch, steps, *refs):
     feat_in, saved, saved_held, along, cross, join, conv, codes, far_in, *refs = refs
-    fout, msg_e, msg_o, own_out, part_out, far_out, tmp, sent, *choices = refs
+    fout, msg_e, msg_o, far_out, sent, *choices = refs
     half = HALO * ch
-    strip = BS * ch
     rows = QUAD * BS
     place = Place()
     layers = conv.shape[0]
@@ -577,8 +598,6 @@
         for n, value in enumerate(values[side]):
             fout[pl.ds((starts[side] + n) * ch, ch), :] = value
     pack_messages(ch, fout, place.odd, sent, choices, msg_e, msg_o)
-    channels_first(fout, pl.multiple_of(place.strip * strip, strip), own_out, tmp, ch)
-    channels_first(fout, pl.multiple_of((place.strip ^ 1) * strip, strip), part_out, tmp, ch)
 
 
 def step_kernel(ch, step, steps, *refs):
@@ -593,16 +612,18 @@
         return taken
 
     xq, halo_e, halo_o, join, conv = take(5)
-    feat, feat_e, feat_o = take(3)
+    feat_e, feat_o = take(2)
     choices = take(len(PARTS) + (0 if last else len(SENT)))
     before, out_a, out_b = take(3)
     backs = take(steps - 1 if last else 0)
     held_back = take(step if step == steps - 2 else 0)
+    (local,) = take(1)
     if last:
         (x_inner,) = take(1)
     else:
         next_edges, fout, msg_e, msg_o = take(4)
-    own_out, part_out, out_f, out_g = take(4)
+    own_out, part_out = take(2) if last else (None, None)
+    out_f, out_g = take(2)
     take(len(held_back))
     tmp, act_a, act_b, held, sems, aligned, recv = take(7)
     if last:
@@ -616,7 +637,6 @@
     quad_rows = QUAD * BS
     rows = 2 * BS if last else quad_rows
     right_side = place.side
-    own = place.core if last else place.strip
 
     copies = own_copies(strip, step - 1, steps, before, out_f, out_g, sems.at[0])
     for n, back in enumerate(backs):
@@ -643,19 +663,19 @@
         @pl.when(right_side == 0)
         def _():
             for n in range(3):
-                align(ch, feat, recv, aligned, HALO, PARTS[n], choices[n])
-            align(ch, feat, recv, aligned, HALO, PARTS[3], choices[3], 0)
+                align(ch, local, recv, aligned, HALO, PARTS[n], choices[n])
+            align(ch, local, recv, aligned, HALO, PARTS[3], choices[3], 0)
 
         @pl.when(right_side == 1)
         def _():
             offset = HALO - 2 * BS
-            align(ch, feat, recv, aligned, offset, PARTS[2], choices[2], 1)
+            align(ch, local, recv, aligned, offset, PARTS[2], choices[2], 1)
             for n in range(3, 6):
-                align(ch, feat, recv, aligned, offset, PARTS[n], choices[n])
+                align(ch, local, recv, aligned, offset, PARTS[n], choices[n])
 
     else:
         for n, rows_part in enumerate(PARTS):
-            align(ch, feat, recv, aligned, HALO, rows_part, choices[n])
+            align(ch, local, recv, aligned, HALO, rows_part, choices[n])
         for n in range(2):
             sent[n, pl.ds(halo_at, half), :] = next_edges[n]
 
@@ -686,8 +706,9 @@
     conv_layers(ch, conv, space, rows, act_a, act_b, held, fout)
     if not last:
         pack_messages(ch, fout, par, sent, choices[-len(SENT) :], msg_e, msg_o)
-    channels_first(fout, pl.multiple_of(own * strip, strip), own_out, tmp, ch)
-    channels_first(fout, pl.multiple_of((own ^ 1) * strip, strip), part_out, tmp, ch)
+    else:
+        channels_first(fout, pl.multiple_of(core * strip, strip), own_out, tmp, ch)
+        channels_first(fout, pl.multiple_of((core ^ 1) * strip, strip), part_out, tmp, ch)
     for n, copy in copies:
         pl.when(core == n)(copy.wait)
 
@@ -822,11 +843,12 @@
     whole = (steps * strip, width)
     flat = frames.reshape(steps, strip, width)
     later = ((steps - 1) * strip, width)
-    mine, other, rest = call(
+    first = (strip + crow, width)
+    mine, mine_edge, other, rest = call(
         functools.partial(pack_first_kernel, ch, crow),
         "pack_first",
         (flat, motion_forward, motion_backward),
-        [(strip + crow + half, width)] * 2 + [later],
+        [first, (half, width), (strip + crow + half, width), later],
         [
             pltpu.VMEM((2, *piece), BF),
             pltpu.VMEM((2, *motion_forward.shape), jnp.int32),
@@ -834,31 +856,34 @@
             pltpu.SemaphoreType.DMA((5 + steps,)),
         ],
         in_hbm=(0, 1, 2),
-        out_any=(2,),
+        out_any=(3,),
     )
-    pair, edge, rest = call(
+    pair, edge, edge_too, rest = call(
         functools.partial(pair_first_kernel, ch, crow),
         "pair_first",
-        (mine, send(other, near(1)), rest),
-        [(2 * (strip + crow), width), (2 * (half + crow), width), later],
+        (mine, mine_edge, send(other, near(1)), rest),
+        [(2 * (strip + crow), width), (2 * (half + crow), width), (2 * (half + crow), width), later],
         [tmp],
-        in_any=(2,),
-        out_any=(2,),
-        aliases={2: 2},
+        in_any=(3,),
+        out_any=(3,),
+        aliases={3: 3},
     )
     received = send(pair, near(2))
-    along, cross = sooner(send(edge, along_pairs)), send(edge, cross_pairs)
     swapped = send(rest, near(1))
+    along = send(edge, along_pairs)
     far_pairs = 2 * (steps - 3) * strip
-    pair_near, pair_far, pair_last = call(
+    pair_near, pair_far, pair_last, edge_too = call(
         functools.partial(pair_kernel, ch),
         "pair_rest",
-        (flat, swapped),
-        [(2 * strip + half, width), (far_pairs + (steps - 2) * half, width), (2 * strip, width)],
+        (flat, swapped, edge_too),
+        [(2 * strip + half, width), (far_pairs + (steps - 2) * half, width), (2 * strip, width), edge.shape],
         [tmp, pltpu.SemaphoreType.DMA((2 * steps,))],
         in_hbm=(0,),
-        in_any=(1,),
+        in_any=(1, 2),
+        out_any=(3,),
+        aliases={2: 3},
     )
+    cross = send(edge_too, cross_pairs)
     layers = conv_weight.shape[1]
     conv, join_both, join_first = call(
         weights_kernel,
@@ -870,21 +895,21 @@
     xq, codes, pair_near = call(
         functools.partial(gather_first_kernel, ch, crow),
         "gather_first",
-        (pair, received, pair_near, conv),
+        (pair, received, conv, pair_near),
         [feature, (QUAD * crow, width), pair_near.shape],
         [tmp],
         in_any=(2, 3),
+        out_any=(2,),
+        aliases={3: 2},
         free=True,
-        out_any=(2,),
-        aliases={2: 2},
     )
+    received_near = send(pair_near, near(2))
     halo_e, halo_o = along, cross
 
     wide_act = pltpu.VMEM((3, (rows + 16) * ch, width), BF)
     flops = 2 * (rows + 2 * HALO) * width * ch * ch * 9 * layers
-    part_shapes, sent_shapes = choice_shapes(width)
+    near_shapes, part_shapes, sent_shapes = choice_shapes(width)
     acts = [wide_act, wide_act, pltpu.VMEM(((rows + 16) * ch, width), BF)]
-    received_near = send(pair_near, near(2))
     inner, saved, saved_held = call(
         functools.partial(inner_kernel, ch),
         "refine_inner",
@@ -893,51 +918,52 @@
         acts,
         free=True,
     )
-    feat, msg_e, msg_o, own, part, pair_far = call(
+    feat, msg_e, msg_o, pair_far = call(
         functools.partial(outer_kernel, ch, steps),
         "refine_outer",
         (inner, saved, saved_held, along, cross, join_first, conv, codes, pair_far),
-        [feature, messages[0], messages[0], piece, piece, pair_far.shape],
-        [tmp, pltpu.VMEM((2, *messages[0]), BF)] + [pltpu.VMEM(shape, BF) for shape in sent_shapes],
+        [feature, messages[0], messages[0], pair_far.shape],
+        [pltpu.VMEM((2, *messages[0]), BF)] + [pltpu.VMEM(shape, BF) for shape in sent_shapes],
         flops // 4,
         in_any=(8,),
-        out_any=(5,),
-        aliases={8: 5},
+        out_any=(3,),
+        aliases={8: 3},
     )
     feat_e, feat_o = sooner(send(msg_e, even)), send(msg_o, odd)
-    parts = [part]
+    parts = []
     received_far = send(pair_far, near(2))
-    outputs = call(lambda after, a, b: None, "results", (part,), [whole, whole], in_any=(0,), out_any=(0, 1), free=True)
+    outputs = call(lambda after, a, b: None, "results", (feat,), [whole, whole], in_any=(0,), out_any=(0, 1), free=True)
 
     def choices_of(step):
         return call(
             functools.partial(choices_kernel, ch, step, steps),
             "choices",
-            (codes, along, cross, msg_e),
-            part_shapes + (sent_shapes if step + 1 < steps else []),
-            in_any=(3,),
+            (codes, along, cross, feat),
+            [((rows + 2 * HALO) * ch, width)] + part_shapes + (sent_shapes if step + 1 < steps else []),
+            [pltpu.VMEM(shape, BF) for shape in near_shapes],
         )
 
     def frame_of(step):
         if step == steps - 1:
             kernel = functools.partial(gather_last_kernel, ch, far_pairs + (steps - 3) * half)
-            args, outs = (pair_last, received_far, msg_e), [(2 * strip, width), (half, width)]
+            args, outs = (pair_last, received_far, feat), [(2 * strip, width), (half, width)]
         elif step == 1:
             kernel = functools.partial(gather_kernel, ch, 0, 2 * strip)
-            args, outs = (pair_near, received_near, msg_e), [feature, (2, half, width)]
+            args, outs = (pair_near, received_near, feat), [feature, (2, half, width)]
         else:
             kernel = functools.partial(gather_kernel, ch, 2 * (step - 2) * strip, far_pairs + (step - 2) * half)
-            args, outs = (pair_far, received_far, msg_e), [feature, (2, half, width)]
-        return call(kernel, "gather", args, outs, [tmp], in_any=(2,))
+            args, outs = (pair_far, received_far, feat), [feature, (2, half, width)]
+        return call(kernel, "gather", args, outs + [piece, piece], [tmp])
 
     for step in range(1, steps):
         last = step == steps - 1
-        choices = choices_of(step)
-        x_now, beside = frame_of(step)
-        args = [x_now, halo_e, halo_o, join_both, conv, feat, feat_e, feat_o, *choices, own, *outputs]
+        local, *choices = choices_of(step)
+        x_now, beside, own, part = frame_of(step)
+        parts = parts + [part]
+        args = [x_now, halo_e, halo_o, join_both, conv, feat_e, feat_o, *choices, own, *outputs]
         many = len(args)
         outs = [] if last else [feature, messages[step], messages[step]]
-        outs += [piece, piece, whole, whole]
+        outs += [piece, piece, whole, whole] if last else [whole, whole]
         in_any = [many - 3, many - 2, many - 1]
         out_any = [len(outs) - 2, len(outs) - 1]
         aliases = {many - 2: len(outs) - 2, many - 1: len(outs) - 1}
@@ -946,13 +972,13 @@
             in_any += range(many, many + len(backs))
             args += backs
         elif step == steps - 2:
-            for n, part in enumerate(parts):
+            for part in parts:
                 aliases[len(args)] = len(outs)
                 in_any.append(len(args))
                 out_any.append(len(outs))
                 args.append(part)
                 outs.append(piece)
-        args += [beside]
+        args += [local, beside]
         scratch = [tmp, *acts, pltpu.SemaphoreType.DMA((steps,))]
         scratch += [pltpu.VMEM(((rows + 2 * HALO) * ch, width), BF), pltpu.VMEM((2, 3 * half, width), BF)]
         scratch += [pltpu.VMEM((2 * strip, width) if last else (2, *messages[step]), BF)]
@@ -970,9 +996,11 @@
         if not last:
             feat, msg_e, msg_o, *results = results
             halo_e, halo_o = feat_e, feat_o = sooner(send(msg_e, even)), send(msg_o, odd)
-        own, part, out_f, out_g, *held_back = results
+        if last:
+            own, part, *results = results
+        out_f, out_g, *passed = results
         outputs = out_f, out_g
-        parts = (held_back or parts) + [part]
+        parts = passed or parts
     back = send(part, near(1))
 
     outputs = call(

time: 52.9 us -> 51.9 us (0.981)
  waiting for transfers between devices: 14.2 us -> 12.7 us
    ppermute x17, waiting for transfers between devices: 14.2 us -> 12.7 us  [send(): return lax.ppermute(value, 'tiles', pairs)]
  transfers between devices with their start and end apart: 17 -> 17, of which waited for: 7 -> 7; matrix products, arithmetic and copies ran while one was open for 0% -> 0% of each run, Pallas kernels for 25% -> 28%
where the time goes in v3:
time: 51.9 us; the launch traced here: 51.8 us
  Pallas kernels  23.1 us (45%)
  starting transfers between devices  15 us (29%)
  waiting for transfers between devices  12.7 us (24%)
  between operations  0.99 us (2%)
    pallas_call x18, Pallas kernels, call(): pl.pallas_call(kernel, out_shape=[jax.ShapeDtypeStruct(o, BF) for o in ou...  23.1 us
    ppermute x17, starting transfers between devices, send(): return lax.ppermute(value, 'tiles', pairs)  15 us
    ppermute x17, waiting for transfers between devices, send(): return lax.ppermute(value, 'tiles', pairs)  12.7 us
  transfers between devices with their start and end apart: 17, of which 7 were waited for; matrix products, arithmetic and copies ran while one was open for 0% of the time, Pallas kernels for 28%

profile of v3, /device:TPU:0, one launch (start us, length us, event | category | flops | bytes accessed | tf_op | source)
XLA Modules:
  0.0 51.8 jit_solution(9337029094338828991)
XLA Ops:
  0.7 1.4 %pack_first.1 = (bf16[528,128]{1,0:T(8,128)(2,1)S(1)}, bf16[256,128]{1,0:T(8,128)(2,1)S(1)}, bf16[784,128]{1,0:T(8,128)(2,1)S(1)}, bf16[1536,128]{1,0:T(8,128)(2,1)S(1)}) custom-call(bf16[4,512,128]{2,1,0:T(8,128)(2,1)} %bitcast.3, s32[3,16]{1,0:T(4,128)} %motion_f.1, s32[3,16]{1,0:T(4,128)} %motion_b.1), custom_call_target="tpu_custom_call" | custom-call | bytes 524672 | tf_op jit(solution)/shard_map/pack_first/pallas_call | solution.py:766
  2.6 1.1 %collective-permute-done.partner = bf16[784,128]{1,0:T(8,128)(2,1)S(1)} collective-permute-done((bf16[784,128]{1,0:T(8,128)(2,1)S(1)}, bf16[784,128]{1,0:T(8,128)(2,1)S(1)}, u32[]{:S(2)}, u32[]{:S(2)}) %collective-permute-start) | collective-permute-done | bytes 200736 | tf_op jit(solution)/shard_map/ppermute | solution.py:836
  4.2 2.6 %collective-permute-start.2 = (bf16[1056,128]{1,0:T(8,128)(2,1)S(1)}, bf16[1056,128]{1,0:T(8,128)(2,1)S(1)}, u32[]{:S(2)}, u32[]{:S(2)}) collective-permute-start(bf16[1056,128]{1,0:T(8,128)(2,1)S(1)} %get-tuple-element.95.pair), channel_id=1, source_target_pairs={{0,2},{1,3},{2,0},{3,1},{4,6},{5,7},{6,4},{7,5},{8,10},{9,11},{10,... | collective-permute-start | bytes 811016 | tf_op jit(solution)/shard_map/ppermute | solution.py:836
  6.9 1.3 %collective-permute-start.3 = (bf16[544,128]{1,0:T(8,128)(2,1)S(1)}, bf16[544,128]{1,0:T(8,128)(2,1)S(1)}, u32[]{:S(2)}, u32[]{:S(2)}) collective-permute-start(bf16[544,128]{1,0:T(8,128)(2,1)S(1)} %get-tuple-element.103), channel_id=1, source_target_pairs={{2,6},{3,7},{4,0},{5,1},{6,10},{7,11},{8,4},{9,5},{10,14},{11,15},... | collective-permute-start | bytes 417800 | tf_op jit(solution)/shard_map/ppermute | solution.py:836
  8.2 1.6 %pair_rest.1 = (bf16[1280,128]{1,0:T(8,128)(2,1)S(1)}, bf16[1536,128]{1,0:T(8,128)(2,1)S(1)}, bf16[1024,128]{1,0:T(8,128)(2,1)S(1)}, bf16[544,128]{1,0:T(8,128)(2,1)S(1)}) custom-call(bf16[4,512,128]{2,1,0:T(8,128)(2,1)} %bitcast.4, bf16[1536,128]{1,0:T(8,128)(2,1)S(1)} %collective-permute-done.1.swapped, ...), custom_call_target="tpu_custom_call", output_to_operand_aliasing={{3}: (2, {})} | custom-call | bytes 1056768 | tf_op jit(solution)/shard_map/pair_rest/pallas_call | solution.py:766
  10.2 3.7 %collective-permute-done.2.received = bf16[1056,128]{1,0:T(8,128)(2,1)S(1)} collective-permute-done((bf16[1056,128]{1,0:T(8,128)(2,1)S(1)}, bf16[1056,128]{1,0:T(8,128)(2,1)S(1)}, u32[]{:S(2)}, u32[]{:S(2)}) %collective-permute-start.2) | collective-permute-done | bytes 270368 | tf_op jit(solution)/shard_map/ppermute | solution.py:836
  14.1 1.8 %collective-permute-start.6 = (bf16[1280,128]{1,0:T(8,128)(2,1)S(1)}, bf16[1280,128]{1,0:T(8,128)(2,1)S(1)}, u32[]{:S(2)}, u32[]{:S(2)}) collective-permute-start(bf16[1280,128]{1,0:T(8,128)(2,1)S(1)} %get-tuple-element.108.pair), channel_id=1, source_target_pairs={{0,2},{1,3},{2,0},{3,1},{4,6},{5,7},{6,4},{7,5},{8,10},{9,11},{10,... | collective-permute-start | bytes 983048 | tf_op jit(solution)/shard_map/ppermute | solution.py:836
  15.9 2.4 %refine_inner.1 = (bf16[2048,128]{1,0:T(8,128)(2,1)S(1)}, bf16[4,2,3,128,128]{4,3,2,1,0:T(8,128)(2,1)S(1)}, bf16[4,2,64,128]{3,2,1,0:T(8,128)(2,1)S(1)}) custom-call(bf16[2048,128]{1,0:T(8,128)(2,1)S(1)} %get-tuple-element.98.xq, bf16[128,128]{1,0:T(8,128)(2,1)S(1)} %get-tuple-element.99.join.refs_5_, ...), custom_call_target="tpu_custom_call" | custom-call | tf_op jit(solution)/shard_map/refine_inner/pallas_call | solution.py:766
  18.3 2.2 %refine_outer.1 = (bf16[2048,128]{1,0:T(8,128)(2,1)S(1)}, bf16[640,128]{1,0:T(8,128)(2,1)S(1)}, bf16[640,128]{1,0:T(8,128)(2,1)S(1)}, bf16[1536,128]{1,0:T(8,128)(2,1)S(1)}) custom-call(bf16[2048,128]{1,0:T(8,128)(2,1)S(1)} %get-tuple-element.100.refs_0_, ...), custom_call_target="tpu_custom_call", output_to_operand_aliasing={{3}: (8, {})} | custom-call | flops 377487360 | bytes 2949120 | tf_op jit(solution)/shard_map/refine_outer/pallas_call | solution.py:766
  20.5 1.6 %collective-permute-start.7 = (bf16[640,128]{1,0:T(8,128)(2,1)S(1)}, bf16[640,128]{1,0:T(8,128)(2,1)S(1)}, u32[]{:S(2)}, u32[]{:S(2)}) collective-permute-start(bf16[640,128]{1,0:T(8,128)(2,1)S(1)} %get-tuple-element.112), channel_id=1, source_target_pairs={{0,4},{1,5},{2,6},{3,7},{4,0},{5,1},{6,2},{7,3},{8,12},{9,13},{10,... | collective-permute-start | bytes 491528 | tf_op jit(solution)/shard_map/ppermute | solution.py:836
  22.2 0.6 %collective-permute-start.5 = (bf16[1536,128]{1,0:T(8,128)(2,1)S(1)}, bf16[1536,128]{1,0:T(8,128)(2,1)S(1)}, u32[]{:S(2)}, u32[]{:S(2)}) collective-permute-start(bf16[1536,128]{1,0:T(8,128)(2,1)S(1)} %get-tuple-element.107.pair), channel_id=1, source_target_pairs={{0,2},{1,3},{2,0},{3,1},{4,6},{5,7},{6,4},{7,5},{8,10},{9,11},{10,... | collective-permute-start | bytes 1179656 | tf_op jit(solution)/shard_map/ppermute | solution.py:836
  22.8 1.1 %choices.3 = (bf16[2560,128]{1,0:T(8,128)(2,1)S(1)}, bf16[256,128]{1,0:T(8,128)(2,1)S(1)}, bf16[256,256]{1,0:T(8,128)(2,1)S(1)}, bf16[256,256]{1,0:T(8,128)(2,1)...) custom-call(bf16[64,128]{1,0:T(8,128)(2,1)S(1)} %get-tuple-element.1, ...), custom_call_target="tpu_custom_call" | custom-call | bytes 819200 | tf_op jit(solution)/shard_map/choices/pallas_call | solution.py:766
  23.9 2.0 %collective-permute-done.7.given = bf16[640,128]{1,0:T(8,128)(2,1)S(1)} collective-permute-done((bf16[640,128]{1,0:T(8,128)(2,1)S(1)}, bf16[640,128]{1,0:T(8,128)(2,1)S(1)}, u32[]{:S(2)}, u32[]{:S(2)}) %collective-permute-start.7) | collective-permute-done | bytes 163872 | tf_op jit(solution)/shard_map/ppermute | solution.py:836
  26.4 3.7 %refine.3 = (bf16[2048,128]{1,0:T(8,128)(2,1)S(1)}, bf16[896,128]{1,0:T(8,128)(2,1)S(1)}, bf16[896,128]{1,0:T(8,128)(2,1)S(1)}, bf16[2048,128]{1,0:T(8,128)(2,1)}, bf16[2048,128]{1,0:T(8,128)(2,1)}) custom-call(bf16[2048,128]{1,0:T(8,128)(2,1)S(1)} %get-tuple-element.110.refs_0_, ...), custom_call_target="tpu_custom_call", output_to_operand_aliasing={{3}: (18, {}), {4}: (19, {})} | custom-call | flops 1509949440 | bytes 4931584 | tf_op jit(solution)/shard_map/refine/pallas_call | solution.py:766
  30.1 2.4 %collective-permute-start.9 = (bf16[896,128]{1,0:T(8,128)(2,1)S(1)}, bf16[896,128]{1,0:T(8,128)(2,1)S(1)}, u32[]{:S(2)}, u32[]{:S(2)}) collective-permute-start(bf16[896,128]{1,0:T(8,128)(2,1)S(1)} %get-tuple-element.131), channel_id=1, source_target_pairs={{0,4},{1,5},{2,6},{3,7},{4,0},{5,1},{6,2},{7,3},{8,12},{9,13},{10,... | collective-permute-start | bytes 688136 | tf_op jit(solution)/shard_map/ppermute | solution.py:836
  32.5 1.1 %choices.4 = (bf16[2560,128]{1,0:T(8,128)(2,1)S(1)}, bf16[256,128]{1,0:T(8,128)(2,1)S(1)}, bf16[256,256]{1,0:T(8,128)(2,1)S(1)}, bf16[256,256]{1,0:T(8,128)(2,1)...) custom-call(bf16[64,128]{1,0:T(8,128)(2,1)S(1)} %get-tuple-element.1, ...), custom_call_target="tpu_custom_call" | custom-call | bytes 819200 | tf_op jit(solution)/shard_map/choices/pallas_call | solution.py:766
  34.1 2.5 %collective-permute-done.9.given = bf16[896,128]{1,0:T(8,128)(2,1)S(1)} collective-permute-done((bf16[896,128]{1,0:T(8,128)(2,1)S(1)}, bf16[896,128]{1,0:T(8,128)(2,1)S(1)}, u32[]{:S(2)}, u32[]{:S(2)}) %collective-permute-start.9) | collective-permute-done | bytes 229408 | tf_op jit(solution)/shard_map/ppermute | solution.py:836
  36.6 3.9 %refine.4 = (bf16[2048,128]{1,0:T(8,128)(2,1)S(1)}, bf16[896,128]{1,0:T(8,128)(2,1)S(1)}, bf16[896,128]{1,0:T(8,128)(2,1)S(1)}, bf16[2048,128]{1,0:T(8,128)(2,1)...) custom-call(bf16[2048,128]{1,0:T(8,128)(2,1)S(1)} %get-tuple-element, ...), custom_call_target="tpu_custom_call", output_to_operand_aliasing={{3}: (18, {}), {4}: (19, {}), {5}: (20, {}), {6}: (21, {})} | custom-call | flops 1509949440 | bytes 5505024 | tf_op jit(solution)/shard_map/refine/pallas_call | solution.py:766
  40.5 2.3 %collective-permute-start.11 = (bf16[896,128]{1,0:T(8,128)(2,1)S(1)}, bf16[896,128]{1,0:T(8,128)(2,1)S(1)}, u32[]{:S(2)}, u32[]{:S(2)}) collective-permute-start(bf16[896,128]{1,0:T(8,128)(2,1)S(1)} %get-tuple-element.152), channel_id=1, source_target_pairs={{0,4},{1,5},{2,6},{3,7},{4,0},{5,1},{6,2},{7,3},{8,12},{9,13},{10,... | collective-permute-start | bytes 688136 | tf_op jit(solution)/shard_map/ppermute | solution.py:836
  44.2 0.8 %choices.5 = (bf16[2560,128]{1,0:T(8,128)(2,1)S(1)}, bf16[256,128]{1,0:T(8,128)(2,1)S(1)}, bf16[256,256]{1,0:T(8,128)(2,1)S(1)}, bf16[256,256]{1,0:T(8,128)(2,1)...) custom-call(bf16[64,128]{1,0:T(8,128)(2,1)S(1)} %get-tuple-element.105.refs_7_.codes,, ...), custom_call_target="tpu_custom_call" | custom-call | bytes 819200 | tf_op jit(solution)/shard_map/choices/pallas_call | solution.py:766
  45.0 1.9 %collective-permute-done.11.given = bf16[896,128]{1,0:T(8,128)(2,1)S(1)} collective-permute-done((bf16[896,128]{1,0:T(8,128)(2,1)S(1)}, bf16[896,128]{1,0:T(8,128)(2,1)S(1)}, u32[]{:S(2)}, u32[]{:S(2)}) %collective-permute-start.11) | collective-permute-done | bytes 229408 | tf_op jit(solution)/shard_map/ppermute | solution.py:836
  46.9 2.6 %refine.5 = (bf16[512,128]{1,0:T(8,128)(2,1)S(1)}, bf16[512,128]{1,0:T(8,128)(2,1)S(1)}, bf16[2048,128]{1,0:T(8,128)(2,1)}, bf16[2048,128]{1,0:T(8,128)(2,1)}) custom-call(bf16[1024,128]{1,0:T(8,128)(2,1)S(1)} %get-tuple-element.151.refs_0_, bf16[896,128]{1,0:T(8,128)(2,1)S(1)} %sooner.5.refs_1_.refs_5_, ...), custom_call_target="tpu_custom_call", output_to_operand_aliasing={{2}: (14, {}), {3}: (15, {})} | custom-call | flops 1509949440 | bytes 4980736 | tf_op jit(solution)/shard_map/refine/pallas_call | solution.py:766
  49.5 1.3 %collective-permute-done.16.back = bf16[512,128]{1,0:T(8,128)(2,1)S(1)} collective-permute-done((bf16[512,128]{1,0:T(8,128)(2,1)S(1)}, bf16[512,128]{1,0:T(8,128)(2,1)S(1)}, u32[]{:S(2)}, u32[]{:S(2)}) %collective-permute-start.16) | collective-permute-done | bytes 131104 | tf_op jit(solution)/shard_map/ppermute | solution.py:836
  50.9 0.7 %finish.1 = (bf16[2048,128]{1,0:T(8,128)(2,1)}, bf16[2048,128]{1,0:T(8,128)(2,1)}) custom-call(bf16[512,128]{1,0:T(8,128)(2,1)S(1)} %get-tuple-element.168.own, bf16[512,128]{1,0:T(8,128)(2,1)S(1)} %collective-permute-done.16.back, bf16[2048,128]{1,0:T(8,128)(2,1)} %get-tuple-element.170.out_a, ...), custom_call_target="tpu_custom_call", output_to_operand_aliasing={{0}: (2, {}), {1}: (3, {})} | custom-call | bytes 1310720 | tf_op jit(solution)/shard_map/finish/pallas_call | solution.py:766
  (35 shorter events, 4.0 us)
Async XLA Ops:
  0.6 9.3 %copy-start = (bf16[2,4,9,64,64]{4,3,2,1,0:T(8,128)(2,1)S(1)}, bf16[2,4,9,64,64]{4,3,2,1,0:T(8,128)(2,1)}, u32[]{:S(2)}) copy-start(bf16[2,4,9,64,64]{4,3,2,1,0:T(8,128)(2,1)} %conv.1) | copy-start | bytes 1769476
  0.6 9.3 %copy-start.1 = (bf16[2,64,128]{2,1,0:T(8,128)(2,1)S(1)}, bf16[2,64,128]{2,1,0:T(8,128)(2,1)}, u32[]{:S(2)}) copy-start(bf16[2,64,128]{2,1,0:T(8,128)(2,1)} %join.1) | copy-start | bytes 98308
  2.1 1.6 %collective-permute-start = (bf16[784,128]{1,0:T(8,128)(2,1)S(1)}, bf16[784,128]{1,0:T(8,128)(2,1)S(1)}, u32[]{:S(2)}, u32[]{:S(2)}) collective-permute-start(bf16[784,128]{1,0:T(8,128)(2,1)S(1)} %get-tuple-element.90), channel_id=1, source_target_pairs={{0,1},{1,0},{2,3},{3,2},{4,5},{5,4},{6,7},{7,6},{8,9},{9,8},{10,11... | collective-permute-start | bytes 602120 | tf_op jit(solution)/shard_map/ppermute | solution.py:836
  3.8 4.4 %collective-permute-start.1 = (bf16[1536,128]{1,0:T(8,128)(2,1)S(1)}, bf16[1536,128]{1,0:T(8,128)(2,1)S(1)}, u32[]{:S(2)}, u32[]{:S(2)}) collective-permute-start(bf16[1536,128]{1,0:T(8,128)(2,1)S(1)} %get-tuple-element.92), channel_id=1, source_target_pairs={{0,1},{1,0},{2,3},{3,2},{4,5},{5,4},{6,7},{7,6},{8,9},{9,8},{10,11... | collective-permute-start | bytes 1179656 | tf_op jit(solution)/shard_map/ppermute | solution.py:836
  4.2 9.6 %collective-permute-start.2 = (bf16[1056,128]{1,0:T(8,128)(2,1)S(1)}, bf16[1056,128]{1,0:T(8,128)(2,1)S(1)}, u32[]{:S(2)}, u32[]{:S(2)}) collective-permute-start(bf16[1056,128]{1,0:T(8,128)(2,1)S(1)} %get-tuple-element.95.pair), channel_id=1, source_target_pairs={{0,2},{1,3},{2,0},{3,1},{4,6},{5,7},{6,4},{7,5},{8,10},{9,11},{10,... | collective-permute-start | bytes 811016 | tf_op jit(solution)/shard_map/ppermute | solution.py:836
  6.9 11.4 %collective-permute-start.3 = (bf16[544,128]{1,0:T(8,128)(2,1)S(1)}, bf16[544,128]{1,0:T(8,128)(2,1)S(1)}, u32[]{:S(2)}, u32[]{:S(2)}) collective-permute-start(bf16[544,128]{1,0:T(8,128)(2,1)S(1)} %get-tuple-element.103), channel_id=1, source_target_pairs={{2,6},{3,7},{4,0},{5,1},{6,10},{7,11},{8,4},{9,5},{10,14},{11,15},... | collective-permute-start | bytes 417800 | tf_op jit(solution)/shard_map/ppermute | solution.py:836
  9.8 8.5 %collective-permute-start.4 = (bf16[544,128]{1,0:T(8,128)(2,1)S(1)}, bf16[544,128]{1,0:T(8,128)(2,1)S(1)}, u32[]{:S(2)}, u32[]{:S(2)}) collective-permute-start(bf16[544,128]{1,0:T(8,128)(2,1)S(1)} %get-tuple-element.104), channel_id=1, source_target_pairs={{0,1},{1,0},{2,4},{3,5},{4,2},{5,3},{6,8},{7,9},{8,6},{9,7},{10,12... | collective-permute-start | bytes 417800 | tf_op jit(solution)/shard_map/ppermute | solution.py:836
  14.1 11.8 %collective-permute-start.6 = (bf16[1280,128]{1,0:T(8,128)(2,1)S(1)}, bf16[1280,128]{1,0:T(8,128)(2,1)S(1)}, u32[]{:S(2)}, u32[]{:S(2)}) collective-permute-start(bf16[1280,128]{1,0:T(8,128)(2,1)S(1)} %get-tuple-element.108.pair), channel_id=1, source_target_pairs={{0,2},{1,3},{2,0},{3,1},{4,6},{5,7},{6,4},{7,5},{8,10},{9,11},{10,... | collective-permute-start | bytes 983048 | tf_op jit(solution)/shard_map/ppermute | solution.py:836
  20.5 5.4 %collective-permute-start.7 = (bf16[640,128]{1,0:T(8,128)(2,1)S(1)}, bf16[640,128]{1,0:T(8,128)(2,1)S(1)}, u32[]{:S(2)}, u32[]{:S(2)}) collective-permute-start(bf16[640,128]{1,0:T(8,128)(2,1)S(1)} %get-tuple-element.112), channel_id=1, source_target_pairs={{0,4},{1,5},{2,6},{3,7},{4,0},{5,1},{6,2},{7,3},{8,12},{9,13},{10,... | collective-permute-start | bytes 491528 | tf_op jit(solution)/shard_map/ppermute | solution.py:836
  22.2 4.2 %collective-permute-start.8 = (bf16[640,128]{1,0:T(8,128)(2,1)S(1)}, bf16[640,128]{1,0:T(8,128)(2,1)S(1)}, u32[]{:S(2)}, u32[]{:S(2)}) collective-permute-start(bf16[640,128]{1,0:T(8,128)(2,1)S(1)} %get-tuple-element.113), channel_id=1, source_target_pairs={{0,1},{1,0},{2,3},{3,2},{4,8},{5,9},{6,10},{7,11},{8,4},{9,5},{10,... | collective-permute-start | bytes 491528 | tf_op jit(solution)/shard_map/ppermute | solution.py:836
  22.2 11.5 %collective-permute-start.5 = (bf16[1536,128]{1,0:T(8,128)(2,1)S(1)}, bf16[1536,128]{1,0:T(8,128)(2,1)S(1)}, u32[]{:S(2)}, u32[]{:S(2)}) collective-permute-start(bf16[1536,128]{1,0:T(8,128)(2,1)S(1)} %get-tuple-element.107.pair), channel_id=1, source_target_pairs={{0,2},{1,3},{2,0},{3,1},{4,6},{5,7},{6,4},{7,5},{8,10},{9,11},{10,... | collective-permute-start | bytes 1179656 | tf_op jit(solution)/shard_map/ppermute | solution.py:836
  30.1 6.5 %collective-permute-start.9 = (bf16[896,128]{1,0:T(8,128)(2,1)S(1)}, bf16[896,128]{1,0:T(8,128)(2,1)S(1)}, u32[]{:S(2)}, u32[]{:S(2)}) collective-permute-start(bf16[896,128]{1,0:T(8,128)(2,1)S(1)} %get-tuple-element.131), channel_id=1, source_target_pairs={{0,4},{1,5},{2,6},{3,7},{4,0},{5,1},{6,2},{7,3},{8,12},{9,13},{10,... | collective-permute-start | bytes 688136 | tf_op jit(solution)/shard_map/ppermute | solution.py:836
  32.5 4.1 %collective-permute-start.10 = (bf16[896,128]{1,0:T(8,128)(2,1)S(1)}, bf16[896,128]{1,0:T(8,128)(2,1)S(1)}, u32[]{:S(2)}, u32[]{:S(2)}) collective-permute-start(bf16[896,128]{1,0:T(8,128)(2,1)S(1)} %get-tuple-element.132), channel_id=1, source_target_pairs={{0,1},{1,0},{2,3},{3,2},{4,8},{5,9},{6,10},{7,11},{8,4},{9,5},{10,... | collective-permute-start | bytes 688136 | tf_op jit(solution)/shard_map/ppermute | solution.py:836
  40.5 6.3 %collective-permute-start.11 = (bf16[896,128]{1,0:T(8,128)(2,1)S(1)}, bf16[896,128]{1,0:T(8,128)(2,1)S(1)}, u32[]{:S(2)}, u32[]{:S(2)}) collective-permute-start(bf16[896,128]{1,0:T(8,128)(2,1)S(1)} %get-tuple-element.152), channel_id=1, source_target_pairs={{0,4},{1,5},{2,6},{3,7},{4,0},{5,1},{6,2},{7,3},{8,12},{9,13},{10,... | collective-permute-start | bytes 688136 | tf_op jit(solution)/shard_map/ppermute | solution.py:836
  42.8 4.0 %collective-permute-start.12 = (bf16[896,128]{1,0:T(8,128)(2,1)S(1)}, bf16[896,128]{1,0:T(8,128)(2,1)S(1)}, u32[]{:S(2)}, u32[]{:S(2)}) collective-permute-start(bf16[896,128]{1,0:T(8,128)(2,1)S(1)} %get-tuple-element.153), channel_id=1, source_target_pairs={{0,1},{1,0},{2,3},{3,2},{4,8},{5,9},{6,10},{7,11},{8,4},{9,5},{10,... | collective-permute-start | bytes 688136 | tf_op jit(solution)/shard_map/ppermute | solution.py:836
  42.8 4.0 %collective-permute-start.13 = (bf16[512,128]{1,0:T(8,128)(2,1)S(1)}, bf16[512,128]{1,0:T(8,128)(2,1)S(1)}, u32[]{:S(2)}, u32[]{:S(2)}) collective-permute-start(bf16[512,128]{1,0:T(8,128)(2,1)S(1)} %get-tuple-element.163), channel_id=1, source_target_pairs={{0,1},{1,0},{2,3},{3,2},{4,5},{5,4},{6,7},{7,6},{8,9},{9,8},{10,11... | collective-permute-start | bytes 393224 | tf_op jit(solution)/shard_map/ppermute | solution.py:836
  43.3 3.5 %collective-permute-start.14 = (bf16[512,128]{1,0:T(8,128)(2,1)S(1)}, bf16[512,128]{1,0:T(8,128)(2,1)S(1)}, u32[]{:S(2)}, u32[]{:S(2)}) collective-permute-start(bf16[512,128]{1,0:T(8,128)(2,1)S(1)} %get-tuple-element.164), channel_id=1, source_target_pairs={{0,1},{1,0},{2,3},{3,2},{4,5},{5,4},{6,7},{7,6},{8,9},{9,8},{10,11... | collective-permute-start | bytes 393224 | tf_op jit(solution)/shard_map/ppermute | solution.py:836
  43.6 3.2 %collective-permute-start.15 = (bf16[512,128]{1,0:T(8,128)(2,1)S(1)}, bf16[512,128]{1,0:T(8,128)(2,1)S(1)}, u32[]{:S(2)}, u32[]{:S(2)}) collective-permute-start(bf16[512,128]{1,0:T(8,128)(2,1)S(1)} %get-tuple-element.165), channel_id=1, source_target_pairs={{0,1},{1,0},{2,3},{3,2},{4,5},{5,4},{6,7},{7,6},{8,9},{9,8},{10,11... | collective-permute-start | bytes 393224 | tf_op jit(solution)/shard_map/ppermute | solution.py:836
  49.5 1.4 %collective-permute-start.16 = (bf16[512,128]{1,0:T(8,128)(2,1)S(1)}, bf16[512,128]{1,0:T(8,128)(2,1)S(1)}, u32[]{:S(2)}, u32[]{:S(2)}) collective-permute-start(bf16[512,128]{1,0:T(8,128)(2,1)S(1)} %get-tuple-element.169), channel_id=1, source_target_pairs={{0,1},{1,0},{2,3},{3,2},{4,5},{5,4},{6,7},{7,6},{8,9},{9,8},{10,11... | collective-permute-start | bytes 393224 | tf_op jit(solution)/shard_map/ppermute | solution.py:836

commit v4 on v3

--- a/solution.py
+++ b/solution.py
@@ -192,7 +192,7 @@
             codes[pl.ds(code_at, crow), :] = piece[pl.ds(2 * strip + m * crow, crow), :]
 
 
-def gather_kernel(ch, pair_at, edge_at, pair, received, feat, xq, edges, own_out, part_out, tmp):
+def gather_kernel(ch, pair_at, edge_at, pair, received, after, xq, edges, tmp):
     strip = BS * ch
     half = HALO * ch
     side = Place().side
@@ -201,7 +201,6 @@
             start = ((side + n) % 2 * 2 + m) * strip
             rows_first(piece, pair_at + m * strip, xq, pl.multiple_of(start, strip), tmp, ch)
         edges[side ^ n] = piece[pl.ds(edge_at, half), :]
-    split_results(ch, feat, own_out, part_out, tmp)
 
 
 def split_results(ch, feat, own_out, part_out, tmp):
@@ -211,12 +210,11 @@
     channels_first(feat, pl.multiple_of((own ^ 1) * strip, strip), part_out, tmp, ch)
 
 
-def gather_last_kernel(ch, inner_at, pair, received, feat, xq, inner, own_out, part_out, tmp):
+def gather_last_kernel(ch, inner_at, pair, received, after, xq, inner, tmp):
     strip = BS * ch
     for m in range(2):
         rows_first(pair, m * strip, xq, m * strip, tmp, ch)
     inner[...] = received[pl.ds(inner_at, HALO * ch), :]
-    split_results(ch, feat, own_out, part_out, tmp)
 
 
 class Codes:
@@ -269,13 +267,13 @@
         )
 
 
-FROM_ABOVE = (((0, -2), (-1, -2), (-1, -3), (1, -1)), ((0, -1), (0, -2)))
-FROM_BELOW = (
-    ((QUAD - 1, QUAD + 1), (QUAD, QUAD + 1), (QUAD, QUAD + 2), (QUAD - 2, QUAD)),
-    ((QUAD - 1, QUAD), (QUAD - 1, QUAD + 1)),
-)
-TO_BELOW = tuple(tuple((d + QUAD, s + QUAD) for d, s in tile) for tile in FROM_ABOVE)
-TO_ABOVE = tuple(tuple((d - QUAD, s - QUAD) for d, s in tile) for tile in FROM_BELOW)
+FROM_ABOVE = ((0, -1), (0, -2), (1, -1))
+FROM_BELOW = ((QUAD - 1, QUAD), (QUAD - 1, QUAD + 1), (QUAD - 2, QUAD))
+TO_BELOW = tuple((d + QUAD, s + QUAD) for d, s in FROM_ABOVE)
+TO_ABOVE = tuple((d - QUAD, s - QUAD) for d, s in FROM_BELOW)
+TAKEN = (FROM_ABOVE, FROM_BELOW)
+GIVEN = (TO_ABOVE, TO_BELOW)
+REGIONS = len(FROM_ABOVE)
 
 
 def step_codes(ch, place, step, steps, codes, along, cross):
@@ -297,140 +295,131 @@
     return Codes(rows)
 
 
-PARTS = (((-1,), True), ((0, 1), False), ((0, 1), True), ((2, 3), False), ((2, 3), True), ((QUAD,), False))
-
-
-def tiles_of(dests, bottom):
-    tiles = [source for source in range(QUAD) if any(abs(source - d) <= REACH for d in dests)]
-    for side, near, tables in ((0, -1, FROM_ABOVE), (1, QUAD, FROM_BELOW)):
-        if any(abs(near - d) <= REACH for d in dests):
-            whole = bottom if side == 0 else not bottom
-            tiles += [(side, 0), (side, 1)] if whole else [(side, 1), (side, 2)]
-    return tiles
-
-
-def receive_choice(code, dests, bottom, near, far):
-    width = code.zero.shape[0]
-    tiles = tiles_of(dests, bottom)
-    own = sum(isinstance(tile, int) for tile in tiles)
-    for n, tile in enumerate(tiles):
-        out, at = (near, n) if n < own else (far, n - own)
-        for m, dest in enumerate(dests):
-            if isinstance(tile, int):
-                value = code.plain(dest, tile)
-            elif tile[1] == 0:
-                value = code.plain(dest, -1 if tile[0] == 0 else QUAD)
-            else:
-                side, kind = tile
-                regions = list(enumerate((FROM_ABOVE, FROM_BELOW)[side][kind - 1]))
-                if kind == 1:
-                    regions = regions[:3] if bottom == (side == 0) else regions[3:]
-                value = sum((code.packed(d, source, at_) for at_, (d, source) in regions if d == dest), code.zero)
-            out[pl.ds(at * width, width), pl.ds(m * width, width)] = value
-
-
-SENT = tuple((side, tile) for side in range(2) for tile in range(2))
-
-
-def sent_regions(side, tile):
-    picks = {}
-    for at, (dest, source) in enumerate((TO_ABOVE, TO_BELOW)[side][tile]):
-        lower = (side == 1) == (tile == 0 and at < 3)
-        picks.setdefault((source, lower), []).append((at, dest))
-    return picks
-
-
-def send_choice(code, side, tile, out):
-    width = out.shape[1]
-    for n, ((source, _), regions) in enumerate(sent_regions(side, tile).items()):
-        total = sum(code.pack(dest, source, at) for at, dest in regions)
-        out[pl.ds(n * width, width), :] = total.astype(BF)
-
-
-def all_pairs(*tables):
-    return sorted({pair for table in tables for tile in table for pair in tile})
-
-
-def choices_kernel(ch, step, steps, codes, along, cross, feat, local, *refs):
-    outs, near = refs[: -len(PARTS)], refs[-len(PARTS) :]
+def own_sources(dest):
+    return [source for source in range(QUAD) if abs(source - dest) <= REACH]
+
+
+def choices_kernel(ch, step, steps, codes, along, cross, feat, local, own_out, part_out, *refs):
     place = Place()
     code = step_codes(ch, place, step, steps, codes, along, cross)
-    code.rank_all(all_pairs(FROM_ABOVE, FROM_BELOW))
+    code.rank_all(FROM_ABOVE + FROM_BELOW)
     half = HALO * ch
+    strip = BS * ch
     width = feat.shape[1]
-    for (dests, bottom), mine, out in zip(PARTS, near, outs):
-        receive_choice(code, dests, bottom, mine, out)
-        shift = half if bottom else 0
-        left = [feat[pl.ds(t * BS * ch + shift, half), :] for t in tiles_of(dests, bottom) if isinstance(t, int)]
-        got = jnp.dot(jnp.concatenate(left, axis=1), mine[...], preferred_element_type=F32).astype(BF)
-        for n, dest in enumerate(dests):
-            local[pl.ds((dest * BS + HALO) * ch + shift, half), :] = got[:, n * width : (n + 1) * width]
+    for pair in range(0, QUAD, 2):
+        left = [feat[pl.ds(source * strip, strip), :] for source in range(QUAD)]
+        right = [
+            jnp.concatenate([code.plain(pair + m, source) for m in range(2)], axis=1) for source in range(QUAD)
+        ]
+        got = jnp.dot(
+            jnp.concatenate(left, axis=1), jnp.concatenate(right, axis=0), preferred_element_type=F32
+        ).astype(BF)
+        for m in range(2):
+            local[pl.ds(half + (pair + m) * strip, strip), :] = got[:, m * width : (m + 1) * width]
+    for dest, shift, at in ((-1, half, 0), (QUAD, 0, half + QUAD * strip)):
+        sources = own_sources(dest)
+        left = [feat[pl.ds(source * strip + shift, half), :] for source in sources]
+        right = [code.plain(dest, source) for source in sources]
+        local[pl.ds(at, half), :] = jnp.dot(
+            jnp.concatenate(left, axis=1), jnp.concatenate(right, axis=0), preferred_element_type=F32
+        ).astype(BF)
+    for side in range(2):
+        for m in range(2):
+            value = [
+                code.packed(dest, source, n) for n, (dest, source) in enumerate(TAKEN[side]) if dest == 2 * side + m
+            ]
+            refs[side][:, pl.ds(m * width, width)] = sum(value[1:], value[0])
     if step + 1 < steps:
-        code = step_codes(ch, place, step + 1, steps, codes, along, cross)
-        code.rank_all(all_pairs(TO_ABOVE, TO_BELOW))
-        for item, out in zip(SENT, outs[len(PARTS) :]):
-            send_choice(code, *item, out)
+        send_choices(code_of_next(ch, place, step, steps, codes, along, cross), refs[2:-1])
+    split_results(ch, feat, own_out, part_out, refs[-1])
+
+
+def code_of_next(ch, place, step, steps, codes, along, cross):
+    code = step_codes(ch, place, step + 1, steps, codes, along, cross)
+    code.rank_all(TO_ABOVE + TO_BELOW)
+    return code
+
+
+def given_sources(side):
+    return sorted({source for _, source in GIVEN[side]})
+
+
+def send_choices(code, outs):
+    width = code.zero.shape[0]
+    for side in range(2):
+        blocks, edge = outs[2 * side : 2 * side + 2]
+        for n, source in enumerate(given_sources(side)):
+            total = sum(code.pack(d, source, at) for at, (d, origin) in enumerate(GIVEN[side]) if origin == source)
+            blocks[pl.ds(n * width, width), :] = total.astype(BF)
+        dest = side * (QUAD - 1)
+        for n, source in enumerate(own_sources(dest)):
+            edge[pl.ds(n * width, width), :] = code.plain(dest, source)
 
 
 def choice_shapes(width):
-    near, far = [], []
-    for dests, bottom in PARTS:
-        tiles = tiles_of(dests, bottom)
-        own = sum(isinstance(tile, int) for tile in tiles)
-        near.append((own * width, len(dests) * width))
-        far.append(((len(tiles) - own) * width, len(dests) * width))
-    return near, far, [(len(sent_regions(*item)) * width, width) for item in SENT]
-
-
-def align(ch, local, recv, aligned, offset, part, choice, only=None):
-    dests, bottom = part
-    half = HALO * ch
-    shift = half if bottom else 0
-    width = local.shape[1]
-    left = [
-        recv[tile[0], pl.ds(tile[1] * half, half), :] for tile in tiles_of(dests, bottom) if not isinstance(tile, int)
-    ]
-    if only is None:
-        right = choice[...]
-    else:
-        right = choice[:, only * width : (only + 1) * width]
-        dests = (dests[only],)
-    got = jnp.dot(jnp.concatenate(left, axis=1), right, preferred_element_type=F32)
-    for n, d in enumerate(dests):
-        near = local[pl.ds((d * BS + HALO) * ch + shift, half), :].astype(F32)
-        both = got[:, n * width : (n + 1) * width] + near
-        aligned[pl.ds((d * BS + offset) * ch + shift, half), :] = both.astype(BF)
-
-
-def pack_messages(ch, fout, par, sent, choices, msg_e, msg_o):
+    sent = []
+    for side in range(2):
+        sent += [(len(given_sources(side)) * width, width), (len(own_sources(side * (QUAD - 1))) * width, width)]
+    return [(width, 2 * width)] * 2, sent
+
+
+def join_rows(ch, join_mat, al, inp, extra=None):
+    width = al.shape[1]
+    sides = []
+    for h in range(2):
+        a, b = 2 * h * ch, (2 * h + 1) * ch
+        sides.append(jnp.concatenate([al[a : a + ch], inp[a : a + ch], al[b : b + ch], inp[b : b + ch]], axis=0))
+    mixed = jnp.dot(join_mat, jnp.concatenate(sides, axis=1), preferred_element_type=F32)
+    rows = [mixed[q * ch : (q + 1) * ch, h * width : (h + 1) * width] for h in range(2) for q in range(2)]
+    if extra is not None:
+        rows = [row + extra[n * ch : (n + 1) * ch].astype(F32) for n, row in enumerate(rows)]
+    return [row.astype(BF) for row in rows]
+
+
+def fold_rows(ch):
+    return BS * ch * REGIONS // (REGIONS + 1)
+
+
+def pack_messages(ch, fout, par, join_mat, choices, inputs, sent, msg_e, msg_o):
     half = HALO * ch
     strip = BS * ch
     width = fout.shape[1]
-    for side, near in ((0, 0), (1, QUAD - 1)):
-        shift = half if side == 1 else 0
-        sent[side, pl.ds(0, half), :] = fout[pl.ds(near * strip + shift, half), :]
-    for (side, tile), choice in zip(SENT, choices):
-        left = [
-            fout[pl.ds(source * strip + (half if lower else 0), half), :] for source, lower in sent_regions(side, tile)
-        ]
-        got = jnp.dot(jnp.concatenate(left, axis=1), choice[...], preferred_element_type=F32).astype(BF)
-        if tile == 0:
-            sent[side, pl.ds(half, half), :] = got
-        else:
-            lane = lax.broadcasted_iota(jnp.int32, (half // 2, width), 1)
-            folded = jnp.where(lane < width // 2, got[: half // 2], pltpu.roll(got[half // 2 :], width // 2, 1))
-            sent[side, pl.ds(2 * half, half // 2), :] = folded
+    fold = fold_rows(ch)
+    piece = strip - fold
+    group = width // (REGIONS + 1)
+    lane = lax.broadcasted_iota(jnp.int32, (piece, width), 1)
+    for side in range(2):
+        blocks, edge = choices[2 * side : 2 * side + 2]
+        left = [fout[pl.ds(source * strip, strip), :] for source in given_sources(side)]
+        got = jnp.dot(jnp.concatenate(left, axis=1), blocks[...], preferred_element_type=F32).astype(BF)
+        for n in range(REGIONS):
+            rolled = pltpu.roll(got[fold:], (REGIONS - n) * group, 1)
+            sent[side, pl.ds(n * piece, piece), :] = jnp.where(
+                lane < REGIONS * group, got[n * piece : (n + 1) * piece], rolled
+            )
+        shift = side * half
+        left = [fout[pl.ds(source * strip + shift, half), :] for source in own_sources(side * (QUAD - 1))]
+        al = jnp.dot(jnp.concatenate(left, axis=1), edge[...], preferred_element_type=F32).astype(BF)
+        inp = jnp.zeros((half, width), BF) if inputs is None else inputs[side]
+        for n, row in enumerate(join_rows(ch, join_mat, al, inp)):
+            sent[side, pl.ds(fold + n * ch, ch), :] = row
     msg_e[...] = sent[1 - par]
     msg_o[...] = sent[par]
 
 
 def unpack_message(ch, message, recv, side):
-    half = HALO * ch
+    strip = BS * ch
     width = message.shape[1]
-    recv[side, pl.ds(0, 2 * half), :] = message[pl.ds(0, 2 * half), :]
-    folded = message[pl.ds(2 * half, half // 2), :]
-    recv[side, pl.ds(2 * half, half // 2), :] = folded
-    recv[side, pl.ds(2 * half + half // 2, half // 2), :] = pltpu.roll(folded, width // 2, 1)
+    fold = fold_rows(ch)
+    piece = strip - fold
+    group = width // (REGIONS + 1)
+    lane = lax.broadcasted_iota(jnp.int32, (piece, width), 1)
+    recv[side, pl.ds(0, fold), :] = message[pl.ds(0, fold), :]
+    total = None
+    for n in range(REGIONS):
+        rolled = pltpu.roll(message[pl.ds(n * piece, piece), :], (n + 1) * group, 1)
+        total = rolled if total is None else jnp.where(lane < n * group, total, rolled)
+    recv[side, pl.ds(fold, piece), :] = total
 
 
 class Rows:
@@ -552,7 +541,7 @@
 
 
 def outer_kernel(ch, steps, *refs):
-    feat_in, saved, saved_held, along, cross, join, conv, codes, far_in, *refs = refs
+    feat_in, saved, saved_held, along, cross, join, join_both, conv, codes, far_in, *refs = refs
     fout, msg_e, msg_o, far_out, sent, *choices = refs
     half = HALO * ch
     rows = QUAD * BS
@@ -560,10 +549,7 @@
     layers = conv.shape[0]
     width = feat_in.shape[1]
     space = Rows(ch, width, jnp.logical_not(place.top), jnp.logical_not(place.bottom), rows)
-    code = step_codes(ch, place, 1, steps, codes, along, cross)
-    code.rank_all(all_pairs(TO_ABOVE, TO_BELOW))
-    for item, out in zip(SENT, choices):
-        send_choice(code, *item, out)
+    send_choices(code_of_next(ch, place, 0, steps, codes, along, cross), choices)
     fout[pl.ds(half, (rows - 2 * HALO) * ch), :] = feat_in[pl.ds(half, (rows - 2 * HALO) * ch), :]
     halos = above_below(place, along[pl.ds(0, half), :], cross[pl.ds(0, half), :])
     join_mat = join[...]
@@ -597,7 +583,7 @@
     for side in range(2):
         for n, value in enumerate(values[side]):
             fout[pl.ds((starts[side] + n) * ch, ch), :] = value
-    pack_messages(ch, fout, place.odd, sent, choices, msg_e, msg_o)
+    pack_messages(ch, fout, place.odd, join_both[...], choices, None, sent, msg_e, msg_o)
 
 
 def step_kernel(ch, step, steps, *refs):
@@ -611,12 +597,10 @@
         del refs[:count]
         return taken
 
-    xq, halo_e, halo_o, join, conv = take(5)
+    xq, along, cross, join, conv = take(5)
     feat_e, feat_o = take(2)
-    choices = take(len(PARTS) + (0 if last else len(SENT)))
+    choices = take(2 if last else 6)
     before, out_a, out_b = take(3)
-    backs = take(steps - 1 if last else 0)
-    held_back = take(step if step == steps - 2 else 0)
     (local,) = take(1)
     if last:
         (x_inner,) = take(1)
@@ -624,7 +608,6 @@
         next_edges, fout, msg_e, msg_o = take(4)
     own_out, part_out = take(2) if last else (None, None)
     out_f, out_g = take(2)
-    take(len(held_back))
     tmp, act_a, act_b, held, sems, aligned, recv = take(7)
     if last:
         (fout,) = take(1)
@@ -634,78 +617,63 @@
     place = Place()
     par = place.odd
     core = place.core
-    quad_rows = QUAD * BS
-    rows = 2 * BS if last else quad_rows
-    right_side = place.side
+    rows = 2 * BS if last else QUAD * BS
+    left_side = place.side == 0
 
     copies = own_copies(strip, step - 1, steps, before, out_f, out_g, sems.at[0])
-    for n, back in enumerate(backs):
-        copies += back_copies(strip, n, steps, back, out_f, out_g, sems.at[1 + n])
     for n, copy in copies:
         pl.when(core == n)(copy.start)
-    halo_at = 5 * half // 2
+
+    def choose(which, one, two):
+        return jnp.where(which, one.astype(F32), two.astype(F32)).astype(BF)
+
+    fold = fold_rows(ch)
+    zero = jnp.zeros((half, width), BF)
+    one, two = feat_e[pl.ds(fold, half), :], feat_o[pl.ds(fold, half), :]
+    over_sent, under_sent = choose(par == 1, one, two), choose(par == 1, two, one)
+    over, under = zero, zero
     if step == 1:
-        over, under = above_below(place, halo_e[pl.ds(half, half), :], halo_o[pl.ds(half, half), :])
-    else:
-        one, two = halo_e[pl.ds(halo_at, half), :].astype(F32), halo_o[pl.ds(halo_at, half), :].astype(F32)
-        over = jnp.where(par == 1, one, two).astype(BF)
-        under = jnp.where(par == 1, two, one).astype(BF)
+        over, under = above_below(place, along[pl.ds(half, half), :], cross[pl.ds(half, half), :])
     if last:
-        inner = x_inner[...].astype(F32)
-        over, under = (
-            jnp.where(right_side == 0, over.astype(F32), inner).astype(BF),
-            jnp.where(right_side == 0, inner, under.astype(F32)).astype(BF),
-        )
+        inner = x_inner[...]
+        over, under = choose(left_side, zero, inner), choose(left_side, inner, zero)
+        over_sent, under_sent = choose(left_side, over_sent, zero), choose(left_side, zero, under_sent)
     unpack_message(ch, feat_e, recv, 1 - par)
     unpack_message(ch, feat_o, recv, par)
+    for edge in (0, half + QUAD * strip):
+        aligned[pl.ds(edge, half), :] = local[pl.ds(edge, half), :]
+    for side in range(2):
+        got = jnp.dot(recv[side], choices[side][...], preferred_element_type=F32)
+        for m in range(2):
+            here = pl.ds(half + (2 * side + m) * strip, strip)
+            both = got[:, m * width : (m + 1) * width] + local[here, :].astype(F32)
+            aligned[here, :] = both.astype(BF)
+
+    space = Rows(ch, width, jnp.logical_not(place.top), jnp.logical_not(place.bottom), rows)
     if last:
-
-        @pl.when(right_side == 0)
-        def _():
-            for n in range(3):
-                align(ch, local, recv, aligned, HALO, PARTS[n], choices[n])
-            align(ch, local, recv, aligned, HALO, PARTS[3], choices[3], 0)
-
-        @pl.when(right_side == 1)
-        def _():
-            offset = HALO - 2 * BS
-            align(ch, local, recv, aligned, offset, PARTS[2], choices[2], 1)
-            for n in range(3, 6):
-                align(ch, local, recv, aligned, offset, PARTS[n], choices[n])
-
-    else:
-        for n, rows_part in enumerate(PARTS):
-            align(ch, local, recv, aligned, HALO, rows_part, choices[n])
-        for n in range(2):
-            sent[n, pl.ds(halo_at, half), :] = next_edges[n]
-
-    top_ok = jnp.logical_not(place.top)
-    bottom_ok = jnp.logical_not(place.bottom)
-    if last:
-        top_ok = top_ok | (right_side == 1)
-        bottom_ok = bottom_ok | (right_side == 0)
-    space = Rows(ch, width, top_ok, bottom_ok, rows)
+        space.top_ok = space.top_ok | (place.side == 1)
+        space.bottom_ok = space.bottom_ok | left_side
     clear_outside(space, ch, rows, (act_a, act_b))
     join_mat = join[...]
-    for g in range((rows + 2 * HALO) // 4):
-        first = g * 4 - HALO
-        inp = over if first < 0 else under if first >= rows else xq[pl.ds(first * ch, 4 * ch), :]
-        al = aligned[pl.ds(g * 4 * ch, 4 * ch), :]
-        sides = []
-        for h in range(2):
-            a, b = 2 * h * ch, (2 * h + 1) * ch
-            sides.append(jnp.concatenate([al[a : a + ch], inp[a : a + ch], al[b : b + ch], inp[b : b + ch]], axis=0))
-        mixed = jnp.dot(join_mat, jnp.concatenate(sides, axis=1), preferred_element_type=F32).astype(BF)
-        for h in range(2):
-            for q in range(2):
-                row = first + 2 * h + q
-                value = mixed[q * ch : (q + 1) * ch, h * width : (h + 1) * width]
-                held[here_of(row, ch), :] = value
-                space.put(act_a, here_of(row, ch), value, row)
+    for first in range(-HALO, rows + HALO, 4):
+        inp, extra = xq, None
+        if first < 0:
+            inp, extra = over, over_sent
+        elif first >= rows:
+            inp, extra = under, under_sent
+        else:
+            inp = xq[pl.ds(first * ch, 4 * ch), :]
+        at = (first + HALO) * ch
+        if last:
+            at = pl.multiple_of(place.side * (2 * strip) + at, half)
+        al = aligned[pl.ds(at, half), :]
+        for n, value in enumerate(join_rows(ch, join_mat, al, inp, extra)):
+            held[here_of(first + n, ch), :] = value
+            space.put(act_a, here_of(first + n, ch), value, first + n)
 
     conv_layers(ch, conv, space, rows, act_a, act_b, held, fout)
     if not last:
-        pack_messages(ch, fout, par, sent, choices[-len(SENT) :], msg_e, msg_o)
+        pack_messages(ch, fout, par, join_mat, choices[2:], next_edges, sent, msg_e, msg_o)
     else:
         channels_first(fout, pl.multiple_of(core * strip, strip), own_out, tmp, ch)
         channels_first(fout, pl.multiple_of((core ^ 1) * strip, strip), part_out, tmp, ch)
@@ -713,6 +681,13 @@
         pl.when(core == n)(copy.wait)
 
 
+def parts_kernel(*refs):
+    out = refs[-1]
+    strip = refs[0].shape[0]
+    for n in range(out.shape[0] // strip):
+        out[pl.ds(n * strip, strip), :] = refs[n][...]
+
+
 def own_copies(strip, step, steps, own, out_f, out_g, sem):
     return [
         (0, pltpu.make_async_copy(own, out_f.at[pl.ds(step * strip, strip)], sem)),
@@ -727,14 +702,24 @@
     ]
 
 
-def finish_kernel(strip, steps, own, back, out_a, out_b, out_f, out_g, sems):
+def run_copies(copies):
     core = Place().core
-    copies = own_copies(strip, steps - 1, steps, own, out_f, out_g, sems.at[0])
-    copies += back_copies(strip, steps - 1, steps, back, out_f, out_g, sems.at[1])
     for n, copy in copies:
         pl.when(core == n)(copy.start)
     for n, copy in copies:
         pl.when(core == n)(copy.wait)
+
+
+def finish_own_kernel(strip, steps, own, backs, out_a, out_b, out_f, out_g, sems):
+    copies = own_copies(strip, steps - 1, steps, own, out_f, out_g, sems.at[0])
+    for step in range(steps - 1):
+        before = backs.at[pl.ds(step * strip, strip)]
+        copies += back_copies(strip, step, steps, before, out_f, out_g, sems.at[1 + step])
+    run_copies(copies)
+
+
+def finish_kernel(strip, steps, back, out_a, out_b, out_f, out_g, sem):
+    run_copies(back_copies(strip, steps - 1, steps, back, out_f, out_g, sem))
 
 
 def weights_kernel(conv, join, wide, join_both, join_first):
@@ -780,17 +765,17 @@
     )(*args)
 
 
-def sooner(value):
+def sooner(value, *after):
     return pl.pallas_call(
-        lambda given, out: None,
+        lambda *refs: None,
         out_shape=jax.ShapeDtypeStruct(value.shape, value.dtype),
-        in_specs=[ANY],
+        in_specs=[ANY] * (1 + len(after)),
         out_specs=ANY,
         input_output_aliases={0: 0},
         compiler_params=pltpu.CompilerParams(vmem_limit_bytes=1 << 20),
         cost_estimate=pl.CostEstimate(flops=0, bytes_accessed=2 << 20, transcendentals=0),
         name="sooner",
-    )(value)
+    )(value, *after)
 
 
 def pairings(count, idle):
@@ -838,7 +823,7 @@
     tmp = pltpu.VMEM((strip, width), F32)
     piece = (strip, width)
     rows = QUAD * BS
-    messages = [(5 * half // 2, width)] + [(7 * half // 2, width)] * (steps - 2)
+    message = (fold_rows(ch) + half, width)
     feature = (rows * ch, width)
     whole = (steps * strip, width)
     flat = frames.reshape(steps, strip, width)
@@ -904,11 +889,10 @@
         free=True,
     )
     received_near = send(pair_near, near(2))
-    halo_e, halo_o = along, cross
 
     wide_act = pltpu.VMEM((3, (rows + 16) * ch, width), BF)
     flops = 2 * (rows + 2 * HALO) * width * ch * ch * 9 * layers
-    near_shapes, part_shapes, sent_shapes = choice_shapes(width)
+    part_shapes, sent_shapes = choice_shapes(width)
     acts = [wide_act, wide_act, pltpu.VMEM(((rows + 16) * ch, width), BF)]
     inner, saved, saved_held = call(
         functools.partial(inner_kernel, ch),
@@ -921,15 +905,15 @@
     feat, msg_e, msg_o, pair_far = call(
         functools.partial(outer_kernel, ch, steps),
         "refine_outer",
-        (inner, saved, saved_held, along, cross, join_first, conv, codes, pair_far),
-        [feature, messages[0], messages[0], pair_far.shape],
-        [pltpu.VMEM((2, *messages[0]), BF)] + [pltpu.VMEM(shape, BF) for shape in sent_shapes],
+        (inner, saved, saved_held, along, cross, join_first, join_both, conv, codes, pair_far),
+        [feature, message, message, pair_far.shape],
+        [pltpu.VMEM((2, *message), BF)] + [pltpu.VMEM(shape, BF) for shape in sent_shapes],
         flops // 4,
-        in_any=(8,),
+        in_any=(9,),
         out_any=(3,),
-        aliases={8: 3},
+        aliases={9: 3},
     )
-    feat_e, feat_o = sooner(send(msg_e, even)), send(msg_o, odd)
+    feat_e, feat_o = send(msg_e, even), send(msg_o, odd)
     parts = []
     received_far = send(pair_far, near(2))
     outputs = call(lambda after, a, b: None, "results", (feat,), [whole, whole], in_any=(0,), out_any=(0, 1), free=True)
@@ -939,8 +923,8 @@
             functools.partial(choices_kernel, ch, step, steps),
             "choices",
             (codes, along, cross, feat),
-            [((rows + 2 * HALO) * ch, width)] + part_shapes + (sent_shapes if step + 1 < steps else []),
-            [pltpu.VMEM(shape, BF) for shape in near_shapes],
+            [((rows + 2 * HALO) * ch, width), piece, piece] + part_shapes + (sent_shapes if step + 1 < steps else []),
+            [tmp],
         )
 
     def frame_of(step):
@@ -953,35 +937,34 @@
         else:
             kernel = functools.partial(gather_kernel, ch, 2 * (step - 2) * strip, far_pairs + (step - 2) * half)
             args, outs = (pair_far, received_far, feat), [feature, (2, half, width)]
-        return call(kernel, "gather", args, outs + [piece, piece], [tmp])
+        return call(kernel, "gather", args, outs, [tmp], in_any=(2,))
 
     for step in range(1, steps):
         last = step == steps - 1
-        local, *choices = choices_of(step)
-        x_now, beside, own, part = frame_of(step)
+        local, own, part, *choices = choices_of(step)
+        x_now, beside = frame_of(step)
+        feat_e = sooner(feat_e, x_now) if step > 1 else sooner(feat_e)
         parts = parts + [part]
-        args = [x_now, halo_e, halo_o, join_both, conv, feat_e, feat_o, *choices, own, *outputs]
+        args = [x_now, along, cross, join_both, conv, feat_e, feat_o, *choices, own, *outputs]
         many = len(args)
-        outs = [] if last else [feature, messages[step], messages[step]]
+        outs = [] if last else [feature, message, message]
         outs += [piece, piece, whole, whole] if last else [whole, whole]
         in_any = [many - 3, many - 2, many - 1]
         out_any = [len(outs) - 2, len(outs) - 1]
         aliases = {many - 2: len(outs) - 2, many - 1: len(outs) - 1}
+        args += [local, beside]
+        scratch = [tmp, *acts, pltpu.SemaphoreType.DMA((1,))]
+        scratch += [pltpu.VMEM(((rows + 2 * HALO) * ch, width), BF), pltpu.VMEM((2, strip, width), BF)]
+        scratch += [pltpu.VMEM((2 * strip, width) if last else (2, *message), BF)]
         if last:
-            backs = [send(part, near(1)) for part in parts]
-            in_any += range(many, many + len(backs))
-            args += backs
-        elif step == steps - 2:
-            for part in parts:
-                aliases[len(args)] = len(outs)
-                in_any.append(len(args))
-                out_any.append(len(outs))
-                args.append(part)
-                outs.append(piece)
-        args += [local, beside]
-        scratch = [tmp, *acts, pltpu.SemaphoreType.DMA((steps,))]
-        scratch += [pltpu.VMEM(((rows + 2 * HALO) * ch, width), BF), pltpu.VMEM((2, 3 * half, width), BF)]
-        scratch += [pltpu.VMEM((2 * strip, width) if last else (2, *messages[step]), BF)]
+            (before,) = call(
+                parts_kernel,
+                "parts",
+                (*parts, feat_e, feat_o),
+                [(len(parts) * strip, width)],
+                in_any=(len(parts), len(parts) + 1),
+            )
+            backs = send(before, near(1))
         results = call(
             functools.partial(step_kernel, ch, step, steps),
             "refine",
@@ -995,23 +978,31 @@
         )
         if not last:
             feat, msg_e, msg_o, *results = results
-            halo_e, halo_o = feat_e, feat_o = sooner(send(msg_e, even)), send(msg_o, odd)
+            feat_e, feat_o = send(msg_e, even), send(msg_o, odd)
         if last:
             own, part, *results = results
-        out_f, out_g, *passed = results
-        outputs = out_f, out_g
-        parts = passed or parts
+        outputs = results
     back = send(part, near(1))
 
+    outputs = call(
+        functools.partial(finish_own_kernel, strip, steps),
+        "finish_own",
+        [own, backs, *outputs],
+        [whole] * 2,
+        [pltpu.SemaphoreType.DMA((steps,))],
+        in_any=(0, 1, 2, 3),
+        out_any=(0, 1),
+        aliases={2: 0, 3: 1},
+    )
     outputs = call(
         functools.partial(finish_kernel, strip, steps),
         "finish",
-        [own, back, *outputs],
+        [back, *outputs],
         [whole] * 2,
-        [pltpu.SemaphoreType.DMA((2,))],
-        in_any=(0, 1, 2, 3),
+        [pltpu.SemaphoreType.DMA],
+        in_any=(0, 1, 2),
         out_any=(0, 1),
-        aliases={2: 0, 3: 1},
+        aliases={1: 0, 2: 1},
     )
     return tuple(o.reshape(frames.shape) for o in outputs)
 

time: 51.9 us -> 50.6 us (0.975)
  waiting for transfers between devices: 12.7 us -> 11.8 us
    ppermute x17 -> x15, waiting for transfers between devices: 12.7 us -> 11.8 us  [send(): return lax.ppermute(value, 'tiles', pairs)]
    ppermute x17 -> x15, starting transfers between devices: 15 us -> 14.6 us  [send(): return lax.ppermute(value, 'tiles', pairs)]
    pallas_call x18 -> x20, Pallas kernels: 23.1 us -> 23 us  [call(): pl.pallas_call(kernel, out_shape=[jax.ShapeDtypeStruct(o, BF) for o in ou...]
  transfers between devices with their start and end apart: 17 -> 15, of which waited for: 7 -> 7; matrix products, arithmetic and copies ran while one was open for 0% -> 0% of each run, Pallas kernels for 28% -> 34%
where the time goes in v4:
time: 50.6 us; the launch traced here: 50.3 us
  Pallas kernels  23 us (45%)
  starting transfers between devices  14.6 us (29%)
  waiting for transfers between devices  11.8 us (23%)
  between operations  0.98 us (2%)
    pallas_call x20, Pallas kernels, call(): pl.pallas_call(kernel, out_shape=[jax.ShapeDtypeStruct(o, BF) for o in ou...  23 us
    ppermute x15, starting transfers between devices, send(): return lax.ppermute(value, 'tiles', pairs)  14.6 us
    ppermute x15, waiting for transfers between devices, send(): return lax.ppermute(value, 'tiles', pairs)  11.8 us
  transfers between devices with their start and end apart: 15, of which 7 were waited for; matrix products, arithmetic and copies ran while one was open for 0% of the time, Pallas kernels for 34%

profile of v4, /device:TPU:0, one launch (start us, length us, event | category | flops | bytes accessed | tf_op | source)
XLA Modules:
  0.0 50.3 jit_solution(8119403249774593784)
XLA Ops:
  0.7 1.4 %pack_first.1 = (bf16[528,128]{1,0:T(8,128)(2,1)S(1)}, bf16[256,128]{1,0:T(8,128)(2,1)S(1)}, bf16[784,128]{1,0:T(8,128)(2,1)S(1)}, bf16[1536,128]{1,0:T(8,128)(2,1)S(1)}) custom-call(bf16[4,512,128]{2,1,0:T(8,128)(2,1)} %bitcast.5, s32[3,16]{1,0:T(4,128)} %motion_f.1, s32[3,16]{1,0:T(4,128)} %motion_b.1), custom_call_target="tpu_custom_call" | custom-call | bytes 524672 | tf_op jit(solution)/shard_map/pack_first/pallas_call | solution.py:751
  2.6 1.1 %collective-permute-done.partner = bf16[784,128]{1,0:T(8,128)(2,1)S(1)} collective-permute-done((bf16[784,128]{1,0:T(8,128)(2,1)S(1)}, bf16[784,128]{1,0:T(8,128)(2,1)S(1)}, u32[]{:S(2)}, u32[]{:S(2)}) %collective-permute-start) | collective-permute-done | bytes 200736 | tf_op jit(solution)/shard_map/ppermute | solution.py:821
  4.3 2.6 %collective-permute-start.2 = (bf16[1056,128]{1,0:T(8,128)(2,1)S(1)}, bf16[1056,128]{1,0:T(8,128)(2,1)S(1)}, u32[]{:S(2)}, u32[]{:S(2)}) collective-permute-start(bf16[1056,128]{1,0:T(8,128)(2,1)S(1)} %get-tuple-element.83.pair), channel_id=1, source_target_pairs={{0,2},{1,3},{2,0},{3,1},{4,6},{5,7},{6,4},{7,5},{8,10},{9,11},{10,... | collective-permute-start | bytes 811016 | tf_op jit(solution)/shard_map/ppermute | solution.py:821
  6.9 1.3 %collective-permute-start.3 = (bf16[544,128]{1,0:T(8,128)(2,1)S(1)}, bf16[544,128]{1,0:T(8,128)(2,1)S(1)}, u32[]{:S(2)}, u32[]{:S(2)}) collective-permute-start(bf16[544,128]{1,0:T(8,128)(2,1)S(1)} %get-tuple-element.91), channel_id=1, source_target_pairs={{2,6},{3,7},{4,0},{5,1},{6,10},{7,11},{8,4},{9,5},{10,14},{11,15},... | collective-permute-start | bytes 417800 | tf_op jit(solution)/shard_map/ppermute | solution.py:821
  8.2 1.6 %pair_rest.1 = (bf16[1280,128]{1,0:T(8,128)(2,1)S(1)}, bf16[1536,128]{1,0:T(8,128)(2,1)S(1)}, bf16[1024,128]{1,0:T(8,128)(2,1)S(1)}, bf16[544,128]{1,0:T(8,128)(2,1)S(1)}) custom-call(bf16[4,512,128]{2,1,0:T(8,128)(2,1)} %bitcast.6, bf16[1536,128]{1,0:T(8,128)(2,1)S(1)} %collective-permute-done.1.swapped, ...), custom_call_target="tpu_custom_call", output_to_operand_aliasing={{3}: (2, {})} | custom-call | bytes 1056768 | tf_op jit(solution)/shard_map/pair_rest/pallas_call | solution.py:751
  10.2 3.7 %collective-permute-done.2.received = bf16[1056,128]{1,0:T(8,128)(2,1)S(1)} collective-permute-done((bf16[1056,128]{1,0:T(8,128)(2,1)S(1)}, bf16[1056,128]{1,0:T(8,128)(2,1)S(1)}, u32[]{:S(2)}, u32[]{:S(2)}) %collective-permute-start.2) | collective-permute-done | bytes 270368 | tf_op jit(solution)/shard_map/ppermute | solution.py:821
  14.1 1.8 %collective-permute-start.6 = (bf16[1280,128]{1,0:T(8,128)(2,1)S(1)}, bf16[1280,128]{1,0:T(8,128)(2,1)S(1)}, u32[]{:S(2)}, u32[]{:S(2)}) collective-permute-start(bf16[1280,128]{1,0:T(8,128)(2,1)S(1)} %get-tuple-element.97.pair), channel_id=1, source_target_pairs={{0,2},{1,3},{2,0},{3,1},{4,6},{5,7},{6,4},{7,5},{8,10},{9,11},{10,... | collective-permute-start | bytes 983048 | tf_op jit(solution)/shard_map/ppermute | solution.py:821
  15.9 2.3 %refine_inner.1 = (bf16[2048,128]{1,0:T(8,128)(2,1)S(1)}, bf16[4,2,3,128,128]{4,3,2,1,0:T(8,128)(2,1)S(1)}, bf16[4,2,64,128]{3,2,1,0:T(8,128)(2,1)S(1)}) custom-call(bf16[2048,128]{1,0:T(8,128)(2,1)S(1)} %get-tuple-element.86.xq, bf16[128,128]{1,0:T(8,128)(2,1)S(1)} %get-tuple-element.87.join.refs_5_, ...), custom_call_target="tpu_custom_call" | custom-call | tf_op jit(solution)/shard_map/refine_inner/pallas_call | solution.py:751
  18.3 2.4 %refine_outer.1 = (bf16[2048,128]{1,0:T(8,128)(2,1)S(1)}, bf16[640,128]{1,0:T(8,128)(2,1)S(1)}, bf16[640,128]{1,0:T(8,128)(2,1)S(1)}, bf16[1536,128]{1,0:T(8,128)(2,1)S(1)}) custom-call(bf16[2048,128]{1,0:T(8,128)(2,1)S(1)} %get-tuple-element.88.refs_0_, bf16[4,2,3,128,128]{4,3,2,1,0:T(8,128)(2,1)S(1)} %get-tuple-element.89.refs_1_, ...), custom_call_target="tpu_custom_call", output_to_operand_aliasing={{3}: (9, {})} | custom-call | flops 377487360 | bytes 3014656 | tf_op jit(solution)/shard_map/refine_outer/pallas_call | solution.py:751
  20.7 1.6 %collective-permute-start.7 = (bf16[640,128]{1,0:T(8,128)(2,1)S(1)}, bf16[640,128]{1,0:T(8,128)(2,1)S(1)}, u32[]{:S(2)}, u32[]{:S(2)}) collective-permute-start(bf16[640,128]{1,0:T(8,128)(2,1)S(1)} %get-tuple-element.100), channel_id=1, source_target_pairs={{0,4},{1,5},{2,6},{3,7},{4,0},{5,1},{6,2},{7,3},{8,12},{9,13},{10,... | collective-permute-start | bytes 491528 | tf_op jit(solution)/shard_map/ppermute | solution.py:821
  22.4 0.6 %collective-permute-start.5 = (bf16[1536,128]{1,0:T(8,128)(2,1)S(1)}, bf16[1536,128]{1,0:T(8,128)(2,1)S(1)}, u32[]{:S(2)}, u32[]{:S(2)}) collective-permute-start(bf16[1536,128]{1,0:T(8,128)(2,1)S(1)} %get-tuple-element.96.pair), channel_id=1, source_target_pairs={{0,2},{1,3},{2,0},{3,1},{4,6},{5,7},{6,4},{7,5},{8,10},{9,11},{10,... | collective-permute-start | bytes 1179656 | tf_op jit(solution)/shard_map/ppermute | solution.py:821
  23.0 1.0 %choices.3 = (bf16[2560,128]{1,0:T(8,128)(2,1)S(1)}, bf16[512,128]{1,0:T(8,128)(2,1)S(1)}, bf16[512,128]{1,0:T(8,128)(2,1)S(1)}, bf16[128,256]{1,0:T(8,128)(2,1)...) custom-call(bf16[64,128]{1,0:T(8,128)(2,1)S(1)} %get-tuple-element.9, ...), custom_call_target="tpu_custom_call" | custom-call | bytes 819200 | tf_op jit(solution)/shard_map/choices/pallas_call | solution.py:751
  24.0 2.2 %collective-permute-done.7.refs_0_ = bf16[640,128]{1,0:T(8,128)(2,1)S(1)} collective-permute-done((bf16[640,128]{1,0:T(8,128)(2,1)S(1)}, bf16[640,128]{1,0:T(8,128)(2,1)S(1)}, u32[]{:S(2)}, u32[]{:S(2)}) %collective-permute-start.7) | collective-permute-done | bytes 163872 | tf_op jit(solution)/shard_map/ppermute | solution.py:821
  26.4 3.7 %refine.3 = (bf16[2048,128]{1,0:T(8,128)(2,1)S(1)}, bf16[640,128]{1,0:T(8,128)(2,1)S(1)}, bf16[640,128]{1,0:T(8,128)(2,1)S(1)}, bf16[2048,128]{1,0:T(8,128)(2,1)}, bf16[2048,128]{1,0:T(8,128)(2,1)}) custom-call(bf16[2048,128]{1,0:T(8,128)(2,1)S(1)} %get-tuple-element.99.refs_0_, ...), custom_call_target="tpu_custom_call", output_to_operand_aliasing={{3}: (14, {}), {4}: (15, {})} | custom-call | flops 1509949440 | bytes 4407296 | tf_op jit(solution)/shard_map/refine/pallas_call | solution.py:751
  30.1 2.5 %collective-permute-start.9 = (bf16[640,128]{1,0:T(8,128)(2,1)S(1)}, bf16[640,128]{1,0:T(8,128)(2,1)S(1)}, u32[]{:S(2)}, u32[]{:S(2)}) collective-permute-start(bf16[640,128]{1,0:T(8,128)(2,1)S(1)} %get-tuple-element.115), channel_id=1, source_target_pairs={{0,4},{1,5},{2,6},{3,7},{4,0},{5,1},{6,2},{7,3},{8,12},{9,13},{10,... | collective-permute-start | bytes 491528 | tf_op jit(solution)/shard_map/ppermute | solution.py:821
  32.6 0.9 %choices.4 = (bf16[2560,128]{1,0:T(8,128)(2,1)S(1)}, bf16[512,128]{1,0:T(8,128)(2,1)S(1)}, bf16[512,128]{1,0:T(8,128)(2,1)S(1)}, bf16[128,256]{1,0:T(8,128)(2,1)...) custom-call(bf16[64,128]{1,0:T(8,128)(2,1)S(1)} %get-tuple-element.9, ...), custom_call_target="tpu_custom_call" | custom-call | bytes 819200 | tf_op jit(solution)/shard_map/choices/pallas_call | solution.py:751
  34.1 1.7 %collective-permute-done.9.refs_0_ = bf16[640,128]{1,0:T(8,128)(2,1)S(1)} collective-permute-done((bf16[640,128]{1,0:T(8,128)(2,1)S(1)}, bf16[640,128]{1,0:T(8,128)(2,1)S(1)}, u32[]{:S(2)}, u32[]{:S(2)}) %collective-permute-start.9) | collective-permute-done | bytes 163872 | tf_op jit(solution)/shard_map/ppermute | solution.py:821
  35.9 3.8 %refine.4 = (bf16[2048,128]{1,0:T(8,128)(2,1)S(1)}, bf16[640,128]{1,0:T(8,128)(2,1)S(1)}, bf16[640,128]{1,0:T(8,128)(2,1)S(1)}, bf16[2048,128]{1,0:T(8,128)(2,1)}, bf16[2048,128]{1,0:T(8,128)(2,1)}) custom-call(bf16[2048,128]{1,0:T(8,128)(2,1)S(1)} %get-tuple-element.114.refs_1_.refs_0_, ...), custom_call_target="tpu_custom_call", output_to_operand_aliasing={{3}: (14, {}), {4}: (15, {})} | custom-call | flops 1509949440 | bytes 4407296 | tf_op jit(solution)/shard_map/refine/pallas_call | solution.py:751
  39.7 2.3 %collective-permute-start.11 = (bf16[640,128]{1,0:T(8,128)(2,1)S(1)}, bf16[640,128]{1,0:T(8,128)(2,1)S(1)}, u32[]{:S(2)}, u32[]{:S(2)}) collective-permute-start(bf16[640,128]{1,0:T(8,128)(2,1)S(1)} %get-tuple-element.130), channel_id=1, source_target_pairs={{0,4},{1,5},{2,6},{3,7},{4,0},{5,1},{6,2},{7,3},{8,12},{9,13},{10,... | collective-permute-start | bytes 491528 | tf_op jit(solution)/shard_map/ppermute | solution.py:821
  42.0 0.7 %choices.5 = (bf16[2560,128]{1,0:T(8,128)(2,1)S(1)}, bf16[512,128]{1,0:T(8,128)(2,1)S(1)}, bf16[512,128]{1,0:T(8,128)(2,1)S(1)}, bf16[128,256]{1,0:T(8,128)(2,1)S(1)}, bf16[128,256]{1,0:T(8,128)(2,1)S(1)}) custom-call(bf16[64,128]{1,0:T(8,128)(2,1)S(1)} %get-tuple-element.94.refs_8_.codes, bf16[544,128]{1,0:T(8,128)(2,1)S(1)} %collective-permute-done.3.refs_3_.along.refs_1_, ...), custom_call_target="tpu_custom_call" | custom-call | bytes 819200 | tf_op jit(solution)/shard_map/choices/pallas_call | solution.py:751
  42.8 2.5 %collective-permute-done.11.refs_0_ = bf16[640,128]{1,0:T(8,128)(2,1)S(1)} collective-permute-done((bf16[640,128]{1,0:T(8,128)(2,1)S(1)}, bf16[640,128]{1,0:T(8,128)(2,1)S(1)}, u32[]{:S(2)}, u32[]{:S(2)}) %collective-permute-start.11) | collective-permute-done | bytes 163872 | tf_op jit(solution)/shard_map/ppermute | solution.py:821
  45.5 2.5 %refine.5 = (bf16[512,128]{1,0:T(8,128)(2,1)S(1)}, bf16[512,128]{1,0:T(8,128)(2,1)S(1)}, bf16[2048,128]{1,0:T(8,128)(2,1)}, bf16[2048,128]{1,0:T(8,128)(2,1)}) custom-call(bf16[1024,128]{1,0:T(8,128)(2,1)S(1)} %get-tuple-element.129.refs_1_.refs_0_, ...), custom_call_target="tpu_custom_call", output_to_operand_aliasing={{2}: (10, {}), {3}: (11, {})} | custom-call | flops 1509949440 | bytes 3751936 | tf_op jit(solution)/shard_map/refine/pallas_call | solution.py:751
  48.5 0.8 %finish_own.1 = (bf16[2048,128]{1,0:T(8,128)(2,1)}, bf16[2048,128]{1,0:T(8,128)(2,1)}) custom-call(bf16[512,128]{1,0:T(8,128)(2,1)S(1)} %get-tuple-element.140.own, bf16[1536,128]{1,0:T(8,128)(2,1)S(1)} %collective-permute-done.14.backs, bf16[2048,128]{1,0:T(8,128)(2,1)} %get-tuple-element.144.out_a, ...), custom_call_target="tpu_custom_call", output_to_operand_aliasing={{0}: (2, {}), {1}: (3, {})} | custom-call | bytes 1572864 | tf_op jit(solution)/shard_map/finish_own/pallas_call | solution.py:751
  49.5 0.7 %finish.1 = (bf16[2048,128]{1,0:T(8,128)(2,1)}, bf16[2048,128]{1,0:T(8,128)(2,1)}) custom-call(bf16[512,128]{1,0:T(8,128)(2,1)S(1)} %collective-permute-done.13.back, bf16[2048,128]{1,0:T(8,128)(2,1)} %get-tuple-element.146.out_a, bf16[2048,128]{1,0:T(8,128)(2,1)} %get-tuple-element.147.out_b), custom_call_target="tpu_custom_call", output_to_operand_aliasing={{0}: (1, {}), {1}: (2, {})} | custom-call | bytes 1179648 | tf_op jit(solution)/shard_map/finish/pallas_call | solution.py:751
  (33 shorter events, 3.5 us)
Async XLA Ops:
  0.6 9.3 %copy-start = (bf16[2,4,9,64,64]{4,3,2,1,0:T(8,128)(2,1)S(1)}, bf16[2,4,9,64,64]{4,3,2,1,0:T(8,128)(2,1)}, u32[]{:S(2)}) copy-start(bf16[2,4,9,64,64]{4,3,2,1,0:T(8,128)(2,1)} %conv.1) | copy-start | bytes 1769476
  0.6 9.3 %copy-start.1 = (bf16[2,64,128]{2,1,0:T(8,128)(2,1)S(1)}, bf16[2,64,128]{2,1,0:T(8,128)(2,1)}, u32[]{:S(2)}) copy-start(bf16[2,64,128]{2,1,0:T(8,128)(2,1)} %join.1) | copy-start | bytes 98308
  2.1 1.6 %collective-permute-start = (bf16[784,128]{1,0:T(8,128)(2,1)S(1)}, bf16[784,128]{1,0:T(8,128)(2,1)S(1)}, u32[]{:S(2)}, u32[]{:S(2)}) collective-permute-start(bf16[784,128]{1,0:T(8,128)(2,1)S(1)} %get-tuple-element.78), channel_id=1, source_target_pairs={{0,1},{1,0},{2,3},{3,2},{4,5},{5,4},{6,7},{7,6},{8,9},{9,8},{10,11... | collective-permute-start | bytes 602120 | tf_op jit(solution)/shard_map/ppermute | solution.py:821
  3.8 4.4 %collective-permute-start.1 = (bf16[1536,128]{1,0:T(8,128)(2,1)S(1)}, bf16[1536,128]{1,0:T(8,128)(2,1)S(1)}, u32[]{:S(2)}, u32[]{:S(2)}) collective-permute-start(bf16[1536,128]{1,0:T(8,128)(2,1)S(1)} %get-tuple-element.80), channel_id=1, source_target_pairs={{0,1},{1,0},{2,3},{3,2},{4,5},{5,4},{6,7},{7,6},{8,9},{9,8},{10,11... | collective-permute-start | bytes 1179656 | tf_op jit(solution)/shard_map/ppermute | solution.py:821
  4.3 9.6 %collective-permute-start.2 = (bf16[1056,128]{1,0:T(8,128)(2,1)S(1)}, bf16[1056,128]{1,0:T(8,128)(2,1)S(1)}, u32[]{:S(2)}, u32[]{:S(2)}) collective-permute-start(bf16[1056,128]{1,0:T(8,128)(2,1)S(1)} %get-tuple-element.83.pair), channel_id=1, source_target_pairs={{0,2},{1,3},{2,0},{3,1},{4,6},{5,7},{6,4},{7,5},{8,10},{9,11},{10,... | collective-permute-start | bytes 811016 | tf_op jit(solution)/shard_map/ppermute | solution.py:821
  6.9 11.4 %collective-permute-start.3 = (bf16[544,128]{1,0:T(8,128)(2,1)S(1)}, bf16[544,128]{1,0:T(8,128)(2,1)S(1)}, u32[]{:S(2)}, u32[]{:S(2)}) collective-permute-start(bf16[544,128]{1,0:T(8,128)(2,1)S(1)} %get-tuple-element.91), channel_id=1, source_target_pairs={{2,6},{3,7},{4,0},{5,1},{6,10},{7,11},{8,4},{9,5},{10,14},{11,15},... | collective-permute-start | bytes 417800 | tf_op jit(solution)/shard_map/ppermute | solution.py:821
  9.8 8.5 %collective-permute-start.4 = (bf16[544,128]{1,0:T(8,128)(2,1)S(1)}, bf16[544,128]{1,0:T(8,128)(2,1)S(1)}, u32[]{:S(2)}, u32[]{:S(2)}) collective-permute-start(bf16[544,128]{1,0:T(8,128)(2,1)S(1)} %get-tuple-element.92), channel_id=1, source_target_pairs={{0,1},{1,0},{2,4},{3,5},{4,2},{5,3},{6,8},{7,9},{8,6},{9,7},{10,12... | collective-permute-start | bytes 417800 | tf_op jit(solution)/shard_map/ppermute | solution.py:821
  14.1 12.0 %collective-permute-start.6 = (bf16[1280,128]{1,0:T(8,128)(2,1)S(1)}, bf16[1280,128]{1,0:T(8,128)(2,1)S(1)}, u32[]{:S(2)}, u32[]{:S(2)}) collective-permute-start(bf16[1280,128]{1,0:T(8,128)(2,1)S(1)} %get-tuple-element.97.pair), channel_id=1, source_target_pairs={{0,2},{1,3},{2,0},{3,1},{4,6},{5,7},{6,4},{7,5},{8,10},{9,11},{10,... | collective-permute-start | bytes 983048 | tf_op jit(solution)/shard_map/ppermute | solution.py:821
  20.7 5.5 %collective-permute-start.7 = (bf16[640,128]{1,0:T(8,128)(2,1)S(1)}, bf16[640,128]{1,0:T(8,128)(2,1)S(1)}, u32[]{:S(2)}, u32[]{:S(2)}) collective-permute-start(bf16[640,128]{1,0:T(8,128)(2,1)S(1)} %get-tuple-element.100), channel_id=1, source_target_pairs={{0,4},{1,5},{2,6},{3,7},{4,0},{5,1},{6,2},{7,3},{8,12},{9,13},{10,... | collective-permute-start | bytes 491528 | tf_op jit(solution)/shard_map/ppermute | solution.py:821
  22.4 4.1 %collective-permute-start.8 = (bf16[640,128]{1,0:T(8,128)(2,1)S(1)}, bf16[640,128]{1,0:T(8,128)(2,1)S(1)}, u32[]{:S(2)}, u32[]{:S(2)}) collective-permute-start(bf16[640,128]{1,0:T(8,128)(2,1)S(1)} %get-tuple-element.101), channel_id=1, source_target_pairs={{0,1},{1,0},{2,3},{3,2},{4,8},{5,9},{6,10},{7,11},{8,4},{9,5},{10,... | collective-permute-start | bytes 491528 | tf_op jit(solution)/shard_map/ppermute | solution.py:821
  22.4 11.5 %collective-permute-start.5 = (bf16[1536,128]{1,0:T(8,128)(2,1)S(1)}, bf16[1536,128]{1,0:T(8,128)(2,1)S(1)}, u32[]{:S(2)}, u32[]{:S(2)}) collective-permute-start(bf16[1536,128]{1,0:T(8,128)(2,1)S(1)} %get-tuple-element.96.pair), channel_id=1, source_target_pairs={{0,2},{1,3},{2,0},{3,1},{4,6},{5,7},{6,4},{7,5},{8,10},{9,11},{10,... | collective-permute-start | bytes 1179656 | tf_op jit(solution)/shard_map/ppermute | solution.py:821
  30.1 5.8 %collective-permute-start.9 = (bf16[640,128]{1,0:T(8,128)(2,1)S(1)}, bf16[640,128]{1,0:T(8,128)(2,1)S(1)}, u32[]{:S(2)}, u32[]{:S(2)}) collective-permute-start(bf16[640,128]{1,0:T(8,128)(2,1)S(1)} %get-tuple-element.115), channel_id=1, source_target_pairs={{0,4},{1,5},{2,6},{3,7},{4,0},{5,1},{6,2},{7,3},{8,12},{9,13},{10,... | collective-permute-start | bytes 491528 | tf_op jit(solution)/shard_map/ppermute | solution.py:821
  32.6 3.3 %collective-permute-start.10 = (bf16[640,128]{1,0:T(8,128)(2,1)S(1)}, bf16[640,128]{1,0:T(8,128)(2,1)S(1)}, u32[]{:S(2)}, u32[]{:S(2)}) collective-permute-start(bf16[640,128]{1,0:T(8,128)(2,1)S(1)} %get-tuple-element.116), channel_id=1, source_target_pairs={{0,1},{1,0},{2,3},{3,2},{4,8},{5,9},{6,10},{7,11},{8,4},{9,5},{10,... | collective-permute-start | bytes 491528 | tf_op jit(solution)/shard_map/ppermute | solution.py:821
  39.7 5.6 %collective-permute-start.11 = (bf16[640,128]{1,0:T(8,128)(2,1)S(1)}, bf16[640,128]{1,0:T(8,128)(2,1)S(1)}, u32[]{:S(2)}, u32[]{:S(2)}) collective-permute-start(bf16[640,128]{1,0:T(8,128)(2,1)S(1)} %get-tuple-element.130), channel_id=1, source_target_pairs={{0,4},{1,5},{2,6},{3,7},{4,0},{5,1},{6,2},{7,3},{8,12},{9,13},{10,... | collective-permute-start | bytes 491528 | tf_op jit(solution)/shard_map/ppermute | solution.py:821
  42.0 3.3 %collective-permute-start.12 = (bf16[640,128]{1,0:T(8,128)(2,1)S(1)}, bf16[640,128]{1,0:T(8,128)(2,1)S(1)}, u32[]{:S(2)}, u32[]{:S(2)}) collective-permute-start(bf16[640,128]{1,0:T(8,128)(2,1)S(1)} %get-tuple-element.131), channel_id=1, source_target_pairs={{0,1},{1,0},{2,3},{3,2},{4,8},{5,9},{6,10},{7,11},{8,4},{9,5},{10,... | collective-permute-start | bytes 491528 | tf_op jit(solution)/shard_map/ppermute | solution.py:821
  45.4 3.2 %collective-permute-start.14 = (bf16[1536,128]{1,0:T(8,128)(2,1)S(1)}, bf16[1536,128]{1,0:T(8,128)(2,1)S(1)}, u32[]{:S(2)}, u32[]{:S(2)}) collective-permute-start(bf16[1536,128]{1,0:T(8,128)(2,1)S(1)} %parts.1), channel_id=1, source_target_pairs={{0,1},{1,0},{2,3},{3,2},{4,5},{5,4},{6,7},{7,6},{8,9},{9,8},{10,11... | collective-permute-start | bytes 1179656 | tf_op jit(solution)/shard_map/ppermute | solution.py:821
  48.0 1.5 %collective-permute-start.13 = (bf16[512,128]{1,0:T(8,128)(2,1)S(1)}, bf16[512,128]{1,0:T(8,128)(2,1)S(1)}, u32[]{:S(2)}, u32[]{:S(2)}) collective-permute-start(bf16[512,128]{1,0:T(8,128)(2,1)S(1)} %get-tuple-element.139), channel_id=1, source_target_pairs={{0,1},{1,0},{2,3},{3,2},{4,5},{5,4},{6,7},{7,6},{8,9},{9,8},{10,11... | collective-permute-start | bytes 393224 | tf_op jit(solution)/shard_map/ppermute | solution.py:821

commit v5 on v4

--- a/solution.py
+++ b/solution.py
@@ -105,7 +105,7 @@
         out[pl.ds(start + r * ch, ch), :] = jnp.where(top, one, two).astype(BF)
 
 
-def pair_first_kernel(ch, crow, mine, mine_edge, partner, rest_in, out, edge, edge_too, rest_out, tmp):
+def pair_first_kernel(ch, crow, mine, mine_edge, partner, rest_in, out, edge, rest_out, tmp):
     place = Place()
     strip = BS * ch
     half = HALO * ch
@@ -119,7 +119,6 @@
         out[pl.ds(pl.multiple_of(at * strip, strip), strip), :] = piece[pl.ds(0, strip), :]
         for ref, start in ((out, 2 * strip), (edge, 2 * half)):
             ref[pl.ds(pl.multiple_of(start + at * crow, crow), crow), :] = piece[pl.ds(strip, crow), :]
-    edge_too[...] = edge[...]
 
 
 def above_below(place, along, cross):
@@ -157,7 +156,7 @@
         edge_of(jnp.logical_not(left), ch, jnp.where(left, two, one), out, start, tmp)
 
 
-def pair_kernel(ch, frames, swapped, edge_in, near_out, far_out, last_out, edge_out, tmp, sems):
+def pair_kernel(ch, frames, swapped, near_out, far_out, last_out, tmp, sems):
     place = Place()
     steps, strip = frames.shape[:2]
     half = HALO * ch
@@ -508,81 +507,23 @@
         source, target = target, source
 
 
-def inner_kernel(ch, xq, join, conv, feat, saved, saved_held, act_a, act_b, held):
-    rows = QUAD * BS
-    layers = conv.shape[0]
-    space = Rows(ch, xq.shape[1], True, True, rows)
-    for buf in (act_a, act_b):
-        for row in (-1, rows):
-            for n in range(3):
-                buf[n, here_of(row, ch), :] = space.zero
-    join_mat = join[...]
-    for first in range(0, rows, 4):
-        for n, value in enumerate(join_first_rows(ch, join_mat, xq[pl.ds(first * ch, 4 * ch), :])):
-            held[here_of(first + n, ch), :] = value
-            space.put(act_a, here_of(first + n, ch), value, first + n)
-    source, target = act_a, act_b
-    for layer in range(layers):
-        for side, row, both in ((0, layer, layer), (1, rows - 1 - layer, rows - 2 - layer)):
-            for n in range(3):
-                saved[layer, side, n] = source[n, here_of(both, ch, 2), :]
-            saved_held[layer, side] = held[here_of(row, ch), :]
-        edge = (layer + 1) // 2 * 2
-
-        def emit(row, value, layer=layer, target=target):
-            if layer < layers - 1:
-                held[here_of(row, ch), :] = value
-                space.put(target, here_of(row, ch), value, row)
-            else:
-                feat[pl.ds(row * ch, ch), :] = value
-
-        conv_layer(ch, conv[layer], source, held, edge, rows - edge, emit)
-        source, target = target, source
-
-
-def outer_kernel(ch, steps, *refs):
-    feat_in, saved, saved_held, along, cross, join, join_both, conv, codes, far_in, *refs = refs
-    fout, msg_e, msg_o, far_out, sent, *choices = refs
+def first_kernel(ch, steps, *refs):
+    xq, along, cross, join, join_both, conv, codes, far_in, *refs = refs
+    fout, msg_e, msg_o, far_out, act_a, act_b, held, sent, *choices = refs
     half = HALO * ch
     rows = QUAD * BS
     place = Place()
-    layers = conv.shape[0]
-    width = feat_in.shape[1]
-    space = Rows(ch, width, jnp.logical_not(place.top), jnp.logical_not(place.bottom), rows)
+    space = Rows(ch, xq.shape[1], jnp.logical_not(place.top), jnp.logical_not(place.bottom), rows)
     send_choices(code_of_next(ch, place, 0, steps, codes, along, cross), choices)
-    fout[pl.ds(half, (rows - 2 * HALO) * ch), :] = feat_in[pl.ds(half, (rows - 2 * HALO) * ch), :]
-    halos = above_below(place, along[pl.ds(0, half), :], cross[pl.ds(0, half), :])
+    above, below = above_below(place, along[pl.ds(0, half), :], cross[pl.ds(0, half), :])
+    clear_outside(space, ch, rows, (act_a, act_b))
     join_mat = join[...]
-    values = [join_first_rows(ch, join_mat, halo) for halo in halos]
-    starts = [-HALO, rows]
-    for layer in range(layers):
-        weight = conv[layer]
-        for side in range(2):
-            acts = [space.active(value, starts[side] + n) for n, value in enumerate(values[side])]
-            kept = [
-                tuple(saved[layer, side, n, pl.ds(m * ch, ch), :] for n in range(3)) for m in range(2)
-            ]
-            beside = saved_held[layer, side]
-            if side == 0:
-                window, base = acts + kept, values[side][1:] + [beside]
-                starts[side] += 1
-            else:
-                window, base = kept + acts, [beside] + values[side][:3]
-                starts[side] -= 1
-            halves = [
-                jnp.concatenate([window[2 * h + m][n] for n in range(3) for m in range(4)], axis=0) for h in range(2)
-            ]
-            out = jnp.dot(weight, jnp.concatenate(halves, axis=1), preferred_element_type=F32)
-            values[side] = [
-                (
-                    base[2 * h + q].astype(F32) + out[q * ch : (q + 1) * ch, h * width : (h + 1) * width]
-                ).astype(BF)
-                for h in range(2)
-                for q in range(2)
-            ]
-    for side in range(2):
-        for n, value in enumerate(values[side]):
-            fout[pl.ds((starts[side] + n) * ch, ch), :] = value
+    for first in range(-HALO, rows + HALO, 4):
+        inp = above if first < 0 else below if first >= rows else xq[pl.ds(first * ch, 4 * ch), :]
+        for n, value in enumerate(join_first_rows(ch, join_mat, inp)):
+            held[here_of(first + n, ch), :] = value
+            space.put(act_a, here_of(first + n, ch), value, first + n)
+    conv_layers(ch, conv, space, rows, act_a, act_b, held, fout)
     pack_messages(ch, fout, place.odd, join_both[...], choices, None, sent, msg_e, msg_o)
 
 
@@ -843,32 +784,29 @@
         in_hbm=(0, 1, 2),
         out_any=(3,),
     )
-    pair, edge, edge_too, rest = call(
+    pair, edge, rest = call(
         functools.partial(pair_first_kernel, ch, crow),
         "pair_first",
         (mine, mine_edge, send(other, near(1)), rest),
-        [(2 * (strip + crow), width), (2 * (half + crow), width), (2 * (half + crow), width), later],
+        [(2 * (strip + crow), width), (2 * (half + crow), width), later],
         [tmp],
         in_any=(3,),
-        out_any=(3,),
-        aliases={3: 3},
+        out_any=(2,),
+        aliases={3: 2},
     )
     received = send(pair, near(2))
     swapped = send(rest, near(1))
-    along = send(edge, along_pairs)
+    along, cross = sooner(send(edge, along_pairs)), send(edge, cross_pairs)
     far_pairs = 2 * (steps - 3) * strip
-    pair_near, pair_far, pair_last, edge_too = call(
+    pair_near, pair_far, pair_last = call(
         functools.partial(pair_kernel, ch),
         "pair_rest",
-        (flat, swapped, edge_too),
-        [(2 * strip + half, width), (far_pairs + (steps - 2) * half, width), (2 * strip, width), edge.shape],
+        (flat, swapped),
+        [(2 * strip + half, width), (far_pairs + (steps - 2) * half, width), (2 * strip, width)],
         [tmp, pltpu.SemaphoreType.DMA((2 * steps,))],
         in_hbm=(0,),
-        in_any=(1, 2),
-        out_any=(3,),
-        aliases={2: 3},
+        in_any=(1,),
     )
-    cross = send(edge_too, cross_pairs)
     layers = conv_weight.shape[1]
     conv, join_both, join_first = call(
         weights_kernel,
@@ -894,24 +832,16 @@
     flops = 2 * (rows + 2 * HALO) * width * ch * ch * 9 * layers
     part_shapes, sent_shapes = choice_shapes(width)
     acts = [wide_act, wide_act, pltpu.VMEM(((rows + 16) * ch, width), BF)]
-    inner, saved, saved_held = call(
-        functools.partial(inner_kernel, ch),
-        "refine_inner",
-        (xq, join_first, conv),
-        [feature, (layers, 2, 3, 2 * ch, width), (layers, 2, ch, width)],
-        acts,
-        free=True,
-    )
     feat, msg_e, msg_o, pair_far = call(
-        functools.partial(outer_kernel, ch, steps),
-        "refine_outer",
-        (inner, saved, saved_held, along, cross, join_first, join_both, conv, codes, pair_far),
+        functools.partial(first_kernel, ch, steps),
+        "refine_first",
+        (xq, along, cross, join_first, join_both, conv, codes, pair_far),
         [feature, message, message, pair_far.shape],
-        [pltpu.VMEM((2, *message), BF)] + [pltpu.VMEM(shape, BF) for shape in sent_shapes],
-        flops // 4,
-        in_any=(9,),
+        [*acts, pltpu.VMEM((2, *message), BF)] + [pltpu.VMEM(shape, BF) for shape in sent_shapes],
+        flops,
+        in_any=(7,),
         out_any=(3,),
-        aliases={9: 3},
+        aliases={7: 3},
     )
     feat_e, feat_o = send(msg_e, even), send(msg_o, odd)
     parts = []

time: 50.6 us -> 50.5 us (level)
  starting transfers between devices: 14.6 us -> 17.2 us
  Pallas kernels: 23 us -> 21.5 us
  waiting for transfers between devices: 11.8 us -> 10.6 us
    ppermute x15, starting transfers between devices: 14.6 us -> 17.2 us  [send(): return lax.ppermute(value, 'tiles', pairs)]
    pallas_call x20 -> x19, Pallas kernels: 23 us -> 21.5 us  [call(): pl.pallas_call(kernel, out_shape=[jax.ShapeDtypeStruct(o, BF) for o in ou...]
    ppermute x15, waiting for transfers between devices: 11.8 us -> 10.6 us  [send(): return lax.ppermute(value, 'tiles', pairs)]
  transfers between devices with their start and end apart: 15 -> 15, of which waited for: 7 -> 7; matrix products, arithmetic and copies ran while one was open for 0% -> 0% of each run, Pallas kernels for 34% -> 31%
where the time goes in v5:
time: 50.5 us; the launch traced here: 50.3 us
  Pallas kernels  21.5 us (43%)
  starting transfers between devices  17.2 us (34%)
  waiting for transfers between devices  10.6 us (21%)
  between operations  0.95 us (2%)
    pallas_call x19, Pallas kernels, call(): pl.pallas_call(kernel, out_shape=[jax.ShapeDtypeStruct(o, BF) for o in ou...  21.5 us
    ppermute x15, starting transfers between devices, send(): return lax.ppermute(value, 'tiles', pairs)  17.2 us
    ppermute x15, waiting for transfers between devices, send(): return lax.ppermute(value, 'tiles', pairs)  10.6 us
  transfers between devices with their start and end apart: 15, of which 7 were waited for; matrix products, arithmetic and copies ran while one was open for 0% of the time, Pallas kernels for 31%

profile of v5, /device:TPU:0, one launch (start us, length us, event | category | flops | bytes accessed | tf_op | source)
XLA Modules:
  0.0 50.3 jit_solution(7038646956150047502)
XLA Ops:
  0.7 1.4 %pack_first.1 = (bf16[528,128]{1,0:T(8,128)(2,1)S(1)}, bf16[256,128]{1,0:T(8,128)(2,1)S(1)}, bf16[784,128]{1,0:T(8,128)(2,1)S(1)}, bf16[1536,128]{1,0:T(8,128)(2,1)S(1)}) custom-call(bf16[4,512,128]{2,1,0:T(8,128)(2,1)} %bitcast.5, s32[3,16]{1,0:T(4,128)} %motion_f.1, s32[3,16]{1,0:T(4,128)} %motion_b.1), custom_call_target="tpu_custom_call" | custom-call | bytes 524672 | tf_op jit(solution)/shard_map/pack_first/pallas_call | solution.py:692
  2.6 1.1 %collective-permute-done.partner = bf16[784,128]{1,0:T(8,128)(2,1)S(1)} collective-permute-done((bf16[784,128]{1,0:T(8,128)(2,1)S(1)}, bf16[784,128]{1,0:T(8,128)(2,1)S(1)}, u32[]{:S(2)}, u32[]{:S(2)}) %collective-permute-start) | collective-permute-done | bytes 200736 | tf_op jit(solution)/shard_map/ppermute | solution.py:762
  4.2 2.6 %collective-permute-start.2 = (bf16[1056,128]{1,0:T(8,128)(2,1)S(1)}, bf16[1056,128]{1,0:T(8,128)(2,1)S(1)}, u32[]{:S(2)}, u32[]{:S(2)}) collective-permute-start(bf16[1056,128]{1,0:T(8,128)(2,1)S(1)} %get-tuple-element.77.pair), channel_id=1, source_target_pairs={{0,2},{1,3},{2,0},{3,1},{4,6},{5,7},{6,4},{7,5},{8,10},{9,11},{10,... | collective-permute-start | bytes 811016 | tf_op jit(solution)/shard_map/ppermute | solution.py:762
  6.9 1.3 %collective-permute-start.3 = (bf16[544,128]{1,0:T(8,128)(2,1)S(1)}, bf16[544,128]{1,0:T(8,128)(2,1)S(1)}, u32[]{:S(2)}, u32[]{:S(2)}) collective-permute-start(bf16[544,128]{1,0:T(8,128)(2,1)S(1)} %get-tuple-element.81), channel_id=1, source_target_pairs={{2,6},{3,7},{4,0},{5,1},{6,10},{7,11},{8,4},{9,5},{10,14},{11,15},... | collective-permute-start | bytes 417800 | tf_op jit(solution)/shard_map/ppermute | solution.py:762
  8.6 1.6 %pair_rest.1 = (bf16[1280,128]{1,0:T(8,128)(2,1)S(1)}, bf16[1536,128]{1,0:T(8,128)(2,1)S(1)}, bf16[1024,128]{1,0:T(8,128)(2,1)S(1)}) custom-call(bf16[4,512,128]{2,1,0:T(8,128)(2,1)} %bitcast.6, bf16[1536,128]{1,0:T(8,128)(2,1)S(1)} %collective-permute-done.1.swapped), custom_call_target="tpu_custom_call" | custom-call | bytes 917504 | tf_op jit(solution)/shard_map/pair_rest/pallas_call | solution.py:692
  10.2 3.7 %collective-permute-done.2.received = bf16[1056,128]{1,0:T(8,128)(2,1)S(1)} collective-permute-done((bf16[1056,128]{1,0:T(8,128)(2,1)S(1)}, bf16[1056,128]{1,0:T(8,128)(2,1)S(1)}, u32[]{:S(2)}, u32[]{:S(2)}) %collective-permute-start.2) | collective-permute-done | bytes 270368 | tf_op jit(solution)/shard_map/ppermute | solution.py:762
  14.1 2.4 %collective-permute-start.6 = (bf16[1280,128]{1,0:T(8,128)(2,1)S(1)}, bf16[1280,128]{1,0:T(8,128)(2,1)S(1)}, u32[]{:S(2)}, u32[]{:S(2)}) collective-permute-start(bf16[1280,128]{1,0:T(8,128)(2,1)S(1)} %get-tuple-element.87.pair), channel_id=1, source_target_pairs={{0,2},{1,3},{2,0},{3,1},{4,6},{5,7},{6,4},{7,5},{8,10},{9,11},{10,... | collective-permute-start | bytes 983048 | tf_op jit(solution)/shard_map/ppermute | solution.py:762
  16.6 3.3 %refine_first.1 = (bf16[2048,128]{1,0:T(8,128)(2,1)S(1)}, bf16[640,128]{1,0:T(8,128)(2,1)S(1)}, bf16[640,128]{1,0:T(8,128)(2,1)S(1)}, bf16[1536,128]{1,0:T(8,128)(2,1)S(1)}) custom-call(bf16[2048,128]{1,0:T(8,128)(2,1)S(1)} %get-tuple-element.80.refs_0_, bf16[544,128]{1,0:T(8,128)(2,1)S(1)} %sooner.4.refs_1_.along, ...), custom_call_target="tpu_custom_call", output_to_operand_aliasing={{3}: (7, {})} | custom-call | flops 1509949440 | bytes 2097152 | tf_op jit(solution)/shard_map/refine_first/pallas_call | solution.py:692
  19.9 2.5 %collective-permute-start.7 = (bf16[640,128]{1,0:T(8,128)(2,1)S(1)}, bf16[640,128]{1,0:T(8,128)(2,1)S(1)}, u32[]{:S(2)}, u32[]{:S(2)}) collective-permute-start(bf16[640,128]{1,0:T(8,128)(2,1)S(1)} %get-tuple-element.90), channel_id=1, source_target_pairs={{0,4},{1,5},{2,6},{3,7},{4,0},{5,1},{6,2},{7,3},{8,12},{9,13},{10,... | collective-permute-start | bytes 491528 | tf_op jit(solution)/shard_map/ppermute | solution.py:762
  22.4 1.5 %collective-permute-start.5 = (bf16[1536,128]{1,0:T(8,128)(2,1)S(1)}, bf16[1536,128]{1,0:T(8,128)(2,1)S(1)}, u32[]{:S(2)}, u32[]{:S(2)}) collective-permute-start(bf16[1536,128]{1,0:T(8,128)(2,1)S(1)} %get-tuple-element.86.pair), channel_id=1, source_target_pairs={{0,2},{1,3},{2,0},{3,1},{4,6},{5,7},{6,4},{7,5},{8,10},{9,11},{10,... | collective-permute-start | bytes 1179656 | tf_op jit(solution)/shard_map/ppermute | solution.py:762
  23.9 1.0 %choices.3 = (bf16[2560,128]{1,0:T(8,128)(2,1)S(1)}, bf16[512,128]{1,0:T(8,128)(2,1)S(1)}, bf16[512,128]{1,0:T(8,128)(2,1)S(1)}, bf16[128,256]{1,0:T(8,128)(2,1)...) custom-call(bf16[64,128]{1,0:T(8,128)(2,1)S(1)} %get-tuple-element.8, ...), custom_call_target="tpu_custom_call" | custom-call | bytes 819200 | tf_op jit(solution)/shard_map/choices/pallas_call | solution.py:692
  24.8 1.1 %collective-permute-done.7.refs_0_ = bf16[640,128]{1,0:T(8,128)(2,1)S(1)} collective-permute-done((bf16[640,128]{1,0:T(8,128)(2,1)S(1)}, bf16[640,128]{1,0:T(8,128)(2,1)S(1)}, u32[]{:S(2)}, u32[]{:S(2)}) %collective-permute-start.7) | collective-permute-done | bytes 163872 | tf_op jit(solution)/shard_map/ppermute | solution.py:762
  26.2 3.7 %refine.3 = (bf16[2048,128]{1,0:T(8,128)(2,1)S(1)}, bf16[640,128]{1,0:T(8,128)(2,1)S(1)}, bf16[640,128]{1,0:T(8,128)(2,1)S(1)}, bf16[2048,128]{1,0:T(8,128)(2,1)}, bf16[2048,128]{1,0:T(8,128)(2,1)}) custom-call(bf16[2048,128]{1,0:T(8,128)(2,1)S(1)} %get-tuple-element.89.refs_0_, ...), custom_call_target="tpu_custom_call", output_to_operand_aliasing={{3}: (14, {}), {4}: (15, {})} | custom-call | flops 1509949440 | bytes 4407296 | tf_op jit(solution)/shard_map/refine/pallas_call | solution.py:692
  29.8 2.7 %collective-permute-start.9 = (bf16[640,128]{1,0:T(8,128)(2,1)S(1)}, bf16[640,128]{1,0:T(8,128)(2,1)S(1)}, u32[]{:S(2)}, u32[]{:S(2)}) collective-permute-start(bf16[640,128]{1,0:T(8,128)(2,1)S(1)} %get-tuple-element.105), channel_id=1, source_target_pairs={{0,4},{1,5},{2,6},{3,7},{4,0},{5,1},{6,2},{7,3},{8,12},{9,13},{10,... | collective-permute-start | bytes 491528 | tf_op jit(solution)/shard_map/ppermute | solution.py:762
  32.6 1.0 %choices.4 = (bf16[2560,128]{1,0:T(8,128)(2,1)S(1)}, bf16[512,128]{1,0:T(8,128)(2,1)S(1)}, bf16[512,128]{1,0:T(8,128)(2,1)S(1)}, bf16[128,256]{1,0:T(8,128)(2,1)...) custom-call(bf16[64,128]{1,0:T(8,128)(2,1)S(1)} %get-tuple-element.8, ...), custom_call_target="tpu_custom_call" | custom-call | bytes 819200 | tf_op jit(solution)/shard_map/choices/pallas_call | solution.py:692
  34.2 1.7 %collective-permute-done.9.refs_0_ = bf16[640,128]{1,0:T(8,128)(2,1)S(1)} collective-permute-done((bf16[640,128]{1,0:T(8,128)(2,1)S(1)}, bf16[640,128]{1,0:T(8,128)(2,1)S(1)}, u32[]{:S(2)}, u32[]{:S(2)}) %collective-permute-start.9) | collective-permute-done | bytes 163872 | tf_op jit(solution)/shard_map/ppermute | solution.py:762
  35.9 3.8 %refine.4 = (bf16[2048,128]{1,0:T(8,128)(2,1)S(1)}, bf16[640,128]{1,0:T(8,128)(2,1)S(1)}, bf16[640,128]{1,0:T(8,128)(2,1)S(1)}, bf16[2048,128]{1,0:T(8,128)(2,1)}, bf16[2048,128]{1,0:T(8,128)(2,1)}) custom-call(bf16[2048,128]{1,0:T(8,128)(2,1)S(1)} %get-tuple-element.104.refs_1_.refs_0_, ...), custom_call_target="tpu_custom_call", output_to_operand_aliasing={{3}: (14, {}), {4}: (15, {})} | custom-call | flops 1509949440 | bytes 4407296 | tf_op jit(solution)/shard_map/refine/pallas_call | solution.py:692
  39.6 2.4 %collective-permute-start.11 = (bf16[640,128]{1,0:T(8,128)(2,1)S(1)}, bf16[640,128]{1,0:T(8,128)(2,1)S(1)}, u32[]{:S(2)}, u32[]{:S(2)}) collective-permute-start(bf16[640,128]{1,0:T(8,128)(2,1)S(1)} %get-tuple-element.120), channel_id=1, source_target_pairs={{0,4},{1,5},{2,6},{3,7},{4,0},{5,1},{6,2},{7,3},{8,12},{9,13},{10,... | collective-permute-start | bytes 491528 | tf_op jit(solution)/shard_map/ppermute | solution.py:762
  42.0 0.7 %choices.5 = (bf16[2560,128]{1,0:T(8,128)(2,1)S(1)}, bf16[512,128]{1,0:T(8,128)(2,1)S(1)}, bf16[512,128]{1,0:T(8,128)(2,1)S(1)}, bf16[128,256]{1,0:T(8,128)(2,1)S(1)}, bf16[128,256]{1,0:T(8,128)(2,1)S(1)}) custom-call(bf16[64,128]{1,0:T(8,128)(2,1)S(1)} %get-tuple-element.84.refs_6_.codes, bf16[544,128]{1,0:T(8,128)(2,1)S(1)} %sooner.4.refs_1_.along, ...), custom_call_target="tpu_custom_call" | custom-call | bytes 819200 | tf_op jit(solution)/shard_map/choices/pallas_call | solution.py:692
  42.8 2.5 %collective-permute-done.11.refs_0_ = bf16[640,128]{1,0:T(8,128)(2,1)S(1)} collective-permute-done((bf16[640,128]{1,0:T(8,128)(2,1)S(1)}, bf16[640,128]{1,0:T(8,128)(2,1)S(1)}, u32[]{:S(2)}, u32[]{:S(2)}) %collective-permute-start.11) | collective-permute-done | bytes 163872 | tf_op jit(solution)/shard_map/ppermute | solution.py:762
  45.4 2.5 %refine.5 = (bf16[512,128]{1,0:T(8,128)(2,1)S(1)}, bf16[512,128]{1,0:T(8,128)(2,1)S(1)}, bf16[2048,128]{1,0:T(8,128)(2,1)}, bf16[2048,128]{1,0:T(8,128)(2,1)}) custom-call(bf16[1024,128]{1,0:T(8,128)(2,1)S(1)} %get-tuple-element.119.refs_1_.refs_0_, bf16[544,128]{1,0:T(8,128)(2,1)S(1)} %sooner.4.refs_1_.along, ...), custom_call_target="tpu_custom_call", output_to_operand_aliasing={{2}: (10, {}), {3}: (11, {})} | custom-call | flops 1509949440 | bytes 3751936 | tf_op jit(solution)/shard_map/refine/pallas_call | solution.py:692
  47.9 0.6 %collective-permute-start.13 = (bf16[512,128]{1,0:T(8,128)(2,1)S(1)}, bf16[512,128]{1,0:T(8,128)(2,1)S(1)}, u32[]{:S(2)}, u32[]{:S(2)}) collective-permute-start(bf16[512,128]{1,0:T(8,128)(2,1)S(1)} %get-tuple-element.129), channel_id=1, source_target_pairs={{0,1},{1,0},{2,3},{3,2},{4,5},{5,4},{6,7},{7,6},{8,9},{9,8},{10,11... | collective-permute-start | bytes 393224 | tf_op jit(solution)/shard_map/ppermute | solution.py:762
  48.5 0.8 %finish_own.1 = (bf16[2048,128]{1,0:T(8,128)(2,1)}, bf16[2048,128]{1,0:T(8,128)(2,1)}) custom-call(bf16[512,128]{1,0:T(8,128)(2,1)S(1)} %get-tuple-element.130.own, bf16[1536,128]{1,0:T(8,128)(2,1)S(1)} %collective-permute-done.14.backs, bf16[2048,128]{1,0:T(8,128)(2,1)} %get-tuple-element.134.out_a, ...), custom_call_target="tpu_custom_call", output_to_operand_aliasing={{0}: (2, {}), {1}: (3, {})} | custom-call | bytes 1572864 | tf_op jit(solution)/shard_map/finish_own/pallas_call | solution.py:692
  49.5 0.7 %finish.1 = (bf16[2048,128]{1,0:T(8,128)(2,1)}, bf16[2048,128]{1,0:T(8,128)(2,1)}) custom-call(bf16[512,128]{1,0:T(8,128)(2,1)S(1)} %collective-permute-done.13.back, bf16[2048,128]{1,0:T(8,128)(2,1)} %get-tuple-element.136.out_a, bf16[2048,128]{1,0:T(8,128)(2,1)} %get-tuple-element.137.out_b), custom_call_target="tpu_custom_call", output_to_operand_aliasing={{0}: (1, {}), {1}: (2, {})} | custom-call | bytes 1179648 | tf_op jit(solution)/shard_map/finish/pallas_call | solution.py:692
  (33 shorter events, 3.0 us)
Async XLA Ops:
  0.6 7.7 %copy-start.1 = (bf16[2,64,128]{2,1,0:T(8,128)(2,1)S(1)}, bf16[2,64,128]{2,1,0:T(8,128)(2,1)}, u32[]{:S(2)}) copy-start(bf16[2,64,128]{2,1,0:T(8,128)(2,1)} %join.1) | copy-start | bytes 98308
  0.6 7.7 %copy-start = (bf16[2,4,9,64,64]{4,3,2,1,0:T(8,128)(2,1)S(1)}, bf16[2,4,9,64,64]{4,3,2,1,0:T(8,128)(2,1)}, u32[]{:S(2)}) copy-start(bf16[2,4,9,64,64]{4,3,2,1,0:T(8,128)(2,1)} %conv.1) | copy-start | bytes 1769476
  2.1 1.6 %collective-permute-start = (bf16[784,128]{1,0:T(8,128)(2,1)S(1)}, bf16[784,128]{1,0:T(8,128)(2,1)S(1)}, u32[]{:S(2)}, u32[]{:S(2)}) collective-permute-start(bf16[784,128]{1,0:T(8,128)(2,1)S(1)} %get-tuple-element.73), channel_id=1, source_target_pairs={{0,1},{1,0},{2,3},{3,2},{4,5},{5,4},{6,7},{7,6},{8,9},{9,8},{10,11... | collective-permute-start | bytes 602120 | tf_op jit(solution)/shard_map/ppermute | solution.py:762
  3.8 4.7 %collective-permute-start.1 = (bf16[1536,128]{1,0:T(8,128)(2,1)S(1)}, bf16[1536,128]{1,0:T(8,128)(2,1)S(1)}, u32[]{:S(2)}, u32[]{:S(2)}) collective-permute-start(bf16[1536,128]{1,0:T(8,128)(2,1)S(1)} %get-tuple-element.75), channel_id=1, source_target_pairs={{0,1},{1,0},{2,3},{3,2},{4,5},{5,4},{6,7},{7,6},{8,9},{9,8},{10,11... | collective-permute-start | bytes 1179656 | tf_op jit(solution)/shard_map/ppermute | solution.py:762
  4.2 9.6 %collective-permute-start.2 = (bf16[1056,128]{1,0:T(8,128)(2,1)S(1)}, bf16[1056,128]{1,0:T(8,128)(2,1)S(1)}, u32[]{:S(2)}, u32[]{:S(2)}) collective-permute-start(bf16[1056,128]{1,0:T(8,128)(2,1)S(1)} %get-tuple-element.77.pair), channel_id=1, source_target_pairs={{0,2},{1,3},{2,0},{3,1},{4,6},{5,7},{6,4},{7,5},{8,10},{9,11},{10,... | collective-permute-start | bytes 811016 | tf_op jit(solution)/shard_map/ppermute | solution.py:762
  6.9 9.7 %collective-permute-start.3 = (bf16[544,128]{1,0:T(8,128)(2,1)S(1)}, bf16[544,128]{1,0:T(8,128)(2,1)S(1)}, u32[]{:S(2)}, u32[]{:S(2)}) collective-permute-start(bf16[544,128]{1,0:T(8,128)(2,1)S(1)} %get-tuple-element.81), channel_id=1, source_target_pairs={{2,6},{3,7},{4,0},{5,1},{6,10},{7,11},{8,4},{9,5},{10,14},{11,15},... | collective-permute-start | bytes 417800 | tf_op jit(solution)/shard_map/ppermute | solution.py:762
  8.2 8.4 %collective-permute-start.4 = (bf16[544,128]{1,0:T(8,128)(2,1)S(1)}, bf16[544,128]{1,0:T(8,128)(2,1)S(1)}, u32[]{:S(2)}, u32[]{:S(2)}) collective-permute-start(bf16[544,128]{1,0:T(8,128)(2,1)S(1)} %get-tuple-element.81), channel_id=1, source_target_pairs={{0,1},{1,0},{2,4},{3,5},{4,2},{5,3},{6,8},{7,9},{8,6},{9,7},{10,12... | collective-permute-start | bytes 417800 | tf_op jit(solution)/shard_map/ppermute | solution.py:762
  14.1 11.8 %collective-permute-start.6 = (bf16[1280,128]{1,0:T(8,128)(2,1)S(1)}, bf16[1280,128]{1,0:T(8,128)(2,1)S(1)}, u32[]{:S(2)}, u32[]{:S(2)}) collective-permute-start(bf16[1280,128]{1,0:T(8,128)(2,1)S(1)} %get-tuple-element.87.pair), channel_id=1, source_target_pairs={{0,2},{1,3},{2,0},{3,1},{4,6},{5,7},{6,4},{7,5},{8,10},{9,11},{10,... | collective-permute-start | bytes 983048 | tf_op jit(solution)/shard_map/ppermute | solution.py:762
  19.9 6.1 %collective-permute-start.7 = (bf16[640,128]{1,0:T(8,128)(2,1)S(1)}, bf16[640,128]{1,0:T(8,128)(2,1)S(1)}, u32[]{:S(2)}, u32[]{:S(2)}) collective-permute-start(bf16[640,128]{1,0:T(8,128)(2,1)S(1)} %get-tuple-element.90), channel_id=1, source_target_pairs={{0,4},{1,5},{2,6},{3,7},{4,0},{5,1},{6,2},{7,3},{8,12},{9,13},{10,... | collective-permute-start | bytes 491528 | tf_op jit(solution)/shard_map/ppermute | solution.py:762
  22.4 3.8 %collective-permute-start.8 = (bf16[640,128]{1,0:T(8,128)(2,1)S(1)}, bf16[640,128]{1,0:T(8,128)(2,1)S(1)}, u32[]{:S(2)}, u32[]{:S(2)}) collective-permute-start(bf16[640,128]{1,0:T(8,128)(2,1)S(1)} %get-tuple-element.91), channel_id=1, source_target_pairs={{0,1},{1,0},{2,3},{3,2},{4,8},{5,9},{6,10},{7,11},{8,4},{9,5},{10,... | collective-permute-start | bytes 491528 | tf_op jit(solution)/shard_map/ppermute | solution.py:762
  22.4 11.5 %collective-permute-start.5 = (bf16[1536,128]{1,0:T(8,128)(2,1)S(1)}, bf16[1536,128]{1,0:T(8,128)(2,1)S(1)}, u32[]{:S(2)}, u32[]{:S(2)}) collective-permute-start(bf16[1536,128]{1,0:T(8,128)(2,1)S(1)} %get-tuple-element.86.pair), channel_id=1, source_target_pairs={{0,2},{1,3},{2,0},{3,1},{4,6},{5,7},{6,4},{7,5},{8,10},{9,11},{10,... | collective-permute-start | bytes 1179656 | tf_op jit(solution)/shard_map/ppermute | solution.py:762
  29.8 6.0 %collective-permute-start.9 = (bf16[640,128]{1,0:T(8,128)(2,1)S(1)}, bf16[640,128]{1,0:T(8,128)(2,1)S(1)}, u32[]{:S(2)}, u32[]{:S(2)}) collective-permute-start(bf16[640,128]{1,0:T(8,128)(2,1)S(1)} %get-tuple-element.105), channel_id=1, source_target_pairs={{0,4},{1,5},{2,6},{3,7},{4,0},{5,1},{6,2},{7,3},{8,12},{9,13},{10,... | collective-permute-start | bytes 491528 | tf_op jit(solution)/shard_map/ppermute | solution.py:762
  32.6 3.3 %collective-permute-start.10 = (bf16[640,128]{1,0:T(8,128)(2,1)S(1)}, bf16[640,128]{1,0:T(8,128)(2,1)S(1)}, u32[]{:S(2)}, u32[]{:S(2)}) collective-permute-start(bf16[640,128]{1,0:T(8,128)(2,1)S(1)} %get-tuple-element.106), channel_id=1, source_target_pairs={{0,1},{1,0},{2,3},{3,2},{4,8},{5,9},{6,10},{7,11},{8,4},{9,5},{10,... | collective-permute-start | bytes 491528 | tf_op jit(solution)/shard_map/ppermute | solution.py:762
  39.6 5.7 %collective-permute-start.11 = (bf16[640,128]{1,0:T(8,128)(2,1)S(1)}, bf16[640,128]{1,0:T(8,128)(2,1)S(1)}, u32[]{:S(2)}, u32[]{:S(2)}) collective-permute-start(bf16[640,128]{1,0:T(8,128)(2,1)S(1)} %get-tuple-element.120), channel_id=1, source_target_pairs={{0,4},{1,5},{2,6},{3,7},{4,0},{5,1},{6,2},{7,3},{8,12},{9,13},{10,... | collective-permute-start | bytes 491528 | tf_op jit(solution)/shard_map/ppermute | solution.py:762
  42.0 3.3 %collective-permute-start.12 = (bf16[640,128]{1,0:T(8,128)(2,1)S(1)}, bf16[640,128]{1,0:T(8,128)(2,1)S(1)}, u32[]{:S(2)}, u32[]{:S(2)}) collective-permute-start(bf16[640,128]{1,0:T(8,128)(2,1)S(1)} %get-tuple-element.121), channel_id=1, source_target_pairs={{0,1},{1,0},{2,3},{3,2},{4,8},{5,9},{6,10},{7,11},{8,4},{9,5},{10,... | collective-permute-start | bytes 491528 | tf_op jit(solution)/shard_map/ppermute | solution.py:762
  45.3 3.2 %collective-permute-start.14 = (bf16[1536,128]{1,0:T(8,128)(2,1)S(1)}, bf16[1536,128]{1,0:T(8,128)(2,1)S(1)}, u32[]{:S(2)}, u32[]{:S(2)}) collective-permute-start(bf16[1536,128]{1,0:T(8,128)(2,1)S(1)} %parts.1), channel_id=1, source_target_pairs={{0,1},{1,0},{2,3},{3,2},{4,5},{5,4},{6,7},{7,6},{8,9},{9,8},{10,11... | collective-permute-start | bytes 1179656 | tf_op jit(solution)/shard_map/ppermute | solution.py:762
  47.9 1.5 %collective-permute-start.13 = (bf16[512,128]{1,0:T(8,128)(2,1)S(1)}, bf16[512,128]{1,0:T(8,128)(2,1)S(1)}, u32[]{:S(2)}, u32[]{:S(2)}) collective-permute-start(bf16[512,128]{1,0:T(8,128)(2,1)S(1)} %get-tuple-element.129), channel_id=1, source_target_pairs={{0,1},{1,0},{2,3},{3,2},{4,5},{5,4},{6,7},{7,6},{8,9},{9,8},{10,11... | collective-permute-start | bytes 393224 | tf_op jit(solution)/shard_map/ppermute | solution.py:762

commit v6 on v5

--- a/solution.py
+++ b/solution.py
@@ -47,7 +47,7 @@
     dst[...] = tmp[...].astype(BF)
 
 
-def pack_first_kernel(ch, crow, frames, motion_f, motion_b, mine, mine_edge, other, rest, following, motion_buf, tmp, sems):
+def pack_first_kernel(ch, crow, frames, motion_f, motion_b, mine, mine_edge, other, following, motion_buf, tmp, sems):
     place = Place()
     steps, strip = frames.shape[:2]
     half = HALO * ch
@@ -61,11 +61,7 @@
         back = 1 - core if n else core
         copies.append(frame_copy(frames, 0, back, outs[n].at[pl.ds(0, strip)], sems.at[n]))
         copies.append(frame_copy(frames, 1, back, following.at[n], sems.at[2 + n]))
-    later = [
-        frame_copy(frames, step, 1 - core, rest.at[pl.ds((step - 1) * strip, strip)], sems.at[5 + step])
-        for step in range(1, steps)
-    ]
-    for copy in lists + copies + later:
+    for copy in lists + copies:
         copy.start()
     for copy in lists:
         copy.wait()
@@ -94,8 +90,6 @@
         copy.wait()
     for n, (out, start) in enumerate(((mine_edge, 0), (other, strip + crow))):
         edge_of(place.side == 0, ch, following[n], out, start, tmp)
-    for copy in later:
-        copy.wait()
 
 
 def edge_of(top, ch, strip_values, out, start, tmp):
@@ -125,6 +119,19 @@
     left = place.side == 0
     along, cross = along.astype(F32), cross.astype(F32)
     return jnp.where(left, cross, along).astype(BF), jnp.where(left, along, cross).astype(BF)
+
+
+def pack_rest_kernel(frames, after, rest, sems):
+    steps, strip = frames.shape[:2]
+    core = Place().core
+    copies = [
+        frame_copy(frames, step, 1 - core, rest.at[pl.ds((step - 1) * strip, strip)], sems.at[step])
+        for step in range(1, steps)
+    ]
+    for copy in copies:
+        copy.start()
+    for copy in copies:
+        copy.wait()
 
 
 def frame_copy(frames, step, back, out, sem):
@@ -770,19 +777,28 @@
     flat = frames.reshape(steps, strip, width)
     later = ((steps - 1) * strip, width)
     first = (strip + crow, width)
-    mine, mine_edge, other, rest = call(
+    mine, mine_edge, other = call(
         functools.partial(pack_first_kernel, ch, crow),
         "pack_first",
         (flat, motion_forward, motion_backward),
-        [first, (half, width), (strip + crow + half, width), later],
+        [first, (half, width), (strip + crow + half, width)],
         [
             pltpu.VMEM((2, *piece), BF),
             pltpu.VMEM((2, *motion_forward.shape), jnp.int32),
             tmp,
-            pltpu.SemaphoreType.DMA((5 + steps,)),
+            pltpu.SemaphoreType.DMA((6,)),
         ],
         in_hbm=(0, 1, 2),
-        out_any=(3,),
+    )
+    (rest,) = call(
+        pack_rest_kernel,
+        "pack_rest",
+        (flat, mine),
+        [later],
+        [pltpu.SemaphoreType.DMA((steps,))],
+        in_hbm=(0,),
+        in_any=(1,),
+        out_any=(0,),
     )
     pair, edge, rest = call(
         functools.partial(pair_first_kernel, ch, crow),

time: 50.5 us -> 50.5 us (level)
  waiting for transfers between devices: 10.6 us -> 9.55 us
  Pallas kernels: 21.5 us -> 22.5 us
    ppermute x15, waiting for transfers between devices: 10.6 us -> 9.55 us  [send(): return lax.ppermute(value, 'tiles', pairs)]
    pallas_call x19 -> x20, Pallas kernels: 21.5 us -> 22.5 us  [call(): pl.pallas_call(kernel, out_shape=[jax.ShapeDtypeStruct(o, BF) for o in ou...]
  transfers between devices with their start and end apart: 15 -> 15, of which waited for: 7 -> 6; matrix products, arithmetic and copies ran while one was open for 0% -> 0% of each run, Pallas kernels for 31% -> 33%
where the time goes in v6:
time: 50.5 us; the launch traced here: 50.2 us
  Pallas kernels  22.5 us (45%)
  starting transfers between devices  17.2 us (34%)
  waiting for transfers between devices  9.55 us (19%)
  between operations  0.97 us (2%)
    pallas_call x20, Pallas kernels, call(): pl.pallas_call(kernel, out_shape=[jax.ShapeDtypeStruct(o, BF) for o in ou...  22.5 us
    ppermute x15, starting transfers between devices, send(): return lax.ppermute(value, 'tiles', pairs)  17.2 us
    ppermute x15, waiting for transfers between devices, send(): return lax.ppermute(value, 'tiles', pairs)  9.55 us
  transfers between devices with their start and end apart: 15, of which 6 were waited for; matrix products, arithmetic and copies ran while one was open for 0% of the time, Pallas kernels for 33%

profile of v6, /device:TPU:0, one launch (start us, length us, event | category | flops | bytes accessed | tf_op | source)
XLA Modules:
  0.0 50.2 jit_solution(11408057327749279725)
XLA Ops:
  0.7 1.4 %pack_first.1 = (bf16[528,128]{1,0:T(8,128)(2,1)S(1)}, bf16[256,128]{1,0:T(8,128)(2,1)S(1)}, bf16[784,128]{1,0:T(8,128)(2,1)S(1)}) custom-call(bf16[4,512,128]{2,1,0:T(8,128)(2,1)} %bitcast.3, s32[3,16]{1,0:T(4,128)} %motion_f.1, s32[3,16]{1,0:T(4,128)} %motion_b.1), custom_call_target="tpu_custom_call" | custom-call | bytes 524672 | tf_op jit(solution)/shard_map/pack_first/pallas_call | solution.py:699
  2.6 1.1 %pack_rest.1.rest_in = bf16[1536,128]{1,0:T(8,128)(2,1)S(1)} custom-call(bf16[4,512,128]{2,1,0:T(8,128)(2,1)} %bitcast.4, bf16[528,128]{1,0:T(8,128)(2,1)S(1)} %get-tuple-element.70.after.mine), custom_call_target="tpu_custom_call" | custom-call | bytes 659456 | tf_op jit(solution)/shard_map/pack_rest/pallas_call | solution.py:699
  4.2 2.6 %collective-permute-start.2 = (bf16[1056,128]{1,0:T(8,128)(2,1)S(1)}, bf16[1056,128]{1,0:T(8,128)(2,1)S(1)}, u32[]{:S(2)}, u32[]{:S(2)}) collective-permute-start(bf16[1056,128]{1,0:T(8,128)(2,1)S(1)} %get-tuple-element.75.pair), channel_id=1, source_target_pairs={{0,2},{1,3},{2,0},{3,1},{4,6},{5,7},{6,4},{7,5},{8,10},{9,11},{10,... | collective-permute-start | bytes 811016 | tf_op jit(solution)/shard_map/ppermute | solution.py:769
  6.8 1.3 %collective-permute-start.3 = (bf16[544,128]{1,0:T(8,128)(2,1)S(1)}, bf16[544,128]{1,0:T(8,128)(2,1)S(1)}, u32[]{:S(2)}, u32[]{:S(2)}) collective-permute-start(bf16[544,128]{1,0:T(8,128)(2,1)S(1)} %get-tuple-element.79), channel_id=1, source_target_pairs={{2,6},{3,7},{4,0},{5,1},{6,10},{7,11},{8,4},{9,5},{10,14},{11,15},... | collective-permute-start | bytes 417800 | tf_op jit(solution)/shard_map/ppermute | solution.py:769
  8.5 1.6 %pair_rest.1 = (bf16[1280,128]{1,0:T(8,128)(2,1)S(1)}, bf16[1536,128]{1,0:T(8,128)(2,1)S(1)}, bf16[1024,128]{1,0:T(8,128)(2,1)S(1)}) custom-call(bf16[4,512,128]{2,1,0:T(8,128)(2,1)} %bitcast.5, bf16[1536,128]{1,0:T(8,128)(2,1)S(1)} %collective-permute-done.1.swapped), custom_call_target="tpu_custom_call" | custom-call | bytes 917504 | tf_op jit(solution)/shard_map/pair_rest/pallas_call | solution.py:699
  10.1 3.7 %collective-permute-done.2.received = bf16[1056,128]{1,0:T(8,128)(2,1)S(1)} collective-permute-done((bf16[1056,128]{1,0:T(8,128)(2,1)S(1)}, bf16[1056,128]{1,0:T(8,128)(2,1)S(1)}, u32[]{:S(2)}, u32[]{:S(2)}) %collective-permute-start.2) | collective-permute-done | bytes 270368 | tf_op jit(solution)/shard_map/ppermute | solution.py:769
  14.1 2.4 %collective-permute-start.6 = (bf16[1280,128]{1,0:T(8,128)(2,1)S(1)}, bf16[1280,128]{1,0:T(8,128)(2,1)S(1)}, u32[]{:S(2)}, u32[]{:S(2)}) collective-permute-start(bf16[1280,128]{1,0:T(8,128)(2,1)S(1)} %get-tuple-element.85.pair), channel_id=1, source_target_pairs={{0,2},{1,3},{2,0},{3,1},{4,6},{5,7},{6,4},{7,5},{8,10},{9,11},{10,... | collective-permute-start | bytes 983048 | tf_op jit(solution)/shard_map/ppermute | solution.py:769
  16.5 3.3 %refine_first.1 = (bf16[2048,128]{1,0:T(8,128)(2,1)S(1)}, bf16[640,128]{1,0:T(8,128)(2,1)S(1)}, bf16[640,128]{1,0:T(8,128)(2,1)S(1)}, bf16[1536,128]{1,0:T(8,128)(2,1)S(1)}) custom-call(bf16[2048,128]{1,0:T(8,128)(2,1)S(1)} %get-tuple-element.78.refs_0_, bf16[544,128]{1,0:T(8,128)(2,1)S(1)} %sooner.4.refs_1_.along, ...), custom_call_target="tpu_custom_call", output_to_operand_aliasing={{3}: (7, {})} | custom-call | flops 1509949440 | bytes 2097152 | tf_op jit(solution)/shard_map/refine_first/pallas_call | solution.py:699
  19.8 2.5 %collective-permute-start.7 = (bf16[640,128]{1,0:T(8,128)(2,1)S(1)}, bf16[640,128]{1,0:T(8,128)(2,1)S(1)}, u32[]{:S(2)}, u32[]{:S(2)}) collective-permute-start(bf16[640,128]{1,0:T(8,128)(2,1)S(1)} %get-tuple-element.88), channel_id=1, source_target_pairs={{0,4},{1,5},{2,6},{3,7},{4,0},{5,1},{6,2},{7,3},{8,12},{9,13},{10,... | collective-permute-start | bytes 491528 | tf_op jit(solution)/shard_map/ppermute | solution.py:769
  22.3 1.5 %collective-permute-start.5 = (bf16[1536,128]{1,0:T(8,128)(2,1)S(1)}, bf16[1536,128]{1,0:T(8,128)(2,1)S(1)}, u32[]{:S(2)}, u32[]{:S(2)}) collective-permute-start(bf16[1536,128]{1,0:T(8,128)(2,1)S(1)} %get-tuple-element.84.pair), channel_id=1, source_target_pairs={{0,2},{1,3},{2,0},{3,1},{4,6},{5,7},{6,4},{7,5},{8,10},{9,11},{10,... | collective-permute-start | bytes 1179656 | tf_op jit(solution)/shard_map/ppermute | solution.py:769
  23.8 0.9 %choices.3 = (bf16[2560,128]{1,0:T(8,128)(2,1)S(1)}, bf16[512,128]{1,0:T(8,128)(2,1)S(1)}, bf16[512,128]{1,0:T(8,128)(2,1)S(1)}, bf16[128,256]{1,0:T(8,128)(2,1)...) custom-call(bf16[64,128]{1,0:T(8,128)(2,1)S(1)} %get-tuple-element.8, ...), custom_call_target="tpu_custom_call" | custom-call | bytes 819200 | tf_op jit(solution)/shard_map/choices/pallas_call | solution.py:699
  24.8 1.1 %collective-permute-done.7.refs_0_ = bf16[640,128]{1,0:T(8,128)(2,1)S(1)} collective-permute-done((bf16[640,128]{1,0:T(8,128)(2,1)S(1)}, bf16[640,128]{1,0:T(8,128)(2,1)S(1)}, u32[]{:S(2)}, u32[]{:S(2)}) %collective-permute-start.7) | collective-permute-done | bytes 163872 | tf_op jit(solution)/shard_map/ppermute | solution.py:769
  26.1 3.7 %refine.3 = (bf16[2048,128]{1,0:T(8,128)(2,1)S(1)}, bf16[640,128]{1,0:T(8,128)(2,1)S(1)}, bf16[640,128]{1,0:T(8,128)(2,1)S(1)}, bf16[2048,128]{1,0:T(8,128)(2,1)}, bf16[2048,128]{1,0:T(8,128)(2,1)}) custom-call(bf16[2048,128]{1,0:T(8,128)(2,1)S(1)} %get-tuple-element.87.refs_0_, ...), custom_call_target="tpu_custom_call", output_to_operand_aliasing={{3}: (14, {}), {4}: (15, {})} | custom-call | flops 1509949440 | bytes 4407296 | tf_op jit(solution)/shard_map/refine/pallas_call | solution.py:699
  29.8 2.7 %collective-permute-start.9 = (bf16[640,128]{1,0:T(8,128)(2,1)S(1)}, bf16[640,128]{1,0:T(8,128)(2,1)S(1)}, u32[]{:S(2)}, u32[]{:S(2)}) collective-permute-start(bf16[640,128]{1,0:T(8,128)(2,1)S(1)} %get-tuple-element.103), channel_id=1, source_target_pairs={{0,4},{1,5},{2,6},{3,7},{4,0},{5,1},{6,2},{7,3},{8,12},{9,13},{10,... | collective-permute-start | bytes 491528 | tf_op jit(solution)/shard_map/ppermute | solution.py:769
  32.5 1.0 %choices.4 = (bf16[2560,128]{1,0:T(8,128)(2,1)S(1)}, bf16[512,128]{1,0:T(8,128)(2,1)S(1)}, bf16[512,128]{1,0:T(8,128)(2,1)S(1)}, bf16[128,256]{1,0:T(8,128)(2,1)...) custom-call(bf16[64,128]{1,0:T(8,128)(2,1)S(1)} %get-tuple-element.8, ...), custom_call_target="tpu_custom_call" | custom-call | bytes 819200 | tf_op jit(solution)/shard_map/choices/pallas_call | solution.py:699
  34.1 1.7 %collective-permute-done.9.refs_0_ = bf16[640,128]{1,0:T(8,128)(2,1)S(1)} collective-permute-done((bf16[640,128]{1,0:T(8,128)(2,1)S(1)}, bf16[640,128]{1,0:T(8,128)(2,1)S(1)}, u32[]{:S(2)}, u32[]{:S(2)}) %collective-permute-start.9) | collective-permute-done | bytes 163872 | tf_op jit(solution)/shard_map/ppermute | solution.py:769
  35.8 3.8 %refine.4 = (bf16[2048,128]{1,0:T(8,128)(2,1)S(1)}, bf16[640,128]{1,0:T(8,128)(2,1)S(1)}, bf16[640,128]{1,0:T(8,128)(2,1)S(1)}, bf16[2048,128]{1,0:T(8,128)(2,1)}, bf16[2048,128]{1,0:T(8,128)(2,1)}) custom-call(bf16[2048,128]{1,0:T(8,128)(2,1)S(1)} %get-tuple-element.102.refs_1_.refs_0_, ...), custom_call_target="tpu_custom_call", output_to_operand_aliasing={{3}: (14, {}), {4}: (15, {})} | custom-call | flops 1509949440 | bytes 4407296 | tf_op jit(solution)/shard_map/refine/pallas_call | solution.py:699
  39.6 2.4 %collective-permute-start.11 = (bf16[640,128]{1,0:T(8,128)(2,1)S(1)}, bf16[640,128]{1,0:T(8,128)(2,1)S(1)}, u32[]{:S(2)}, u32[]{:S(2)}) collective-permute-start(bf16[640,128]{1,0:T(8,128)(2,1)S(1)} %get-tuple-element.118), channel_id=1, source_target_pairs={{0,4},{1,5},{2,6},{3,7},{4,0},{5,1},{6,2},{7,3},{8,12},{9,13},{10,... | collective-permute-start | bytes 491528 | tf_op jit(solution)/shard_map/ppermute | solution.py:769
  41.9 0.7 %choices.5 = (bf16[2560,128]{1,0:T(8,128)(2,1)S(1)}, bf16[512,128]{1,0:T(8,128)(2,1)S(1)}, bf16[512,128]{1,0:T(8,128)(2,1)S(1)}, bf16[128,256]{1,0:T(8,128)(2,1)S(1)}, bf16[128,256]{1,0:T(8,128)(2,1)S(1)}) custom-call(bf16[64,128]{1,0:T(8,128)(2,1)S(1)} %get-tuple-element.82.refs_6_.codes, bf16[544,128]{1,0:T(8,128)(2,1)S(1)} %sooner.4.refs_1_.along, ...), custom_call_target="tpu_custom_call" | custom-call | bytes 819200 | tf_op jit(solution)/shard_map/choices/pallas_call | solution.py:699
  42.7 2.5 %collective-permute-done.11.refs_0_ = bf16[640,128]{1,0:T(8,128)(2,1)S(1)} collective-permute-done((bf16[640,128]{1,0:T(8,128)(2,1)S(1)}, bf16[640,128]{1,0:T(8,128)(2,1)S(1)}, u32[]{:S(2)}, u32[]{:S(2)}) %collective-permute-start.11) | collective-permute-done | bytes 163872 | tf_op jit(solution)/shard_map/ppermute | solution.py:769
  45.3 2.5 %refine.5 = (bf16[512,128]{1,0:T(8,128)(2,1)S(1)}, bf16[512,128]{1,0:T(8,128)(2,1)S(1)}, bf16[2048,128]{1,0:T(8,128)(2,1)}, bf16[2048,128]{1,0:T(8,128)(2,1)}) custom-call(bf16[1024,128]{1,0:T(8,128)(2,1)S(1)} %get-tuple-element.117.refs_1_.refs_0_, bf16[544,128]{1,0:T(8,128)(2,1)S(1)} %sooner.4.refs_1_.along, ...), custom_call_target="tpu_custom_call", output_to_operand_aliasing={{2}: (10, {}), {3}: (11, {})} | custom-call | flops 1509949440 | bytes 3751936 | tf_op jit(solution)/shard_map/refine/pallas_call | solution.py:699
  47.9 0.6 %collective-permute-start.13 = (bf16[512,128]{1,0:T(8,128)(2,1)S(1)}, bf16[512,128]{1,0:T(8,128)(2,1)S(1)}, u32[]{:S(2)}, u32[]{:S(2)}) collective-permute-start(bf16[512,128]{1,0:T(8,128)(2,1)S(1)} %get-tuple-element.127), channel_id=1, source_target_pairs={{0,1},{1,0},{2,3},{3,2},{4,5},{5,4},{6,7},{7,6},{8,9},{9,8},{10,11... | collective-permute-start | bytes 393224 | tf_op jit(solution)/shard_map/ppermute | solution.py:769
  48.4 0.8 %finish_own.1 = (bf16[2048,128]{1,0:T(8,128)(2,1)}, bf16[2048,128]{1,0:T(8,128)(2,1)}) custom-call(bf16[512,128]{1,0:T(8,128)(2,1)S(1)} %get-tuple-element.128.own, bf16[1536,128]{1,0:T(8,128)(2,1)S(1)} %collective-permute-done.14.backs, bf16[2048,128]{1,0:T(8,128)(2,1)} %get-tuple-element.132.out_a, ...), custom_call_target="tpu_custom_call", output_to_operand_aliasing={{0}: (2, {}), {1}: (3, {})} | custom-call | bytes 1572864 | tf_op jit(solution)/shard_map/finish_own/pallas_call | solution.py:699
  49.4 0.7 %finish.1 = (bf16[2048,128]{1,0:T(8,128)(2,1)}, bf16[2048,128]{1,0:T(8,128)(2,1)}) custom-call(bf16[512,128]{1,0:T(8,128)(2,1)S(1)} %collective-permute-done.13.back, bf16[2048,128]{1,0:T(8,128)(2,1)} %get-tuple-element.134.out_a, bf16[2048,128]{1,0:T(8,128)(2,1)} %get-tuple-element.135.out_b), custom_call_target="tpu_custom_call", output_to_operand_aliasing={{0}: (1, {}), {1}: (2, {})} | custom-call | bytes 1179648 | tf_op jit(solution)/shard_map/finish/pallas_call | solution.py:699
  (34 shorter events, 3.0 us)
Async XLA Ops:
  0.6 7.6 %copy-start = (bf16[2,4,9,64,64]{4,3,2,1,0:T(8,128)(2,1)S(1)}, bf16[2,4,9,64,64]{4,3,2,1,0:T(8,128)(2,1)}, u32[]{:S(2)}) copy-start(bf16[2,4,9,64,64]{4,3,2,1,0:T(8,128)(2,1)} %conv.1) | copy-start | bytes 1769476
  0.6 7.6 %copy-start.1 = (bf16[2,64,128]{2,1,0:T(8,128)(2,1)S(1)}, bf16[2,64,128]{2,1,0:T(8,128)(2,1)}, u32[]{:S(2)}) copy-start(bf16[2,64,128]{2,1,0:T(8,128)(2,1)} %join.1) | copy-start | bytes 98308
  2.0 1.6 %collective-permute-start = (bf16[784,128]{1,0:T(8,128)(2,1)S(1)}, bf16[784,128]{1,0:T(8,128)(2,1)S(1)}, u32[]{:S(2)}, u32[]{:S(2)}) collective-permute-start(bf16[784,128]{1,0:T(8,128)(2,1)S(1)} %get-tuple-element.72), channel_id=1, source_target_pairs={{0,1},{1,0},{2,3},{3,2},{4,5},{5,4},{6,7},{7,6},{8,9},{9,8},{10,11... | collective-permute-start | bytes 602120 | tf_op jit(solution)/shard_map/ppermute | solution.py:769
  3.8 4.7 %collective-permute-start.1 = (bf16[1536,128]{1,0:T(8,128)(2,1)S(1)}, bf16[1536,128]{1,0:T(8,128)(2,1)S(1)}, u32[]{:S(2)}, u32[]{:S(2)}) collective-permute-start(bf16[1536,128]{1,0:T(8,128)(2,1)S(1)} %get-tuple-element.73), channel_id=1, source_target_pairs={{0,1},{1,0},{2,3},{3,2},{4,5},{5,4},{6,7},{7,6},{8,9},{9,8},{10,11... | collective-permute-start | bytes 1179656 | tf_op jit(solution)/shard_map/ppermute | solution.py:769
  4.2 9.6 %collective-permute-start.2 = (bf16[1056,128]{1,0:T(8,128)(2,1)S(1)}, bf16[1056,128]{1,0:T(8,128)(2,1)S(1)}, u32[]{:S(2)}, u32[]{:S(2)}) collective-permute-start(bf16[1056,128]{1,0:T(8,128)(2,1)S(1)} %get-tuple-element.75.pair), channel_id=1, source_target_pairs={{0,2},{1,3},{2,0},{3,1},{4,6},{5,7},{6,4},{7,5},{8,10},{9,11},{10,... | collective-permute-start | bytes 811016 | tf_op jit(solution)/shard_map/ppermute | solution.py:769
  6.8 9.7 %collective-permute-start.3 = (bf16[544,128]{1,0:T(8,128)(2,1)S(1)}, bf16[544,128]{1,0:T(8,128)(2,1)S(1)}, u32[]{:S(2)}, u32[]{:S(2)}) collective-permute-start(bf16[544,128]{1,0:T(8,128)(2,1)S(1)} %get-tuple-element.79), channel_id=1, source_target_pairs={{2,6},{3,7},{4,0},{5,1},{6,10},{7,11},{8,4},{9,5},{10,14},{11,15},... | collective-permute-start | bytes 417800 | tf_op jit(solution)/shard_map/ppermute | solution.py:769
  8.1 8.4 %collective-permute-start.4 = (bf16[544,128]{1,0:T(8,128)(2,1)S(1)}, bf16[544,128]{1,0:T(8,128)(2,1)S(1)}, u32[]{:S(2)}, u32[]{:S(2)}) collective-permute-start(bf16[544,128]{1,0:T(8,128)(2,1)S(1)} %get-tuple-element.79), channel_id=1, source_target_pairs={{0,1},{1,0},{2,4},{3,5},{4,2},{5,3},{6,8},{7,9},{8,6},{9,7},{10,12... | collective-permute-start | bytes 417800 | tf_op jit(solution)/shard_map/ppermute | solution.py:769
  14.1 11.8 %collective-permute-start.6 = (bf16[1280,128]{1,0:T(8,128)(2,1)S(1)}, bf16[1280,128]{1,0:T(8,128)(2,1)S(1)}, u32[]{:S(2)}, u32[]{:S(2)}) collective-permute-start(bf16[1280,128]{1,0:T(8,128)(2,1)S(1)} %get-tuple-element.85.pair), channel_id=1, source_target_pairs={{0,2},{1,3},{2,0},{3,1},{4,6},{5,7},{6,4},{7,5},{8,10},{9,11},{10,... | collective-permute-start | bytes 983048 | tf_op jit(solution)/shard_map/ppermute | solution.py:769
  19.8 6.0 %collective-permute-start.7 = (bf16[640,128]{1,0:T(8,128)(2,1)S(1)}, bf16[640,128]{1,0:T(8,128)(2,1)S(1)}, u32[]{:S(2)}, u32[]{:S(2)}) collective-permute-start(bf16[640,128]{1,0:T(8,128)(2,1)S(1)} %get-tuple-element.88), channel_id=1, source_target_pairs={{0,4},{1,5},{2,6},{3,7},{4,0},{5,1},{6,2},{7,3},{8,12},{9,13},{10,... | collective-permute-start | bytes 491528 | tf_op jit(solution)/shard_map/ppermute | solution.py:769
  22.3 3.8 %collective-permute-start.8 = (bf16[640,128]{1,0:T(8,128)(2,1)S(1)}, bf16[640,128]{1,0:T(8,128)(2,1)S(1)}, u32[]{:S(2)}, u32[]{:S(2)}) collective-permute-start(bf16[640,128]{1,0:T(8,128)(2,1)S(1)} %get-tuple-element.89), channel_id=1, source_target_pairs={{0,1},{1,0},{2,3},{3,2},{4,8},{5,9},{6,10},{7,11},{8,4},{9,5},{10,... | collective-permute-start | bytes 491528 | tf_op jit(solution)/shard_map/ppermute | solution.py:769
  22.3 11.5 %collective-permute-start.5 = (bf16[1536,128]{1,0:T(8,128)(2,1)S(1)}, bf16[1536,128]{1,0:T(8,128)(2,1)S(1)}, u32[]{:S(2)}, u32[]{:S(2)}) collective-permute-start(bf16[1536,128]{1,0:T(8,128)(2,1)S(1)} %get-tuple-element.84.pair), channel_id=1, source_target_pairs={{0,2},{1,3},{2,0},{3,1},{4,6},{5,7},{6,4},{7,5},{8,10},{9,11},{10,... | collective-permute-start | bytes 1179656 | tf_op jit(solution)/shard_map/ppermute | solution.py:769
  29.8 6.0 %collective-permute-start.9 = (bf16[640,128]{1,0:T(8,128)(2,1)S(1)}, bf16[640,128]{1,0:T(8,128)(2,1)S(1)}, u32[]{:S(2)}, u32[]{:S(2)}) collective-permute-start(bf16[640,128]{1,0:T(8,128)(2,1)S(1)} %get-tuple-element.103), channel_id=1, source_target_pairs={{0,4},{1,5},{2,6},{3,7},{4,0},{5,1},{6,2},{7,3},{8,12},{9,13},{10,... | collective-permute-start | bytes 491528 | tf_op jit(solution)/shard_map/ppermute | solution.py:769
  32.5 3.3 %collective-permute-start.10 = (bf16[640,128]{1,0:T(8,128)(2,1)S(1)}, bf16[640,128]{1,0:T(8,128)(2,1)S(1)}, u32[]{:S(2)}, u32[]{:S(2)}) collective-permute-start(bf16[640,128]{1,0:T(8,128)(2,1)S(1)} %get-tuple-element.104), channel_id=1, source_target_pairs={{0,1},{1,0},{2,3},{3,2},{4,8},{5,9},{6,10},{7,11},{8,4},{9,5},{10,... | collective-permute-start | bytes 491528 | tf_op jit(solution)/shard_map/ppermute | solution.py:769
  39.6 5.7 %collective-permute-start.11 = (bf16[640,128]{1,0:T(8,128)(2,1)S(1)}, bf16[640,128]{1,0:T(8,128)(2,1)S(1)}, u32[]{:S(2)}, u32[]{:S(2)}) collective-permute-start(bf16[640,128]{1,0:T(8,128)(2,1)S(1)} %get-tuple-element.118), channel_id=1, source_target_pairs={{0,4},{1,5},{2,6},{3,7},{4,0},{5,1},{6,2},{7,3},{8,12},{9,13},{10,... | collective-permute-start | bytes 491528 | tf_op jit(solution)/shard_map/ppermute | solution.py:769
  41.9 3.3 %collective-permute-start.12 = (bf16[640,128]{1,0:T(8,128)(2,1)S(1)}, bf16[640,128]{1,0:T(8,128)(2,1)S(1)}, u32[]{:S(2)}, u32[]{:S(2)}) collective-permute-start(bf16[640,128]{1,0:T(8,128)(2,1)S(1)} %get-tuple-element.119), channel_id=1, source_target_pairs={{0,1},{1,0},{2,3},{3,2},{4,8},{5,9},{6,10},{7,11},{8,4},{9,5},{10,... | collective-permute-start | bytes 491528 | tf_op jit(solution)/shard_map/ppermute | solution.py:769
  45.3 3.2 %collective-permute-start.14 = (bf16[1536,128]{1,0:T(8,128)(2,1)S(1)}, bf16[1536,128]{1,0:T(8,128)(2,1)S(1)}, u32[]{:S(2)}, u32[]{:S(2)}) collective-permute-start(bf16[1536,128]{1,0:T(8,128)(2,1)S(1)} %parts.1), channel_id=1, source_target_pairs={{0,1},{1,0},{2,3},{3,2},{4,5},{5,4},{6,7},{7,6},{8,9},{9,8},{10,11... | collective-permute-start | bytes 1179656 | tf_op jit(solution)/shard_map/ppermute | solution.py:769
  47.9 1.5 %collective-permute-start.13 = (bf16[512,128]{1,0:T(8,128)(2,1)S(1)}, bf16[512,128]{1,0:T(8,128)(2,1)S(1)}, u32[]{:S(2)}, u32[]{:S(2)}) collective-permute-start(bf16[512,128]{1,0:T(8,128)(2,1)S(1)} %get-tuple-element.127), channel_id=1, source_target_pairs={{0,1},{1,0},{2,3},{3,2},{4,5},{5,4},{6,7},{7,6},{8,9},{9,8},{10,11... | collective-permute-start | bytes 393224 | tf_op jit(solution)/shard_map/ppermute | solution.py:769

commit v7 on v6

--- a/solution.py
+++ b/solution.py
@@ -521,7 +521,6 @@
     rows = QUAD * BS
     place = Place()
     space = Rows(ch, xq.shape[1], jnp.logical_not(place.top), jnp.logical_not(place.bottom), rows)
-    send_choices(code_of_next(ch, place, 0, steps, codes, along, cross), choices)
     above, below = above_below(place, along[pl.ds(0, half), :], cross[pl.ds(0, half), :])
     clear_outside(space, ch, rows, (act_a, act_b))
     join_mat = join[...]
@@ -530,6 +529,7 @@
         for n, value in enumerate(join_first_rows(ch, join_mat, inp)):
             held[here_of(first + n, ch), :] = value
             space.put(act_a, here_of(first + n, ch), value, first + n)
+    send_choices(code_of_next(ch, place, 0, steps, codes, along, cross), choices)
     conv_layers(ch, conv, space, rows, act_a, act_b, held, fout)
     pack_messages(ch, fout, place.odd, join_both[...], choices, None, sent, msg_e, msg_o)
 

time: 50.5 us -> 50.5 us (level)
  no operation moved by 1% of the time
where the time goes in v7:
time: 50.5 us; the launch traced here: 50.2 us
  Pallas kernels  22.5 us (45%)
  starting transfers between devices  17.2 us (34%)
  waiting for transfers between devices  9.54 us (19%)
  between operations  0.97 us (2%)
    pallas_call x20, Pallas kernels, call(): pl.pallas_call(kernel, out_shape=[jax.ShapeDtypeStruct(o, BF) for o in ou...  22.5 us
    ppermute x15, starting transfers between devices, send(): return lax.ppermute(value, 'tiles', pairs)  17.2 us
    ppermute x15, waiting for transfers between devices, send(): return lax.ppermute(value, 'tiles', pairs)  9.54 us
  transfers between devices with their start and end apart: 15, of which 6 were waited for; matrix products, arithmetic and copies ran while one was open for 0% of the time, Pallas kernels for 33%

profile of v7, /device:TPU:0, one launch (start us, length us, event | category | flops | bytes accessed | tf_op | source)
XLA Modules:
  0.0 50.2 jit_solution(8094599154901767330)
XLA Ops:
  0.7 1.4 %pack_first.1 = (bf16[528,128]{1,0:T(8,128)(2,1)S(1)}, bf16[256,128]{1,0:T(8,128)(2,1)S(1)}, bf16[784,128]{1,0:T(8,128)(2,1)S(1)}) custom-call(bf16[4,512,128]{2,1,0:T(8,128)(2,1)} %bitcast.3, s32[3,16]{1,0:T(4,128)} %motion_f.1, s32[3,16]{1,0:T(4,128)} %motion_b.1), custom_call_target="tpu_custom_call" | custom-call | bytes 524672 | tf_op jit(solution)/shard_map/pack_first/pallas_call | solution.py:699
  2.6 1.1 %pack_rest.1.rest_in = bf16[1536,128]{1,0:T(8,128)(2,1)S(1)} custom-call(bf16[4,512,128]{2,1,0:T(8,128)(2,1)} %bitcast.4, bf16[528,128]{1,0:T(8,128)(2,1)S(1)} %get-tuple-element.70.after.mine), custom_call_target="tpu_custom_call" | custom-call | bytes 659456 | tf_op jit(solution)/shard_map/pack_rest/pallas_call | solution.py:699
  4.2 2.6 %collective-permute-start.2 = (bf16[1056,128]{1,0:T(8,128)(2,1)S(1)}, bf16[1056,128]{1,0:T(8,128)(2,1)S(1)}, u32[]{:S(2)}, u32[]{:S(2)}) collective-permute-start(bf16[1056,128]{1,0:T(8,128)(2,1)S(1)} %get-tuple-element.75.pair), channel_id=1, source_target_pairs={{0,2},{1,3},{2,0},{3,1},{4,6},{5,7},{6,4},{7,5},{8,10},{9,11},{10,... | collective-permute-start | bytes 811016 | tf_op jit(solution)/shard_map/ppermute | solution.py:769
  6.8 1.3 %collective-permute-start.3 = (bf16[544,128]{1,0:T(8,128)(2,1)S(1)}, bf16[544,128]{1,0:T(8,128)(2,1)S(1)}, u32[]{:S(2)}, u32[]{:S(2)}) collective-permute-start(bf16[544,128]{1,0:T(8,128)(2,1)S(1)} %get-tuple-element.79), channel_id=1, source_target_pairs={{2,6},{3,7},{4,0},{5,1},{6,10},{7,11},{8,4},{9,5},{10,14},{11,15},... | collective-permute-start | bytes 417800 | tf_op jit(solution)/shard_map/ppermute | solution.py:769
  8.5 1.6 %pair_rest.1 = (bf16[1280,128]{1,0:T(8,128)(2,1)S(1)}, bf16[1536,128]{1,0:T(8,128)(2,1)S(1)}, bf16[1024,128]{1,0:T(8,128)(2,1)S(1)}) custom-call(bf16[4,512,128]{2,1,0:T(8,128)(2,1)} %bitcast.5, bf16[1536,128]{1,0:T(8,128)(2,1)S(1)} %collective-permute-done.1.swapped), custom_call_target="tpu_custom_call" | custom-call | bytes 917504 | tf_op jit(solution)/shard_map/pair_rest/pallas_call | solution.py:699
  10.1 3.7 %collective-permute-done.2.received = bf16[1056,128]{1,0:T(8,128)(2,1)S(1)} collective-permute-done((bf16[1056,128]{1,0:T(8,128)(2,1)S(1)}, bf16[1056,128]{1,0:T(8,128)(2,1)S(1)}, u32[]{:S(2)}, u32[]{:S(2)}) %collective-permute-start.2) | collective-permute-done | bytes 270368 | tf_op jit(solution)/shard_map/ppermute | solution.py:769
  14.1 2.4 %collective-permute-start.6 = (bf16[1280,128]{1,0:T(8,128)(2,1)S(1)}, bf16[1280,128]{1,0:T(8,128)(2,1)S(1)}, u32[]{:S(2)}, u32[]{:S(2)}) collective-permute-start(bf16[1280,128]{1,0:T(8,128)(2,1)S(1)} %get-tuple-element.85.pair), channel_id=1, source_target_pairs={{0,2},{1,3},{2,0},{3,1},{4,6},{5,7},{6,4},{7,5},{8,10},{9,11},{10,... | collective-permute-start | bytes 983048 | tf_op jit(solution)/shard_map/ppermute | solution.py:769
  16.5 3.3 %refine_first.1 = (bf16[2048,128]{1,0:T(8,128)(2,1)S(1)}, bf16[640,128]{1,0:T(8,128)(2,1)S(1)}, bf16[640,128]{1,0:T(8,128)(2,1)S(1)}, bf16[1536,128]{1,0:T(8,128)(2,1)S(1)}) custom-call(bf16[2048,128]{1,0:T(8,128)(2,1)S(1)} %get-tuple-element.78.refs_0_, bf16[544,128]{1,0:T(8,128)(2,1)S(1)} %sooner.4.refs_1_.along, ...), custom_call_target="tpu_custom_call", output_to_operand_aliasing={{3}: (7, {})} | custom-call | flops 1509949440 | bytes 2097152 | tf_op jit(solution)/shard_map/refine_first/pallas_call | solution.py:699
  19.8 2.5 %collective-permute-start.7 = (bf16[640,128]{1,0:T(8,128)(2,1)S(1)}, bf16[640,128]{1,0:T(8,128)(2,1)S(1)}, u32[]{:S(2)}, u32[]{:S(2)}) collective-permute-start(bf16[640,128]{1,0:T(8,128)(2,1)S(1)} %get-tuple-element.88), channel_id=1, source_target_pairs={{0,4},{1,5},{2,6},{3,7},{4,0},{5,1},{6,2},{7,3},{8,12},{9,13},{10,... | collective-permute-start | bytes 491528 | tf_op jit(solution)/shard_map/ppermute | solution.py:769
  22.3 1.5 %collective-permute-start.5 = (bf16[1536,128]{1,0:T(8,128)(2,1)S(1)}, bf16[1536,128]{1,0:T(8,128)(2,1)S(1)}, u32[]{:S(2)}, u32[]{:S(2)}) collective-permute-start(bf16[1536,128]{1,0:T(8,128)(2,1)S(1)} %get-tuple-element.84.pair), channel_id=1, source_target_pairs={{0,2},{1,3},{2,0},{3,1},{4,6},{5,7},{6,4},{7,5},{8,10},{9,11},{10,... | collective-permute-start | bytes 1179656 | tf_op jit(solution)/shard_map/ppermute | solution.py:769
  23.8 0.9 %choices.3 = (bf16[2560,128]{1,0:T(8,128)(2,1)S(1)}, bf16[512,128]{1,0:T(8,128)(2,1)S(1)}, bf16[512,128]{1,0:T(8,128)(2,1)S(1)}, bf16[128,256]{1,0:T(8,128)(2,1)...) custom-call(bf16[64,128]{1,0:T(8,128)(2,1)S(1)} %get-tuple-element.8, ...), custom_call_target="tpu_custom_call" | custom-call | bytes 819200 | tf_op jit(solution)/shard_map/choices/pallas_call | solution.py:699
  24.8 1.0 %collective-permute-done.7.refs_0_ = bf16[640,128]{1,0:T(8,128)(2,1)S(1)} collective-permute-done((bf16[640,128]{1,0:T(8,128)(2,1)S(1)}, bf16[640,128]{1,0:T(8,128)(2,1)S(1)}, u32[]{:S(2)}, u32[]{:S(2)}) %collective-permute-start.7) | collective-permute-done | bytes 163872 | tf_op jit(solution)/shard_map/ppermute | solution.py:769
  26.1 3.7 %refine.3 = (bf16[2048,128]{1,0:T(8,128)(2,1)S(1)}, bf16[640,128]{1,0:T(8,128)(2,1)S(1)}, bf16[640,128]{1,0:T(8,128)(2,1)S(1)}, bf16[2048,128]{1,0:T(8,128)(2,1)}, bf16[2048,128]{1,0:T(8,128)(2,1)}) custom-call(bf16[2048,128]{1,0:T(8,128)(2,1)S(1)} %get-tuple-element.87.refs_0_, ...), custom_call_target="tpu_custom_call", output_to_operand_aliasing={{3}: (14, {}), {4}: (15, {})} | custom-call | flops 1509949440 | bytes 4407296 | tf_op jit(solution)/shard_map/refine/pallas_call | solution.py:699
  29.7 2.7 %collective-permute-start.9 = (bf16[640,128]{1,0:T(8,128)(2,1)S(1)}, bf16[640,128]{1,0:T(8,128)(2,1)S(1)}, u32[]{:S(2)}, u32[]{:S(2)}) collective-permute-start(bf16[640,128]{1,0:T(8,128)(2,1)S(1)} %get-tuple-element.103), channel_id=1, source_target_pairs={{0,4},{1,5},{2,6},{3,7},{4,0},{5,1},{6,2},{7,3},{8,12},{9,13},{10,... | collective-permute-start | bytes 491528 | tf_op jit(solution)/shard_map/ppermute | solution.py:769
  32.5 0.9 %choices.4 = (bf16[2560,128]{1,0:T(8,128)(2,1)S(1)}, bf16[512,128]{1,0:T(8,128)(2,1)S(1)}, bf16[512,128]{1,0:T(8,128)(2,1)S(1)}, bf16[128,256]{1,0:T(8,128)(2,1)...) custom-call(bf16[64,128]{1,0:T(8,128)(2,1)S(1)} %get-tuple-element.8, ...), custom_call_target="tpu_custom_call" | custom-call | bytes 819200 | tf_op jit(solution)/shard_map/choices/pallas_call | solution.py:699
  34.1 1.7 %collective-permute-done.9.refs_0_ = bf16[640,128]{1,0:T(8,128)(2,1)S(1)} collective-permute-done((bf16[640,128]{1,0:T(8,128)(2,1)S(1)}, bf16[640,128]{1,0:T(8,128)(2,1)S(1)}, u32[]{:S(2)}, u32[]{:S(2)}) %collective-permute-start.9) | collective-permute-done | bytes 163872 | tf_op jit(solution)/shard_map/ppermute | solution.py:769
  35.8 3.8 %refine.4 = (bf16[2048,128]{1,0:T(8,128)(2,1)S(1)}, bf16[640,128]{1,0:T(8,128)(2,1)S(1)}, bf16[640,128]{1,0:T(8,128)(2,1)S(1)}, bf16[2048,128]{1,0:T(8,128)(2,1)}, bf16[2048,128]{1,0:T(8,128)(2,1)}) custom-call(bf16[2048,128]{1,0:T(8,128)(2,1)S(1)} %get-tuple-element.102.refs_1_.refs_0_, ...), custom_call_target="tpu_custom_call", output_to_operand_aliasing={{3}: (14, {}), {4}: (15, {})} | custom-call | flops 1509949440 | bytes 4407296 | tf_op jit(solution)/shard_map/refine/pallas_call | solution.py:699
  39.6 2.4 %collective-permute-start.11 = (bf16[640,128]{1,0:T(8,128)(2,1)S(1)}, bf16[640,128]{1,0:T(8,128)(2,1)S(1)}, u32[]{:S(2)}, u32[]{:S(2)}) collective-permute-start(bf16[640,128]{1,0:T(8,128)(2,1)S(1)} %get-tuple-element.118), channel_id=1, source_target_pairs={{0,4},{1,5},{2,6},{3,7},{4,0},{5,1},{6,2},{7,3},{8,12},{9,13},{10,... | collective-permute-start | bytes 491528 | tf_op jit(solution)/shard_map/ppermute | solution.py:769
  41.9 0.7 %choices.5 = (bf16[2560,128]{1,0:T(8,128)(2,1)S(1)}, bf16[512,128]{1,0:T(8,128)(2,1)S(1)}, bf16[512,128]{1,0:T(8,128)(2,1)S(1)}, bf16[128,256]{1,0:T(8,128)(2,1)S(1)}, bf16[128,256]{1,0:T(8,128)(2,1)S(1)}) custom-call(bf16[64,128]{1,0:T(8,128)(2,1)S(1)} %get-tuple-element.82.refs_6_.codes, bf16[544,128]{1,0:T(8,128)(2,1)S(1)} %sooner.4.refs_1_.along, ...), custom_call_target="tpu_custom_call" | custom-call | bytes 819200 | tf_op jit(solution)/shard_map/choices/pallas_call | solution.py:699
  42.7 2.5 %collective-permute-done.11.refs_0_ = bf16[640,128]{1,0:T(8,128)(2,1)S(1)} collective-permute-done((bf16[640,128]{1,0:T(8,128)(2,1)S(1)}, bf16[640,128]{1,0:T(8,128)(2,1)S(1)}, u32[]{:S(2)}, u32[]{:S(2)}) %collective-permute-start.11) | collective-permute-done | bytes 163872 | tf_op jit(solution)/shard_map/ppermute | solution.py:769
  45.3 2.5 %refine.5 = (bf16[512,128]{1,0:T(8,128)(2,1)S(1)}, bf16[512,128]{1,0:T(8,128)(2,1)S(1)}, bf16[2048,128]{1,0:T(8,128)(2,1)}, bf16[2048,128]{1,0:T(8,128)(2,1)}) custom-call(bf16[1024,128]{1,0:T(8,128)(2,1)S(1)} %get-tuple-element.117.refs_1_.refs_0_, bf16[544,128]{1,0:T(8,128)(2,1)S(1)} %sooner.4.refs_1_.along, ...), custom_call_target="tpu_custom_call", output_to_operand_aliasing={{2}: (10, {}), {3}: (11, {})} | custom-call | flops 1509949440 | bytes 3751936 | tf_op jit(solution)/shard_map/refine/pallas_call | solution.py:699
  47.8 0.6 %collective-permute-start.13 = (bf16[512,128]{1,0:T(8,128)(2,1)S(1)}, bf16[512,128]{1,0:T(8,128)(2,1)S(1)}, u32[]{:S(2)}, u32[]{:S(2)}) collective-permute-start(bf16[512,128]{1,0:T(8,128)(2,1)S(1)} %get-tuple-element.127), channel_id=1, source_target_pairs={{0,1},{1,0},{2,3},{3,2},{4,5},{5,4},{6,7},{7,6},{8,9},{9,8},{10,11... | collective-permute-start | bytes 393224 | tf_op jit(solution)/shard_map/ppermute | solution.py:769
  48.4 0.8 %finish_own.1 = (bf16[2048,128]{1,0:T(8,128)(2,1)}, bf16[2048,128]{1,0:T(8,128)(2,1)}) custom-call(bf16[512,128]{1,0:T(8,128)(2,1)S(1)} %get-tuple-element.128.own, bf16[1536,128]{1,0:T(8,128)(2,1)S(1)} %collective-permute-done.14.backs, bf16[2048,128]{1,0:T(8,128)(2,1)} %get-tuple-element.132.out_a, ...), custom_call_target="tpu_custom_call", output_to_operand_aliasing={{0}: (2, {}), {1}: (3, {})} | custom-call | bytes 1572864 | tf_op jit(solution)/shard_map/finish_own/pallas_call | solution.py:699
  49.4 0.7 %finish.1 = (bf16[2048,128]{1,0:T(8,128)(2,1)}, bf16[2048,128]{1,0:T(8,128)(2,1)}) custom-call(bf16[512,128]{1,0:T(8,128)(2,1)S(1)} %collective-permute-done.13.back, bf16[2048,128]{1,0:T(8,128)(2,1)} %get-tuple-element.134.out_a, bf16[2048,128]{1,0:T(8,128)(2,1)} %get-tuple-element.135.out_b), custom_call_target="tpu_custom_call", output_to_operand_aliasing={{0}: (1, {}), {1}: (2, {})} | custom-call | bytes 1179648 | tf_op jit(solution)/shard_map/finish/pallas_call | solution.py:699
  (34 shorter events, 2.9 us)
Async XLA Ops:
  0.6 7.6 %copy-start = (bf16[2,4,9,64,64]{4,3,2,1,0:T(8,128)(2,1)S(1)}, bf16[2,4,9,64,64]{4,3,2,1,0:T(8,128)(2,1)}, u32[]{:S(2)}) copy-start(bf16[2,4,9,64,64]{4,3,2,1,0:T(8,128)(2,1)} %conv.1) | copy-start | bytes 1769476
  0.6 7.6 %copy-start.1 = (bf16[2,64,128]{2,1,0:T(8,128)(2,1)S(1)}, bf16[2,64,128]{2,1,0:T(8,128)(2,1)}, u32[]{:S(2)}) copy-start(bf16[2,64,128]{2,1,0:T(8,128)(2,1)} %join.1) | copy-start | bytes 98308
  2.0 1.6 %collective-permute-start = (bf16[784,128]{1,0:T(8,128)(2,1)S(1)}, bf16[784,128]{1,0:T(8,128)(2,1)S(1)}, u32[]{:S(2)}, u32[]{:S(2)}) collective-permute-start(bf16[784,128]{1,0:T(8,128)(2,1)S(1)} %get-tuple-element.72), channel_id=1, source_target_pairs={{0,1},{1,0},{2,3},{3,2},{4,5},{5,4},{6,7},{7,6},{8,9},{9,8},{10,11... | collective-permute-start | bytes 602120 | tf_op jit(solution)/shard_map/ppermute | solution.py:769
  3.8 4.7 %collective-permute-start.1 = (bf16[1536,128]{1,0:T(8,128)(2,1)S(1)}, bf16[1536,128]{1,0:T(8,128)(2,1)S(1)}, u32[]{:S(2)}, u32[]{:S(2)}) collective-permute-start(bf16[1536,128]{1,0:T(8,128)(2,1)S(1)} %get-tuple-element.73), channel_id=1, source_target_pairs={{0,1},{1,0},{2,3},{3,2},{4,5},{5,4},{6,7},{7,6},{8,9},{9,8},{10,11... | collective-permute-start | bytes 1179656 | tf_op jit(solution)/shard_map/ppermute | solution.py:769
  4.2 9.6 %collective-permute-start.2 = (bf16[1056,128]{1,0:T(8,128)(2,1)S(1)}, bf16[1056,128]{1,0:T(8,128)(2,1)S(1)}, u32[]{:S(2)}, u32[]{:S(2)}) collective-permute-start(bf16[1056,128]{1,0:T(8,128)(2,1)S(1)} %get-tuple-element.75.pair), channel_id=1, source_target_pairs={{0,2},{1,3},{2,0},{3,1},{4,6},{5,7},{6,4},{7,5},{8,10},{9,11},{10,... | collective-permute-start | bytes 811016 | tf_op jit(solution)/shard_map/ppermute | solution.py:769
  6.8 9.7 %collective-permute-start.3 = (bf16[544,128]{1,0:T(8,128)(2,1)S(1)}, bf16[544,128]{1,0:T(8,128)(2,1)S(1)}, u32[]{:S(2)}, u32[]{:S(2)}) collective-permute-start(bf16[544,128]{1,0:T(8,128)(2,1)S(1)} %get-tuple-element.79), channel_id=1, source_target_pairs={{2,6},{3,7},{4,0},{5,1},{6,10},{7,11},{8,4},{9,5},{10,14},{11,15},... | collective-permute-start | bytes 417800 | tf_op jit(solution)/shard_map/ppermute | solution.py:769
  8.1 8.4 %collective-permute-start.4 = (bf16[544,128]{1,0:T(8,128)(2,1)S(1)}, bf16[544,128]{1,0:T(8,128)(2,1)S(1)}, u32[]{:S(2)}, u32[]{:S(2)}) collective-permute-start(bf16[544,128]{1,0:T(8,128)(2,1)S(1)} %get-tuple-element.79), channel_id=1, source_target_pairs={{0,1},{1,0},{2,4},{3,5},{4,2},{5,3},{6,8},{7,9},{8,6},{9,7},{10,12... | collective-permute-start | bytes 417800 | tf_op jit(solution)/shard_map/ppermute | solution.py:769
  14.1 11.7 %collective-permute-start.6 = (bf16[1280,128]{1,0:T(8,128)(2,1)S(1)}, bf16[1280,128]{1,0:T(8,128)(2,1)S(1)}, u32[]{:S(2)}, u32[]{:S(2)}) collective-permute-start(bf16[1280,128]{1,0:T(8,128)(2,1)S(1)} %get-tuple-element.85.pair), channel_id=1, source_target_pairs={{0,2},{1,3},{2,0},{3,1},{4,6},{5,7},{6,4},{7,5},{8,10},{9,11},{10,... | collective-permute-start | bytes 983048 | tf_op jit(solution)/shard_map/ppermute | solution.py:769
  19.8 6.0 %collective-permute-start.7 = (bf16[640,128]{1,0:T(8,128)(2,1)S(1)}, bf16[640,128]{1,0:T(8,128)(2,1)S(1)}, u32[]{:S(2)}, u32[]{:S(2)}) collective-permute-start(bf16[640,128]{1,0:T(8,128)(2,1)S(1)} %get-tuple-element.88), channel_id=1, source_target_pairs={{0,4},{1,5},{2,6},{3,7},{4,0},{5,1},{6,2},{7,3},{8,12},{9,13},{10,... | collective-permute-start | bytes 491528 | tf_op jit(solution)/shard_map/ppermute | solution.py:769
  22.3 3.8 %collective-permute-start.8 = (bf16[640,128]{1,0:T(8,128)(2,1)S(1)}, bf16[640,128]{1,0:T(8,128)(2,1)S(1)}, u32[]{:S(2)}, u32[]{:S(2)}) collective-permute-start(bf16[640,128]{1,0:T(8,128)(2,1)S(1)} %get-tuple-element.89), channel_id=1, source_target_pairs={{0,1},{1,0},{2,3},{3,2},{4,8},{5,9},{6,10},{7,11},{8,4},{9,5},{10,... | collective-permute-start | bytes 491528 | tf_op jit(solution)/shard_map/ppermute | solution.py:769
  22.3 11.5 %collective-permute-start.5 = (bf16[1536,128]{1,0:T(8,128)(2,1)S(1)}, bf16[1536,128]{1,0:T(8,128)(2,1)S(1)}, u32[]{:S(2)}, u32[]{:S(2)}) collective-permute-start(bf16[1536,128]{1,0:T(8,128)(2,1)S(1)} %get-tuple-element.84.pair), channel_id=1, source_target_pairs={{0,2},{1,3},{2,0},{3,1},{4,6},{5,7},{6,4},{7,5},{8,10},{9,11},{10,... | collective-permute-start | bytes 1179656 | tf_op jit(solution)/shard_map/ppermute | solution.py:769
  29.7 6.0 %collective-permute-start.9 = (bf16[640,128]{1,0:T(8,128)(2,1)S(1)}, bf16[640,128]{1,0:T(8,128)(2,1)S(1)}, u32[]{:S(2)}, u32[]{:S(2)}) collective-permute-start(bf16[640,128]{1,0:T(8,128)(2,1)S(1)} %get-tuple-element.103), channel_id=1, source_target_pairs={{0,4},{1,5},{2,6},{3,7},{4,0},{5,1},{6,2},{7,3},{8,12},{9,13},{10,... | collective-permute-start | bytes 491528 | tf_op jit(solution)/shard_map/ppermute | solution.py:769
  32.5 3.3 %collective-permute-start.10 = (bf16[640,128]{1,0:T(8,128)(2,1)S(1)}, bf16[640,128]{1,0:T(8,128)(2,1)S(1)}, u32[]{:S(2)}, u32[]{:S(2)}) collective-permute-start(bf16[640,128]{1,0:T(8,128)(2,1)S(1)} %get-tuple-element.104), channel_id=1, source_target_pairs={{0,1},{1,0},{2,3},{3,2},{4,8},{5,9},{6,10},{7,11},{8,4},{9,5},{10,... | collective-permute-start | bytes 491528 | tf_op jit(solution)/shard_map/ppermute | solution.py:769
  39.6 5.6 %collective-permute-start.11 = (bf16[640,128]{1,0:T(8,128)(2,1)S(1)}, bf16[640,128]{1,0:T(8,128)(2,1)S(1)}, u32[]{:S(2)}, u32[]{:S(2)}) collective-permute-start(bf16[640,128]{1,0:T(8,128)(2,1)S(1)} %get-tuple-element.118), channel_id=1, source_target_pairs={{0,4},{1,5},{2,6},{3,7},{4,0},{5,1},{6,2},{7,3},{8,12},{9,13},{10,... | collective-permute-start | bytes 491528 | tf_op jit(solution)/shard_map/ppermute | solution.py:769
  41.9 3.3 %collective-permute-start.12 = (bf16[640,128]{1,0:T(8,128)(2,1)S(1)}, bf16[640,128]{1,0:T(8,128)(2,1)S(1)}, u32[]{:S(2)}, u32[]{:S(2)}) collective-permute-start(bf16[640,128]{1,0:T(8,128)(2,1)S(1)} %get-tuple-element.119), channel_id=1, source_target_pairs={{0,1},{1,0},{2,3},{3,2},{4,8},{5,9},{6,10},{7,11},{8,4},{9,5},{10,... | collective-permute-start | bytes 491528 | tf_op jit(solution)/shard_map/ppermute | solution.py:769
  45.2 3.2 %collective-permute-start.14 = (bf16[1536,128]{1,0:T(8,128)(2,1)S(1)}, bf16[1536,128]{1,0:T(8,128)(2,1)S(1)}, u32[]{:S(2)}, u32[]{:S(2)}) collective-permute-start(bf16[1536,128]{1,0:T(8,128)(2,1)S(1)} %parts.1), channel_id=1, source_target_pairs={{0,1},{1,0},{2,3},{3,2},{4,5},{5,4},{6,7},{7,6},{8,9},{9,8},{10,11... | collective-permute-start | bytes 1179656 | tf_op jit(solution)/shard_map/ppermute | solution.py:769
  47.8 1.5 %collective-permute-start.13 = (bf16[512,128]{1,0:T(8,128)(2,1)S(1)}, bf16[512,128]{1,0:T(8,128)(2,1)S(1)}, u32[]{:S(2)}, u32[]{:S(2)}) collective-permute-start(bf16[512,128]{1,0:T(8,128)(2,1)S(1)} %get-tuple-element.127), channel_id=1, source_target_pairs={{0,1},{1,0},{2,3},{3,2},{4,5},{5,4},{6,7},{7,6},{8,9},{9,8},{10,11... | collective-permute-start | bytes 393224 | tf_op jit(solution)/shard_map/ppermute | solution.py:769
